TPU v7x, 128 devices: a whole 4x4x4 slice. The times are simulated.
128 devices in a mesh: cand: 2 (over core), dp: 64 (over x, y, z).
Axes of the slice: x: 4, y: 4, z: 4, core: 2. Of those that a mesh axis runs over, the one named last changes fastest.
Arguments:
- token_ids: int32 [64, 6, 64], P('dp', 'cand'), may hold values from 0 to 50303
- token_mask: int32 [64, 6, 32], P('dp', 'cand'), may hold values 0 or 1
- resp_lengths: int32 [64, 6], P('dp', 'cand'), may hold values from 1 to 32, as said below
- cand_counts: int32 [64], P('dp'), may hold values from 2 to 5
- cand_rank: int32 [64, 6], P('dp', 'cand'), may hold values from 0 to 5, each once within a row
- rewards: float32 [64, 6], P('dp', 'cand')
- embed_table: float32 [50304, 1024], P(None, 'dp'), may hold values from -0.6 to 0.6
- embed_first: float32 [50304, 1024], P(None, 'dp'), may hold values from -6.137985e-05 to 6.137985e-05
- embed_second: float32 [50304, 1024], P(None, 'dp'), may hold values from 8.648958e-12 to 3.4595833e-11
- head_table: float32 [50304, 1024], P('dp')
- head_first: float32 [50304, 1024], P('dp'), may hold values from -6.137985e-05 to 6.137985e-05
- head_second: float32 [50304, 1024], P('dp'), may hold values from 8.648958e-12 to 3.4595833e-11
- qkv_weight: float32 [1024, 3072], P(('cand', 'dp')), may hold values from -0.1875 to 0.1875
- qkv_first: float32 [1024, 3072], P(('cand', 'dp')), may hold values from -6.137985e-05 to 6.137985e-05
- qkv_second: float32 [1024, 3072], P(('cand', 'dp')), may hold values from 8.648958e-12 to 3.4595833e-11
- proj_weight: float32 [1024, 1024], P(('cand', 'dp')), may hold values from -0.5 to 0.5
- proj_first: float32 [1024, 1024], P(('cand', 'dp')), may hold values from -6.137985e-05 to 6.137985e-05
- proj_second: float32 [1024, 1024], P(('cand', 'dp')), may hold values from 8.648958e-12 to 3.4595833e-11
- up_weight: float32 [1024, 4096], P(('cand', 'dp')), may hold values from -0.1875 to 0.1875
- up_first: float32 [1024, 4096], P(('cand', 'dp')), may hold values from -6.137985e-05 to 6.137985e-05
- up_second: float32 [1024, 4096], P(('cand', 'dp')), may hold values from 8.648958e-12 to 3.4595833e-11
- down_weight: float32 [4096, 1024], P(('cand', 'dp')), may hold values from -0.09375 to 0.09375
- down_first: float32 [4096, 1024], P(('cand', 'dp')), may hold values from -6.137985e-05 to 6.137985e-05
- down_second: float32 [4096, 1024], P(('cand', 'dp')), may hold values from 8.648958e-12 to 3.4595833e-11
- vector_params: float32 [15360], replicated
- vector_first: float32 [15360], P(('cand', 'dp')), may hold values from -0.0006137985 to 0.0006137985
- vector_second: float32 [15360], P(('cand', 'dp')), may hold values from 8.648958e-10 to 3.4595833e-09
Outputs:
- loss_parts: float32 [3], replicated
- grad_norm: float32 [], replicated
- score_grads: float32 [64, 6], P('dp', 'cand')
- embed_first_new: float32 [50304, 1024], P(None, 'dp')
- embed_second_new: float32 [50304, 1024], P(None, 'dp')
- embed_table_new: float32 [50304, 1024], P(None, 'dp')
- head_first_new: float32 [50304, 1024], P('dp')
- head_second_new: float32 [50304, 1024], P('dp')
- head_table_new: float32 [50304, 1024], P('dp')
- qkv_first_new: float32 [1024, 3072], P(('cand', 'dp'))
- qkv_second_new: float32 [1024, 3072], P(('cand', 'dp'))
- qkv_weight_new: float32 [1024, 3072], P(('cand', 'dp'))
- proj_first_new: float32 [1024, 1024], P(('cand', 'dp'))
- proj_second_new: float32 [1024, 1024], P(('cand', 'dp'))
- proj_weight_new: float32 [1024, 1024], P(('cand', 'dp'))
- up_first_new: float32 [1024, 4096], P(('cand', 'dp'))
- up_second_new: float32 [1024, 4096], P(('cand', 'dp'))
- up_weight_new: float32 [1024, 4096], P(('cand', 'dp'))
- down_first_new: float32 [4096, 1024], P(('cand', 'dp'))
- down_second_new: float32 [4096, 1024], P(('cand', 'dp'))
- down_weight_new: float32 [4096, 1024], P(('cand', 'dp'))
- vector_first_new: float32 [15360], P(('cand', 'dp'))
- vector_second_new: float32 [15360], P(('cand', 'dp'))
Inputs may be any that keep to these rules, and one draw needn't show every extreme that they name: `resp_lengths`: response lengths rise in spread with the prompt's index; 32 is reached in every draw. cand_rank orders the slots of a prompt; slots of rank below the prompt's count are its candidates.
All inputs are finite; a program needn't handle non-finite values. No bound on the sum of `token_mask` on one device may be relied on, other than what follows from the above.
Results may differ from a plain program's by a relative error of at most 0.03.
Values may be sent and summed in bfloat16 or wider, within the bound.
No kernel may reach another device: no remote copies, remote signals or barrier semaphores. Data moves between devices by JAX's collectives and lax.ppermute only.
A program may use at most 320 MiB of HBM per device.

v0:
```python
import jax
import jax.numpy as jnp
from jax import lax
from jax.sharding import PartitionSpec as P

D = 1024
HEADS = 16
HEAD_DIM = 64
ROT = 16
FF = 4096
SEQ = 64
STEP = 10
RESP = 32


NORM_EPS = 1e-05
CLIP_NORM = 1.0
LEARN_RATE = 0.05
BETA_ONE = 0.9
BETA_TWO = 0.999
ADAM_EPS = 1e-08
DECAY = 0.1


def merged(part, axis, combine):
    gathered = jax.tree.map(lambda a: lax.all_gather(a, axis), part)

    def take(source):
        return jax.tree.map(lambda a: lax.dynamic_index_in_dim(a, source, 0, False), gathered)

    return lax.fori_loop(
        1, lax.axis_size(axis), lambda source, state: combine(state, take(source)), take(0)
    )


def matmul(left, right):
    return jnp.dot(left, right, preferred_element_type=jnp.float32)


def matmul_tn(left, right):
    return lax.dot_general(
        left, right, (((0,), (0,)), ((), ())), preferred_element_type=jnp.float32
    )


def matmul_nt(left, right):
    return lax.dot_general(
        left, right, (((1,), (1,)), ((), ())), preferred_element_type=jnp.float32
    )


def layer_norm(inputs, gain, bias):
    mean = jnp.mean(inputs, -1, keepdims=True)
    centred = inputs - mean
    variance = jnp.mean(centred * centred, -1, keepdims=True)
    return centred * lax.rsqrt(variance + NORM_EPS) * gain + bias


def norm_back(inputs, gain, bias, grad):
    outputs, pullback = jax.vjp(layer_norm, inputs, gain, bias)
    return pullback(grad)


def rotary(inputs, sign):
    seqlen = inputs.shape[-3]
    half = ROT // 2
    freq = 10000.0 ** (-jnp.arange(half).astype(jnp.float32) * (2.0 / ROT))
    angle = jnp.arange(seqlen).astype(jnp.float32)[:, None] * freq[None, :]
    cosine = jnp.cos(angle)[:, None, :]
    sine = sign * jnp.sin(angle)[:, None, :]
    first = inputs[..., :half]
    second = inputs[..., half:ROT]
    return jnp.concatenate(
        [first * cosine - second * sine, second * cosine + first * sine, inputs[..., ROT:]], axis=-1
    )


def split_params(vector):
    spans = [D, D, D, D, D, D, 3 * D, D, FF, D]
    pieces = []
    begin = 0
    for span_len in spans:
        pieces.append(vector[begin : begin + span_len])
        begin = begin + span_len
    return pieces


def attention_probs(query, keys):
    scores = jnp.einsum(
        "cqhd,ckhd->chqk", query, keys, preferred_element_type=jnp.float32
    ) * HEAD_DIM ** (-0.5)
    causal = jnp.arange(SEQ)[:, None] >= jnp.arange(SEQ)[None, :]
    return jax.nn.softmax(jnp.where(causal, scores, -1e30), axis=-1)


def gelu_exact(values):
    return jax.nn.gelu(values, approximate=False)


def layer_forward(inputs, mats, pieces):
    qkv_w, proj_w, up_w, down_w = mats
    slots = inputs.shape[0] // SEQ
    attn_in = layer_norm(inputs, pieces[0], pieces[1]).astype(jnp.bfloat16)
    mlp_in = layer_norm(inputs, pieces[2], pieces[3]).astype(jnp.bfloat16)
    qkv = (matmul(attn_in, qkv_w) + pieces[6]).reshape(slots, SEQ, 3, HEADS, HEAD_DIM)
    query = rotary(qkv[:, :, 0], 1.0).astype(jnp.bfloat16)
    keys = rotary(qkv[:, :, 1], 1.0).astype(jnp.bfloat16)
    values = qkv[:, :, 2].astype(jnp.bfloat16)
    probs_low = attention_probs(query, keys).astype(jnp.bfloat16)
    mixed = jnp.einsum("chqk,ckhd->cqhd", probs_low, values, preferred_element_type=jnp.float32)
    mixed = mixed.astype(jnp.bfloat16).reshape(-1, D)
    up_val = matmul(mlp_in, up_w) + pieces[8]
    act = gelu_exact(up_val).astype(jnp.bfloat16)
    hidden = inputs + (matmul(mixed, proj_w) + pieces[7]) + (matmul(act, down_w) + pieces[9])
    return (hidden, (attn_in, mlp_in, query, keys, values, mixed, up_val, act))


def layer_backward(inputs, saved, mats, pieces, grad_hidden):
    qkv_w, proj_w, up_w, down_w = mats
    attn_in, mlp_in, query, keys, values, mixed, up_val, act = saved
    slots = inputs.shape[0] // SEQ
    grad_low = grad_hidden.astype(jnp.bfloat16)
    grad_sum = jnp.sum(grad_low.astype(jnp.float32), 0)
    down_grad = matmul_tn(act, grad_low)
    act_grad = matmul_nt(grad_low, down_w)
    gelu_out, gelu_pull = jax.vjp(gelu_exact, up_val)
    up_grad_low = gelu_pull(act_grad)[0].astype(jnp.bfloat16)
    up_w_grad = matmul_tn(mlp_in, up_grad_low)
    mlp_in_grad = matmul_nt(up_grad_low, up_w)
    proj_grad = matmul_tn(mixed, grad_low)
    mixed_grad = (
        matmul_nt(grad_low, proj_w).astype(jnp.bfloat16).reshape(slots, SEQ, HEADS, HEAD_DIM)
    )
    probs = attention_probs(query, keys)
    probs_low = probs.astype(jnp.bfloat16)
    probs_grad = jnp.einsum(
        "cqhd,ckhd->chqk", mixed_grad, values, preferred_element_type=jnp.float32
    )
    value_grad = jnp.einsum(
        "chqk,cqhd->ckhd", probs_low, mixed_grad, preferred_element_type=jnp.float32
    )
    score_grad = probs * (probs_grad - jnp.sum(probs * probs_grad, -1, keepdims=True))
    score_grad = score_grad.astype(jnp.bfloat16)
    scale = HEAD_DIM ** (-0.5)
    query_grad = (
        jnp.einsum("chqk,ckhd->cqhd", score_grad, keys, preferred_element_type=jnp.float32) * scale
    )
    key_grad = (
        jnp.einsum("chqk,cqhd->ckhd", score_grad, query, preferred_element_type=jnp.float32) * scale
    )
    qkv_grad = jnp.stack([rotary(query_grad, -1.0), rotary(key_grad, -1.0), value_grad], axis=2)
    qkv_grad = qkv_grad.reshape(-1, 3 * D).astype(jnp.bfloat16)
    qkv_w_grad = matmul_tn(attn_in, qkv_grad)
    attn_in_grad = matmul_nt(qkv_grad, qkv_w)
    input_one, gain_one_grad, bias_one_grad = norm_back(inputs, pieces[0], pieces[1], attn_in_grad)
    input_two, gain_two_grad, bias_two_grad = norm_back(inputs, pieces[2], pieces[3], mlp_in_grad)
    input_grad = grad_hidden + input_one + input_two
    vector_head = [gain_one_grad, bias_one_grad, gain_two_grad, bias_two_grad]
    vector_tail = [
        jnp.sum(qkv_grad.astype(jnp.float32), 0),
        grad_sum,
        jnp.sum(up_grad_low.astype(jnp.float32), 0),
        grad_sum,
    ]
    return (input_grad, (qkv_w_grad, proj_grad, up_w_grad, down_grad), vector_head, vector_tail)


def pro_single(scores, weight, ranks, count):
    valid = ranks < count
    head = ranks < count - 1
    peak = jnp.max(jnp.where(valid, scores, -1e30))
    expo = jnp.where(valid, jnp.exp(scores - peak), 0.0)
    later = ranks[None, :] >= ranks[:, None]
    suffix = jnp.sum(jnp.where(later, expo[None, :], 0.0), -1)
    return jnp.sum(
        jnp.where(head, -weight * (scores - peak - jnp.log(jnp.where(head, suffix, 1.0))), 0.0)
    )


def combine_rows(first, second):
    biggest = jnp.maximum(first[0], second[0])
    totals = first[1] * jnp.exp(first[0] - biggest) + second[1] * jnp.exp(second[0] - biggest)
    return (biggest, totals, first[2] + second[2], first[3] + second[3])


def moments(first, second, grad, factor):
    clipped = grad * factor
    first_new = BETA_ONE * first + (1.0 - BETA_ONE) * clipped
    second_new = BETA_TWO * second + (1.0 - BETA_TWO) * clipped * clipped
    return (first_new, second_new)


def adam_update(weight, first, second, grad, factor):
    first_new, second_new = moments(first, second, grad, factor)
    first_hat = first_new / (1.0 - BETA_ONE**STEP)
    second_hat = second_new / (1.0 - BETA_TWO**STEP)
    weight_new = weight - LEARN_RATE * (
        first_hat / (jnp.sqrt(second_hat) + ADAM_EPS) + DECAY * weight
    )
    return (first_new, second_new, weight_new)


def body(
    token_ids,
    token_mask,
    resp_lengths,
    cand_counts,
    cand_rank,
    rewards,
    embed_table,
    embed_first,
    embed_second,
    head_table,
    head_first,
    head_second,
    qkv_weight,
    qkv_first,
    qkv_second,
    proj_weight,
    proj_first,
    proj_second,
    up_weight,
    up_first,
    up_second,
    down_weight,
    down_first,
    down_second,
    vector_params,
    vector_first,
    vector_second,
):
    slots = token_ids.shape[1]
    pieces = split_params(vector_params)
    group_ids = lax.all_gather(token_ids, "dp", axis=0, tiled=True)
    flat_ids = group_ids.reshape(-1)
    looked = jnp.take(embed_table.astype(jnp.bfloat16), flat_ids, axis=0)
    inputs = lax.all_to_all(looked, "dp", split_axis=0, concat_axis=1, tiled=True).astype(
        jnp.float32
    )
    mats = (
        lax.all_gather(qkv_weight.astype(jnp.bfloat16), ("cand", "dp"), axis=0, tiled=True),
        lax.all_gather(proj_weight.astype(jnp.bfloat16), ("cand", "dp"), axis=0, tiled=True),
        lax.all_gather(up_weight.astype(jnp.bfloat16), ("cand", "dp"), axis=0, tiled=True),
        lax.all_gather(down_weight.astype(jnp.bfloat16), ("cand", "dp"), axis=0, tiled=True),
    )
    hidden, saved = layer_forward(inputs, mats, pieces)
    rows_in = hidden.reshape(slots, SEQ, D)[:, SEQ - RESP - 1 : SEQ - 1].reshape(-1, D)
    rows_low = layer_norm(rows_in, pieces[4], pieces[5]).astype(jnp.bfloat16)
    group_rows = lax.all_gather(rows_low, "dp", axis=0, tiled=True)
    head_low = head_table.astype(jnp.bfloat16)
    logits = matmul_nt(group_rows, head_low)
    vocab_local = head_table.shape[0]
    targets = group_ids[:, :, SEQ - RESP :].reshape(-1) - lax.axis_index("dp") * vocab_local
    hits = jnp.arange(vocab_local)[None, :] == targets[:, None]
    local_max = jnp.max(logits, -1)
    local_sum = jnp.sum(jnp.exp(logits - local_max[:, None]), -1)
    local_target = jnp.sum(jnp.where(hits, logits, 0.0), -1)
    live = (
        (jnp.arange(RESP)[None, None, :] < resp_lengths[:, :, None]) & (token_mask == 1)
    ).astype(jnp.float32)
    valid = (cand_rank < cand_counts[:, None]).astype(jnp.float32)
    top_mask = (cand_rank == 0).astype(jnp.float32)
    local_stats = jnp.stack(
        [
            jnp.sum(valid),
            jnp.sum(rewards * valid),
            jnp.sum(rewards * rewards * valid),
            jnp.sum(live * top_mask[..., None]),
        ]
    )
    merged_max, merged_sum, merged_target, stats_dp = merged(
        (local_max, local_sum, local_target, local_stats), "dp", combine_rows
    )
    row_lse = merged_max + jnp.log(merged_sum)
    group_logp = merged_target - row_lse
    own_logp = lax.dynamic_slice_in_dim(
        group_logp, lax.axis_index("dp") * (slots * RESP), slots * RESP
    ).reshape(1, slots, RESP)
    own_count = jnp.sum(live, -1)
    own_scores = jnp.sum(own_logp * live, -1) / jnp.maximum(own_count, 1.0)
    all_scores, all_rank_f, all_rewards, stats_two = (
        lax.all_gather(own_scores.reshape(-1), "cand", axis=0, tiled=True),
        lax.all_gather(cand_rank.reshape(-1).astype(jnp.float32), "cand", axis=0, tiled=True),
        lax.all_gather(rewards.reshape(-1), "cand", axis=0, tiled=True),
        lax.all_gather(stats_dp, "cand", axis=0, tiled=True),
    )
    stats = stats_two[:4] + stats_two[4:]
    mean = stats[1] / stats[0]
    variance = stats[2] / stats[0] - mean * mean
    weight = jax.nn.softplus((all_rewards - mean) * lax.rsqrt(variance + NORM_EPS))
    pro_value, pro_grad = jax.value_and_grad(pro_single)(
        all_scores, weight, all_rank_f.astype(jnp.int32), cand_counts[0]
    )
    my_grad = lax.dynamic_slice_in_dim(pro_grad, lax.axis_index("cand") * slots, slots).reshape(
        1, slots
    )
    prompts_all = lax.axis_size("dp") * token_ids.shape[0]
    sft_scale = prompts_all / jnp.maximum(stats[3], 1.0)
    row_grad = (
        my_grad[..., None] / jnp.maximum(own_count, 1.0)[..., None]
        - sft_scale * top_mask[..., None]
    ) * live
    group_grad = lax.all_gather(row_grad.reshape(-1), "dp", axis=0, tiled=True)
    vocab_probs = jnp.exp(logits - row_lse[:, None])
    logit_grad = (group_grad[:, None] * (hits.astype(jnp.float32) - vocab_probs)).astype(
        jnp.bfloat16
    )
    head_grad = matmul_tn(logit_grad, group_rows)
    rows_grad = lax.psum_scatter(
        matmul(logit_grad, head_low), "dp", scatter_dimension=0, tiled=True
    )
    rows_in_grad, gain_fin_grad, bias_fin_grad = norm_back(rows_in, pieces[4], pieces[5], rows_grad)
    grad_hidden = jnp.pad(
        rows_in_grad.reshape(slots, RESP, D), ((0, 0), (SEQ - RESP - 1, 1), (0, 0))
    ).reshape(-1, D)
    input_grad, mat_grads, vector_head, vector_tail = layer_backward(
        inputs, saved, mats, pieces, grad_hidden
    )
    embed_rows = lax.all_to_all(input_grad, "dp", split_axis=1, concat_axis=0, tiled=True)
    embed_grad = jax.ops.segment_sum(embed_rows, flat_ids, num_segments=embed_table.shape[0])
    embed_grad, head_grad = lax.psum((embed_grad, head_grad), "cand")
    vector_grad = jnp.concatenate(vector_head + [gain_fin_grad, bias_fin_grad] + vector_tail)
    grads = (mat_grads[0], mat_grads[1], mat_grads[2], mat_grads[3], vector_grad)
    shards = (
        lax.psum_scatter(grads[0], ("cand", "dp"), scatter_dimension=0, tiled=True),
        lax.psum_scatter(grads[1], ("cand", "dp"), scatter_dimension=0, tiled=True),
        lax.psum_scatter(grads[2], ("cand", "dp"), scatter_dimension=0, tiled=True),
        lax.psum_scatter(grads[3], ("cand", "dp"), scatter_dimension=0, tiled=True),
        lax.psum_scatter(grads[4], ("cand", "dp"), scatter_dimension=0, tiled=True),
    )
    pair_count = lax.axis_size("cand")
    local_squares = sum((jnp.sum(piece * piece) for piece in shards))
    local_squares = (
        local_squares
        + (jnp.sum(embed_grad * embed_grad) + jnp.sum(head_grad * head_grad)) / pair_count
    )
    sft_local = -jnp.sum(own_logp * live * top_mask[..., None])
    squares, pro_total, sft_total = lax.psum(
        (local_squares, pro_value / pair_count, sft_local), ("cand", "dp")
    )
    grad_norm = jnp.sqrt(squares)
    factor = jnp.minimum(1.0, CLIP_NORM / (grad_norm + 1e-06))
    embed_new = adam_update(embed_table, embed_first, embed_second, embed_grad, factor)
    head_new = adam_update(head_table, head_first, head_second, head_grad, factor)
    qkv_new = adam_update(qkv_weight, qkv_first, qkv_second, shards[0], factor)
    proj_new = adam_update(proj_weight, proj_first, proj_second, shards[1], factor)
    up_new = adam_update(up_weight, up_first, up_second, shards[2], factor)
    down_new = adam_update(down_weight, down_first, down_second, shards[3], factor)
    vector_first_new, vector_second_new = moments(vector_first, vector_second, shards[4], factor)
    loss_parts = jnp.stack([pro_total, sft_total, stats[3]])
    return (
        loss_parts,
        grad_norm,
        my_grad,
        embed_new[0],
        embed_new[1],
        embed_new[2],
        head_new[0],
        head_new[1],
        head_new[2],
        qkv_new[0],
        qkv_new[1],
        qkv_new[2],
        proj_new[0],
        proj_new[1],
        proj_new[2],
        up_new[0],
        up_new[1],
        up_new[2],
        down_new[0],
        down_new[1],
        down_new[2],
        vector_first_new,
        vector_second_new,
    )


def solution(mesh):
    in_specs = (
        P("dp", "cand", None),
        P("dp", "cand", None),
        P("dp", "cand"),
        P("dp"),
        P("dp", "cand"),
        P("dp", "cand"),
        P(None, "dp"),
        P(None, "dp"),
        P(None, "dp"),
        P("dp", None),
        P("dp", None),
        P("dp", None),
        P(("cand", "dp"), None),
        P(("cand", "dp"), None),
        P(("cand", "dp"), None),
        P(("cand", "dp"), None),
        P(("cand", "dp"), None),
        P(("cand", "dp"), None),
        P(("cand", "dp"), None),
        P(("cand", "dp"), None),
        P(("cand", "dp"), None),
        P(("cand", "dp"), None),
        P(("cand", "dp"), None),
        P(("cand", "dp"), None),
        P(),
        P(("cand", "dp")),
        P(("cand", "dp")),
    )
    out_specs = (
        P(),
        P(),
        P("dp", "cand"),
        P(None, "dp"),
        P(None, "dp"),
        P(None, "dp"),
        P("dp", None),
        P("dp", None),
        P("dp", None),
        P(("cand", "dp"), None),
        P(("cand", "dp"), None),
        P(("cand", "dp"), None),
        P(("cand", "dp"), None),
        P(("cand", "dp"), None),
        P(("cand", "dp"), None),
        P(("cand", "dp"), None),
        P(("cand", "dp"), None),
        P(("cand", "dp"), None),
        P(("cand", "dp"), None),
        P(("cand", "dp"), None),
        P(("cand", "dp"), None),
        P(("cand", "dp")),
        P(("cand", "dp")),
    )
    return jax.shard_map(body, mesh=mesh, in_specs=in_specs, out_specs=out_specs, check_vma=False)
```

profile of v0, /device:TPU:1, one launch (start us, length us, event | category | flops | bytes accessed | tf_op | source)
XLA Modules:
  0.0 3885.3 jit_solution(16475570700077652872)
XLA Ops:
  12.7 152.2 %all_gather.59 = s32[64,3,64]{2,1,0:T(4,128)S(1)} all-gather(s32[1,3,64]{2,1,0:T(4,128)S(1)} %copy.213), channel_id=1, replica_groups=mesh['cand'=2,'dp'=64] {'dp'}, dimensions={0}, use_global_device_ids=true | all-gather | bytes 49920 | tf_op jit(solution)/shard_map/all_gather | solution.py:234
  176.0 39.1 %gather_fusion = bf16[12288,16]{1,0:T(8,128)(2,1)S(1)} fusion(bf16[50304,16]{1,0:T(8,128)(2,1)} %copy.216, s32[12288]{0:T(1024)S(1)} %broadcast_clamp_fusion), kind=kCustom, calls=%fused_computation | custom fusion | bytes 835584 | tf_op jit(solution)/shard_map/jit(_take)/gather | solution.py:236
  262.9 12.8 multiply_convert_fusion.1
  282.3 41.9 %all-gather.17.cloned.1.call-done = bf16[1024,1024]{1,0:T(8,128)(2,1)} async-done(((bf16[8,1024]{1,0:T(8,128)(2,1)}), bf16[1024,1024]{1,0:T(8,128)(2,1)}) %all-gather.17.cloned.1.call-update) | async-done | bytes 2097168 | tf_op jit(solution)/shard_map/all_gather | solution.py:242
  328.0 88.2 %all-gather.23.cloned.1.call-done = bf16[6144,1024]{1,0:T(8,128)(2,1)} async-done(((bf16[96,1024]{1,0:T(8,128)(2,1)}), bf16[6144,1024]{1,0:T(8,128)(2,1)}) %all-gather.23.cloned.1.call-update) | async-done | bytes 12582928 | tf_op jit(solution)/shard_map/all_gather | solution.py:249
  416.2 18.5 fusion.73
  435.2 10.7 select_reduce_fusion
  452.6 148.8 %all-reduce.3 = f32[256]{0:T(256)S(1)} all-reduce(f32[256]{0:T(256)S(1)} %maximum_dynamic-update-slice_fusion), channel_id=7, replica_groups=mesh['cand'=2,'dp'=64] {'dp'}, use_global_device_ids=true, to_apply=%add.3 | all-reduce | flops 256 | bytes 2048
  608.6 20.4 all-gather.29.cloned.1.call-done
  631.6 74.9 %while.21 = (s32[]{:T(128)}, f32[6144]{0:T(1024)S(1)}, f32[6144]{0:T(1024)S(1)}, f32[6144]{0:T(1024)S(1)}, f32[4]{0:T(128)S(1)}, /*index=5*/f32[64,6144]{1,0:T(8...) while((s32[]{:T(128)}, f32[6144]{0:T(1024)S(1)}, ...), condition=%wide.region_14.15_spmd, body=%wide.region_13.14_spmd.sunk | while | flops 43017 | bytes 368851 | solution.py:31
  707.7 11.0 all-reduce.9
  729.2 286.1 %all-reduce.6 = f32[6144]{0:T(1024)S(1)} all-reduce(f32[6144]{0:T(1024)S(1)} %dynamic-update-slice.5), channel_id=1, replica_groups=mesh['cand'=2,'dp'=64] {'dp'}, use_global_device_ids=true, to_apply=%add.6 | all-reduce | flops 6144 | bytes 49152
  1015.3 23.9 fusion.18
  1040.6 294.2 %reduce-scatter.6.cloned.1.call-done = f32[96,1024]{1,0:T(8,128)} async-done(((f32[6144,1024]{1,0:T(8,128)}), f32[96,1024]{1,0:T(8,128)}) %reduce-scatter.6.cloned.1.call-update) | async-done | bytes 393232 | tf_op jit(solution)/shard_map/reduce_scatter | solution.py:309
  1385.0 19.9 fusion.56
  1409.1 76.1 %scatter_custom_fusion = f32[50304,16]{1,0:T(8,128)} fusion(s32[12288]{0:T(1024)} %reshape.501, f32[12288,16]{1,0:T(8,128)} %bitcast.136, f32[]{:T(128)} %constant.104.clone.1), kind=kCustom, calls=%fused_computation.14 | custom fusion | flops 196608 | bytes 3219968 | tf_op jit(solution)/shard_map/scatter-add | solution.py:320
  1485.1 14.9 copy.242
  1513.3 9.3 fusion.55
  1534.8 68.3 %all-reduce.7 = f32[15360]{0:T(1024)S(1)} all-reduce(f32[15360]{0:T(1024)S(1)} %constant_dynamic-update-slice_fusion), channel_id=13, replica_groups=mesh['cand'=2,'dp'=64] {'cand','dp'}, use_global_device_ids=true, to_apply=%region_48.49.clone | all-reduce | flops 15360 | bytes 122880
  1611.9 592.2 %reduce-scatter.10.cloned.1.call-done = f32[8,1024]{1,0:T(8,128)} async-done(((f32[1024,1024]{1,0:T(8,128)}), f32[8,1024]{1,0:T(8,128)}) %reduce-scatter.10.cloned.1.call-update) | async-done | bytes 32784 | tf_op jit(solution)/shard_map/reduce_scatter | solution.py:326
  2205.5 222.8 %reduce-scatter.8.cloned.1.call-done = f32[8,3072]{1,0:T(8,128)} async-done(((f32[1024,3072]{1,0:T(8,128)}), f32[8,3072]{1,0:T(8,128)}) %reduce-scatter.8.cloned.1.call-update) | async-done | bytes 98320 | tf_op jit(solution)/shard_map/reduce_scatter | solution.py:325
  2431.1 679.7 %reduce-scatter.12.cloned.1.call-done = f32[8,4096]{1,0:T(8,128)} async-done(((f32[1024,4096]{1,0:T(8,128)}), f32[8,4096]{1,0:T(8,128)}) %reduce-scatter.12.cloned.1.call-update) | async-done | bytes 131088 | tf_op jit(solution)/shard_map/reduce_scatter | solution.py:327
  3113.1 675.4 %reduce-scatter.14.cloned.1.call-done = f32[32,1024]{1,0:T(8,128)} async-done(((f32[4096,1024]{1,0:T(8,128)}), f32[32,1024]{1,0:T(8,128)}) %reduce-scatter.14.cloned.1.call-update) | async-done | bytes 131088 | tf_op jit(solution)/shard_map/reduce_scatter | solution.py:328
  3791.3 63.0 %all-reduce.8 = (f32[1]{0:T(128)}, f32[1]{0:T(128)}, f32[]{:T(128)}) all-reduce(f32[1]{0:T(128)} %bitcast.31, f32[1]{0:T(128)} %bitcast.30, f32[]{:T(128)S(6)} %add.416), channel_id=1, replica_groups=mesh['cand'=2,'dp'=64] {'cand','dp'}, use_global_device_ids=true, to_apply=%region_22.23 | all-reduce | flops 3 | bytes 24 | tf_op jit(solution)/shard_map/psum | solution.py:338
  (691 shorter events, 280.9 us)
Async XLA Ops:
  7.2 229.3 %all-gather.15.cloned.1.call-start = ((), (), s32[]{:S(2)}) async-start(), calls=%async_computation.7 | async-start | bytes 6340608 | tf_op jit(solution)/shard_map/all_gather | solution.py:241
  8.8 254.1 %all-gather.19.cloned.1.call-start = ((), (), s32[]{:S(2)}) async-start(), calls=%async_computation.9 | async-start | bytes 8454144 | tf_op jit(solution)/shard_map/all_gather | solution.py:243
  10.4 265.3 %all-gather.21.cloned.1.call-start = ((), (), s32[]{:S(2)}) async-start(), calls=%async_computation.10 | async-start | bytes 8454144 | tf_op jit(solution)/shard_map/all_gather | solution.py:244
  220.0 15.3 all-to-all-start
  224.8 99.5 %all-gather.17.cloned.1.call-start = ((), (), s32[]{:S(2)}) async-start(), calls=%async_computation.8 | async-start | bytes 2113536 | tf_op jit(solution)/shard_map/all_gather | solution.py:242
  225.5 190.7 %all-gather.23.cloned.1.call-start = ((), (), s32[]{:S(2)}) async-start(), calls=%async_computation.11 | async-start | bytes 12779520 | tf_op jit(solution)/shard_map/all_gather | solution.py:249
  328.0 276.3 %all-gather.25.cloned.1.call-start = ((), (), s32[]{:S(2)}) async-start(), calls=%async_computation.17 | async-start | bytes 1597440 | tf_op jit(solution)/shard_map/all_gather | solution.py:26
  434.8 171.1 %all-gather.27.cloned.1.call-start = ((), (), s32[]{:S(2)}) async-start(), calls=%async_computation.18 | async-start | bytes 1597440 | tf_op jit(solution)/shard_map/all_gather | solution.py:26
  435.1 580.2 %copy-start.46 = (s32[6144]{0:T(1024)}, s32[6144]{0:T(1024)S(1)}, u32[]{:S(2)}) copy-start(s32[6144]{0:T(1024)S(1)} %sub.193) | copy-start | bytes 73732
  435.1 167.1 %copy-start.78 = (u32[128]{0:T(128)S(1)}, u32[128]{0:T(128)}, u32[]{:S(2)}) copy-start(u32[128]{0:T(128)} %constant.327) | copy-start | bytes 1540
  445.9 183.1 %all-gather.29.cloned.1.call-start = ((), (), s32[]{:S(2)}) async-start(), calls=%async_computation.19 | async-start | bytes 1597440 | tf_op jit(solution)/shard_map/all_gather | solution.py:26
  446.6 888.3 %reduce-scatter.6.cloned.1.call-start = ((), (), s32[]{:S(2)}) async-start(), calls=%async_computation.12 | async-start | bytes 25559040 | tf_op jit(solution)/shard_map/reduce_scatter | solution.py:309
  706.6 332.6 %copy-start.56 = (f32[6144]{0:T(1024)}, f32[6144]{0:T(1024)S(1)}, u32[]{:S(2)}) copy-start(f32[6144]{0:T(1024)S(1)} %log_add_fusion) | copy-start | bytes 73732
  1039.2 297.5 %copy-start.76 = (f32[96]{0:T(128)S(1)}, f32[96]{0:T(128)}, u32[]{:S(2)}) copy-start(f32[96]{0:T(128)} %copy-done.75) | copy-start | bytes 1156
  1039.2 300.6 %copy-start.4 = (bf16[1024,1024]{1,0:T(8,128)(2,1)S(1)}, bf16[1024,1024]{1,0:T(8,128)(2,1)}, u32[]{:S(2)}) copy-start(bf16[1024,1024]{1,0:T(8,128)(2,1)} %all-gather.17.cloned.1.call-done) | copy-start | bytes 6291460
  1378.1 26.8 all-to-all-start.1
  1384.9 218.9 %all-reduce.13.cloned.1.call-start = ((), (), s32[]{:S(2)}) async-start(), calls=%async_computation.20 | async-start | bytes 12926976 | tf_op jit(solution)/shard_map/psum | solution.py:321
  1500.0 704.1 %reduce-scatter.10.cloned.1.call-start = ((), (), s32[]{:S(2)}) async-start(), calls=%async_computation.14 | async-start | bytes 4227072 | tf_op jit(solution)/shard_map/reduce_scatter | solution.py:326
  1503.7 924.6 %reduce-scatter.8.cloned.1.call-start = ((), (), s32[]{:S(2)}) async-start(), calls=%async_computation.13 | async-start | bytes 12681216 | tf_op jit(solution)/shard_map/reduce_scatter | solution.py:325
  1511.4 1599.4 %reduce-scatter.12.cloned.1.call-start = ((), (), s32[]{:S(2)}) async-start(), calls=%async_computation.15 | async-start | bytes 16908288 | tf_op jit(solution)/shard_map/reduce_scatter | solution.py:327
  1522.7 2265.8 %reduce-scatter.14.cloned.1.call-start = ((), (), s32[]{:S(2)}) async-start(), calls=%async_computation.16 | async-start | bytes 16908288 | tf_op jit(solution)/shard_map/reduce_scatter | solution.py:328
  1603.7 2253.8 %copy-start.73 = (f32[120]{0:T(128)S(1)}, f32[120]{0:T(128)}, u32[]{:S(2)}) copy-start(f32[120]{0:T(128)} %param.55) | copy-start | bytes 1444
  1603.8 2253.8 %copy-start.74 = (f32[120]{0:T(128)S(1)}, f32[120]{0:T(128)}, u32[]{:S(2)}) copy-start(f32[120]{0:T(128)} %param.54) | copy-start | bytes 1444
  1603.8 2254.4 %copy-start.3 = (f32[50304,16]{0,1:T(8,128)S(1)}, f32[50304,16]{0,1:T(8,128)}, u32[]{:S(2)}) copy-start(f32[50304,16]{0,1:T(8,128)} %param.35) | copy-start | bytes 9658372
  (81 other events, 737.7 us)
Sparse Core Ops, SparseCore 0:
  11.7 71.8 all-gather.14
  87.3 67.8 all-gather.18
  158.9 67.6 all-gather.20
  230.0 94.2 all-gather.16
  328.1 88.0 all-gather.22
  434.9 62.8 all-gather.24
  501.2 62.0 all-gather.26
  566.6 62.2 all-gather.28
  1039.3 295.5 reduce-scatter.5
  1500.2 41.4 all-reduce.12
  1544.0 660.1 reduce-scatter.9
  2209.7 218.5 reduce-scatter.7
  2430.8 680.0 reduce-scatter.11
  3113.2 675.1 reduce-scatter.13
where the time goes:
time: 3890 us
  waiting for transfers between devices  2620 us (67%)
  blocking collectives  729 us (19%)
  local copies, waits for them, and re-layouts  185 us (5%)
  other arithmetic  154 us (4%)
  matrix products  144 us (4%)
    reduce_scatter x1, waiting for transfers between devices, body(): lax.psum_scatter(grads[2], ('cand', 'dp'), scatter_dimension=0, tiled=True)  680 us
    reduce_scatter x1, waiting for transfers between devices, body(): lax.psum_scatter(grads[3], ('cand', 'dp'), scatter_dimension=0, tiled=True)  675 us
    reduce_scatter x1, waiting for transfers between devices, body(): lax.psum_scatter(grads[1], ('cand', 'dp'), scatter_dimension=0, tiled=True)  592 us
    unnamed x4, blocking collectives  514 us
    reduce_scatter x1, waiting for transfers between devices, body(): lax.psum_scatter(matmul(logit_grad, head_low), 'dp', scatter_dimension=0,...  294 us
    reduce_scatter x1, waiting for transfers between devices, body(): lax.psum_scatter(grads[0], ('cand', 'dp'), scatter_dimension=0, tiled=True)  223 us
    all_gather x1, blocking collectives, body(): group_ids = lax.all_gather(token_ids, 'dp', axis=0, tiled=True)  152 us
    all_gather x1, waiting for transfers between devices, body(): group_rows = lax.all_gather(rows_low, 'dp', axis=0, tiled=True)  88.2 us
  transfers between devices with their start and end apart: 16, of which 9 were waited for; matrix products, arithmetic and copies ran while one was open for 5% of the time, Pallas kernels for 0%

commit v1 on v0

v1 whole, which is shorter than its diff:
```python
import jax
import jax.numpy as jnp
from jax import lax
from jax.sharding import Mesh
from jax.sharding import PartitionSpec as P

D = 1024
HEADS = 16
HEAD_DIM = 64
ROT = 16
FF = 4096
SEQ = 64
STEP = 10
RESP = 32


NORM_EPS = 1e-05
CLIP_NORM = 1.0
LEARN_RATE = 0.05
BETA_ONE = 0.9
BETA_TWO = 0.999
ADAM_EPS = 1e-08
DECAY = 0.1


RING = 4
VOCAB_PAD = 896
AXES = ("x", "y", "z")


def shift(value, axis, step):
    return lax.ppermute(value, axis, [(i, (i + step) % RING) for i in range(RING)])


def swap(value):
    return lax.ppermute(value, "cand", [(0, 1), (1, 0)])


def near_gather(value, axis):
    return jnp.stack([value, shift(value, axis, -1), shift(value, axis, 2), shift(value, axis, 1)])


def near_scatter(pieces, axis):
    return [pieces[0], shift(pieces[1], axis, 1), shift(pieces[2], axis, 2), shift(pieces[3], axis, -1)]


def total(value, axis):
    near = shift(value, axis, 1) + shift(value, axis, -1)
    return (value + shift(value, axis, 2)) + near


def total_all(value):
    value = value + swap(value)
    for axis in AXES:
        value = total(value, axis)
    return value


def halves(value):
    mid = value.shape[-1] // 2
    return (value[..., :mid], value[..., mid:])


def ring_gather(value, axis):
    before = shift(value, axis, 1)
    after = shift(value, axis, -1)
    far = jnp.concatenate(
        [shift(halves(before)[0], axis, 1), shift(halves(after)[1], axis, -1)], axis=-1
    )
    return [value, after, far, before]


def add_low(first, second):
    return (first.astype(jnp.float32) + second.astype(jnp.float32)).astype(first.dtype)


def ring_scatter(chunks, axis):
    own, after, far, before = chunks
    far_a, far_b = halves(far)
    after_a, after_b = halves(after)
    before_a, before_b = halves(before)
    got_a = shift(far_a, axis, -1)
    got_b = shift(far_b, axis, 1)
    from_after_b = shift(before_b, axis, -1)
    from_before_a = shift(after_a, axis, 1)
    from_after_a = shift(add_low(before_a, got_a), axis, -1)
    from_before_b = shift(add_low(after_b, got_b), axis, 1)
    from_after = jnp.concatenate([from_after_a, from_after_b], axis=-1).astype(jnp.float32)
    from_before = jnp.concatenate([from_before_a, from_before_b], axis=-1).astype(jnp.float32)
    return own.astype(jnp.float32) + (from_after + from_before)


def rolled_chunks(value, axis, dim):
    me = lax.axis_index(axis)
    return [
        lax.dynamic_index_in_dim(value, (me + k) % RING, dim, keepdims=False) for k in range(RING)
    ]


def owner_sum(grad, order):
    rows = grad.shape[0] // 128
    parts = grad.reshape(2, 64 * rows, grad.shape[1])
    core = lax.axis_index("cand")
    sent = swap(lax.dynamic_index_in_dim(parts, 1 - core, 0, keepdims=False))
    kept = lax.dynamic_index_in_dim(parts, core, 0, keepdims=False)
    value = add_low(kept, sent).reshape(RING, RING, RING, rows, -1)
    left = list(AXES)
    for axis in order:
        dim = left.index(axis)
        value = ring_scatter(rolled_chunks(value, axis, dim), axis)
        left.remove(axis)
        if left:
            value = value.astype(jnp.bfloat16)
    return value


def owner_sum_small(vector):
    parts = vector.reshape(2, RING, RING, RING, -1)
    core = lax.axis_index("cand")
    sent = swap(lax.dynamic_index_in_dim(parts, 1 - core, 0, keepdims=False))
    value = lax.dynamic_index_in_dim(parts, core, 0, keepdims=False) + sent
    for axis in AXES:
        got = near_scatter(rolled_chunks(value, axis, 0), axis)
        value = (got[0] + got[2]) + (got[1] + got[3])
    return value


def matmul(left, right):
    return jnp.dot(left, right, preferred_element_type=jnp.float32)


def matmul_tn(left, right):
    return lax.dot_general(
        left, right, (((0,), (0,)), ((), ())), preferred_element_type=jnp.float32
    )


def matmul_nt(left, right):
    return lax.dot_general(
        left, right, (((1,), (1,)), ((), ())), preferred_element_type=jnp.float32
    )


def layer_norm(inputs, gain, bias):
    mean = jnp.mean(inputs, -1, keepdims=True)
    centred = inputs - mean
    variance = jnp.mean(centred * centred, -1, keepdims=True)
    return centred * lax.rsqrt(variance + NORM_EPS) * gain + bias


def norm_back(inputs, gain, bias, grad):
    outputs, pullback = jax.vjp(layer_norm, inputs, gain, bias)
    return pullback(grad)


def split_params(vector):
    spans = [D, D, D, D, D, D, 3 * D, D, FF, D]
    pieces = []
    begin = 0
    for span_len in spans:
        pieces.append(vector[begin : begin + span_len])
        begin = begin + span_len
    return pieces


def gelu_exact(values):
    return jax.nn.gelu(values, approximate=False)


def rotary(inputs, places, sign):
    half = ROT // 2
    freq = 10000.0 ** (-jnp.arange(half).astype(jnp.float32) * (2.0 / ROT))
    angle = places.astype(jnp.float32)[:, None] * freq[None, :]
    cosine = jnp.cos(angle)[:, None, :]
    sine = sign * jnp.sin(angle)[:, None, :]
    first = inputs[..., :half]
    second = inputs[..., half:ROT]
    return jnp.concatenate(
        [first * cosine - second * sine, second * cosine + first * sine, inputs[..., ROT:]], axis=-1
    )


def key_places():
    return (jnp.arange(SEQ) + (SEQ - RESP - 1)) % SEQ


def attention_probs(query, keys):
    scores = jnp.einsum(
        "cqhd,ckhd->chqk", query, keys, preferred_element_type=jnp.float32
    ) * HEAD_DIM ** (-0.5)
    places = key_places()
    causal = places[:RESP, None] >= places[None, :]
    return jax.nn.softmax(jnp.where(causal, scores, -1e30), axis=-1)


def joined(rows, slots):
    cut = rows.reshape(2, slots, RESP, *rows.shape[1:])
    return jnp.concatenate([cut[0], cut[1]], axis=1)


def parted(rows):
    cut = jnp.stack([rows[:, :RESP], rows[:, RESP:]])
    return cut.reshape(-1, *rows.shape[2:])


def layer_forward(inputs, mats, pieces):
    query_w, kv_w, proj_w, up_w, down_w = mats
    live = inputs.shape[0] // 2
    slots = live // RESP
    first = inputs[:live]
    attn_in = layer_norm(inputs, pieces[0], pieces[1]).astype(jnp.bfloat16)
    mlp_in = layer_norm(first, pieces[2], pieces[3]).astype(jnp.bfloat16)
    query = matmul(attn_in[:live], query_w) + pieces[6][:D]
    both = matmul(attn_in, kv_w) + pieces[6][D:]
    query = rotary(query.reshape(slots, RESP, HEADS, HEAD_DIM), key_places()[:RESP], 1.0)
    keys = joined(both[:, :D], slots).reshape(slots, SEQ, HEADS, HEAD_DIM)
    keys = rotary(keys, key_places(), 1.0)
    values = joined(both[:, D:], slots).reshape(slots, SEQ, HEADS, HEAD_DIM)
    query, keys, values = [part.astype(jnp.bfloat16) for part in (query, keys, values)]
    probs_low = attention_probs(query, keys).astype(jnp.bfloat16)
    mixed = jnp.einsum("chqk,ckhd->cqhd", probs_low, values, preferred_element_type=jnp.float32)
    mixed = mixed.astype(jnp.bfloat16).reshape(-1, D)
    up_val = matmul(mlp_in, up_w) + pieces[8]
    act = gelu_exact(up_val).astype(jnp.bfloat16)
    hidden = first + (matmul(mixed, proj_w) + pieces[7]) + (matmul(act, down_w) + pieces[9])
    return (hidden, (attn_in, mlp_in, query, keys, values, mixed, up_val, act))


def layer_backward(inputs, saved, mats, pieces, grad_hidden):
    query_w, kv_w, proj_w, up_w, down_w = mats
    attn_in, mlp_in, query, keys, values, mixed, up_val, act = saved
    live = inputs.shape[0] // 2
    slots = live // RESP
    first = inputs[:live]
    grad_low = grad_hidden.astype(jnp.bfloat16)
    grad_sum = jnp.sum(grad_low.astype(jnp.float32), 0)
    down_grad = matmul_tn(act, grad_low).astype(jnp.bfloat16)
    act_grad = matmul_nt(grad_low, down_w)
    gelu_out, gelu_pull = jax.vjp(gelu_exact, up_val)
    up_grad_low = gelu_pull(act_grad)[0].astype(jnp.bfloat16)
    up_w_grad = matmul_tn(mlp_in, up_grad_low).astype(jnp.bfloat16)
    mlp_in_grad = matmul_nt(up_grad_low, up_w)
    proj_grad = matmul_tn(mixed, grad_low).astype(jnp.bfloat16)
    mixed_grad = (
        matmul_nt(grad_low, proj_w).astype(jnp.bfloat16).reshape(slots, RESP, HEADS, HEAD_DIM)
    )
    probs = attention_probs(query, keys)
    probs_low = probs.astype(jnp.bfloat16)
    probs_grad = jnp.einsum(
        "cqhd,ckhd->chqk", mixed_grad, values, preferred_element_type=jnp.float32
    )
    value_grad = jnp.einsum(
        "chqk,cqhd->ckhd", probs_low, mixed_grad, preferred_element_type=jnp.float32
    )
    score_grad = probs * (probs_grad - jnp.sum(probs * probs_grad, -1, keepdims=True))
    score_grad = score_grad.astype(jnp.bfloat16)
    scale = HEAD_DIM ** (-0.5)
    query_grad = (
        jnp.einsum("chqk,ckhd->cqhd", score_grad, keys, preferred_element_type=jnp.float32) * scale
    )
    key_grad = (
        jnp.einsum("chqk,cqhd->ckhd", score_grad, query, preferred_element_type=jnp.float32) * scale
    )
    query_grad = rotary(query_grad, key_places()[:RESP], -1.0).reshape(live, D)
    key_grad = rotary(key_grad, key_places(), -1.0).reshape(slots, SEQ, D)
    value_grad = value_grad.reshape(slots, SEQ, D)
    query_grad = query_grad.astype(jnp.bfloat16)
    both_grad = jnp.concatenate([parted(key_grad), parted(value_grad)], axis=1).astype(jnp.bfloat16)
    qkv_w_grad = jnp.concatenate(
        [
            matmul_tn(attn_in[:live], query_grad).astype(jnp.bfloat16),
            matmul_tn(attn_in, both_grad).astype(jnp.bfloat16),
        ],
        axis=1,
    )
    attn_in_grad = matmul_nt(both_grad, kv_w)
    attn_in_grad = attn_in_grad + jnp.pad(matmul_nt(query_grad, query_w), ((0, live), (0, 0)))
    input_one, gain_one_grad, bias_one_grad = norm_back(inputs, pieces[0], pieces[1], attn_in_grad)
    input_two, gain_two_grad, bias_two_grad = norm_back(first, pieces[2], pieces[3], mlp_in_grad)
    input_grad = input_one + jnp.pad(grad_hidden + input_two, ((0, live), (0, 0)))
    vector_head = [gain_one_grad, bias_one_grad, gain_two_grad, bias_two_grad]
    vector_tail = [
        jnp.sum(query_grad.astype(jnp.float32), 0),
        jnp.sum(both_grad.astype(jnp.float32), 0),
        grad_sum,
        jnp.sum(up_grad_low.astype(jnp.float32), 0),
        grad_sum,
    ]
    return (input_grad, (qkv_w_grad, proj_grad, up_w_grad, down_grad), vector_head, vector_tail)


def pro_single(scores, weight, ranks, count):
    valid = ranks < count
    head = ranks < count - 1
    peak = jnp.max(jnp.where(valid, scores, -1e30))
    expo = jnp.where(valid, jnp.exp(scores - peak), 0.0)
    later = ranks[None, :] >= ranks[:, None]
    suffix = jnp.sum(jnp.where(later, expo[None, :], 0.0), -1)
    return jnp.sum(
        jnp.where(head, -weight * (scores - peak - jnp.log(jnp.where(head, suffix, 1.0))), 0.0)
    )


def moments(first, second, grad, factor):
    clipped = grad * factor
    first_new = BETA_ONE * first + (1.0 - BETA_ONE) * clipped
    second_new = BETA_TWO * second + (1.0 - BETA_TWO) * clipped * clipped
    return (first_new, second_new)


def adam_update(weight, first, second, grad, factor):
    first_new, second_new = moments(first, second, grad, factor)
    first_hat = first_new / (1.0 - BETA_ONE**STEP)
    second_hat = second_new / (1.0 - BETA_TWO**STEP)
    weight_new = weight - LEARN_RATE * (
        first_hat / (jnp.sqrt(second_hat) + ADAM_EPS) + DECAY * weight
    )
    return (first_new, second_new, weight_new)


def body(
    token_ids,
    token_mask,
    resp_lengths,
    cand_counts,
    cand_rank,
    rewards,
    embed_table,
    embed_first,
    embed_second,
    head_table,
    head_first,
    head_second,
    qkv_weight,
    qkv_first,
    qkv_second,
    proj_weight,
    proj_first,
    proj_second,
    up_weight,
    up_first,
    up_second,
    down_weight,
    down_first,
    down_second,
    vector_params,
    vector_first,
    vector_second,
):
    slots = token_ids.shape[1]
    rows_own = slots * RESP
    core = lax.axis_index("cand")
    here = [lax.axis_index(axis) for axis in AXES]
    vocab_local = head_table.shape[0]
    pieces = split_params(vector_params)

    packed = jnp.concatenate(
        [
            qkv_weight.astype(jnp.bfloat16),
            up_weight.astype(jnp.bfloat16),
            proj_weight.astype(jnp.bfloat16),
            down_weight.astype(jnp.bfloat16).reshape(4, 8, D).transpose(1, 0, 2).reshape(8, 4 * D),
        ],
        axis=1,
    )
    gathered = lax.all_gather(packed, ("cand", "x", "y", "z"), axis=0, tiled=True)
    mats = (
        gathered[:, :D],
        gathered[:, D : 3 * D],
        gathered[:, 7 * D : 8 * D],
        gathered[:, 3 * D : 7 * D],
        gathered[:, 8 * D :].reshape(128, 8, 4, D).transpose(0, 2, 1, 3).reshape(FF, D),
    )

    turned = jnp.concatenate(
        [token_ids[0, :, SEQ - RESP - 1 :], token_ids[0, :, : SEQ - RESP - 1]], axis=1
    )
    near_ids = near_gather(near_gather(near_gather(turned, "z"), "y"), "x")
    group_targets = near_ids[:, :, 0, :, 1 : RESP + 1].reshape(-1)
    all_ids = near_ids
    for dim in range(3):
        twice = jnp.concatenate([all_ids, all_ids], axis=dim)
        all_ids = lax.dynamic_slice_in_dim(twice, (RING - here[dim]) % RING, RING, axis=dim)
    flat_ids = all_ids.reshape(64, slots, 2, RESP).transpose(0, 2, 1, 3).reshape(-1)
    looked = jnp.take(embed_table.astype(jnp.bfloat16), flat_ids, axis=0)
    inputs = lax.all_to_all(looked, AXES, split_axis=0, concat_axis=1, tiled=True).astype(
        jnp.float32
    )

    head_low = jnp.pad(head_table.astype(jnp.bfloat16), ((0, VOCAB_PAD - vocab_local), (0, 0)))
    head_half = lax.dynamic_slice_in_dim(head_low, core * (VOCAB_PAD // 2), VOCAB_PAD // 2)
    mine = jnp.stack(ring_gather(head_half, "z")[1:])
    theirs = swap(mine)
    ordered = jnp.where(
        core == 0, jnp.stack([mine, theirs], axis=1), jnp.stack([theirs, mine], axis=1)
    )
    head_group = jnp.concatenate([head_low, ordered.reshape(-1, D)], axis=0)

    live = (
        (jnp.arange(RESP)[None, None, :] < resp_lengths[:, :, None]) & (token_mask == 1)
    ).astype(jnp.float32)
    valid = (cand_rank < cand_counts[:, None]).astype(jnp.float32)
    top_mask = (cand_rank == 0).astype(jnp.float32)
    stats = total_all(
        jnp.stack(
            [
                jnp.sum(valid),
                jnp.sum(rewards * valid),
                jnp.sum(rewards * rewards * valid),
                jnp.sum(live * top_mask[..., None]),
            ]
        )
    )
    mean = stats[1] / stats[0]
    variance = stats[2] / stats[0] - mean * mean

    def pair(value):
        other = swap(value)
        return jnp.where(
            core == 0, jnp.concatenate([value, other]), jnp.concatenate([other, value])
        )

    all_rank = pair(cand_rank.reshape(-1))
    weight = jax.nn.softplus((pair(rewards.reshape(-1)) - mean) * lax.rsqrt(variance + NORM_EPS))

    hidden, saved = layer_forward(inputs, mats, pieces)
    rows_low = layer_norm(hidden, pieces[4], pieces[5]).astype(jnp.bfloat16)

    half_one, half_two = halves(rows_low)
    half_one = jnp.stack(ring_gather(jnp.stack(ring_gather(half_one, "y")), "x"))
    half_two = jnp.stack(ring_gather(jnp.stack(ring_gather(half_two, "x")), "y"))
    group_rows = jnp.concatenate([half_one, half_two.swapaxes(0, 1)], axis=-1).reshape(-1, D)

    shard = group_targets // vocab_local
    place = (shard % RING - here[2]) % RING
    local = (shard // RING) == here[0] * RING + here[1]
    targets = jnp.where(local, place * VOCAB_PAD + group_targets % vocab_local, -1)
    column = jnp.arange(RING * VOCAB_PAD)[None, :]
    logits = jnp.where(column % VOCAB_PAD < vocab_local, matmul_nt(group_rows, head_group), -1e30)
    hits = column == targets[:, None]
    local_max = jnp.max(logits, -1)
    local_sum = jnp.sum(jnp.exp(logits - local_max[:, None]), -1)
    local_target = jnp.sum(jnp.where(hits, logits, 0.0), -1)

    held = jnp.stack([local_max, local_sum, local_target]).reshape(3, RING, RING, rows_own)
    for axis in ("x", "y"):
        got = jnp.stack(near_scatter([held[:, k] for k in range(RING)], axis))
        biggest = jnp.max(got[:, 0], 0)
        held = jnp.stack(
            [
                biggest,
                jnp.sum(got[:, 1] * jnp.exp(got[:, 0] - biggest), 0),
                jnp.sum(got[:, 2], 0),
            ]
        )
    row_lse = held[0] + jnp.log(held[1])
    own_logp = (held[2] - row_lse).reshape(1, slots, RESP)
    own_count = jnp.sum(live, -1)
    own_scores = jnp.sum(own_logp * live, -1) / jnp.maximum(own_count, 1.0)
    all_scores = pair(own_scores.reshape(-1))
    pro_value, pro_grad = jax.value_and_grad(pro_single)(
        all_scores, weight, all_rank, cand_counts[0]
    )
    my_grad = lax.dynamic_slice_in_dim(pro_grad, core * slots, slots).reshape(1, slots)
    sft_scale = 64 / jnp.maximum(stats[3], 1.0)
    row_grad = (
        my_grad[..., None] / jnp.maximum(own_count, 1.0)[..., None]
        - sft_scale * top_mask[..., None]
    ) * live
    back = jnp.stack([row_grad.reshape(-1), row_lse])
    back = near_gather(near_gather(back, "y"), "x")
    group_grad = back[:, :, 0].reshape(-1)
    group_lse = back[:, :, 1].reshape(-1)

    vocab_probs = jnp.exp(logits - group_lse[:, None])
    logit_grad = (group_grad[:, None] * (hits.astype(jnp.float32) - vocab_probs)).astype(
        jnp.bfloat16
    )
    rows_part = matmul(logit_grad, head_group).astype(jnp.bfloat16)
    rows_part = rows_part.reshape(RING, RING, rows_own, D)
    part_one, part_two = halves(rows_part)
    part_one = ring_scatter([part_one[k] for k in range(RING)], "x").astype(jnp.bfloat16)
    part_one = ring_scatter([part_one[k] for k in range(RING)], "y")
    part_two = ring_scatter([part_two[:, k] for k in range(RING)], "y").astype(jnp.bfloat16)
    part_two = ring_scatter([part_two[k] for k in range(RING)], "x")
    rows_grad = jnp.concatenate([part_one, part_two], axis=-1)

    grad_hidden, gain_fin_grad, bias_fin_grad = norm_back(hidden, pieces[4], pieces[5], rows_grad)
    input_grad, mat_grads, vector_head, vector_tail = layer_backward(
        inputs, saved, mats, pieces, grad_hidden
    )

    head_part = matmul_tn(logit_grad, group_rows).astype(jnp.bfloat16)
    head_part = head_part.reshape(RING, 2, VOCAB_PAD // 2, D)
    sent = swap(lax.dynamic_index_in_dim(head_part, 1 - core, 1, keepdims=False))
    kept = lax.dynamic_index_in_dim(head_part, core, 1, keepdims=False)
    head_part = add_low(kept, sent)
    head_own = ring_scatter([head_part[k] for k in range(RING)], "z")
    head_other = swap(head_own)
    head_grad = jnp.where(
        core == 0,
        jnp.concatenate([head_own, head_other]),
        jnp.concatenate([head_other, head_own]),
    )[:vocab_local]

    embed_rows = lax.all_to_all(input_grad, AXES, split_axis=1, concat_axis=0, tiled=True)
    embed_grad = jax.ops.segment_sum(embed_rows, flat_ids, num_segments=embed_table.shape[0])
    embed_grad = embed_grad + swap(embed_grad)

    vector_grad = jnp.concatenate(vector_head + [gain_fin_grad, bias_fin_grad] + vector_tail)
    shards = (
        owner_sum(mat_grads[0], ("z", "x", "y")),
        owner_sum(mat_grads[1], ("z", "x", "y")),
        owner_sum(mat_grads[2], ("y", "z", "x")),
        owner_sum(mat_grads[3], ("x", "y", "z")),
        owner_sum_small(vector_grad),
    )
    local_squares = sum((jnp.sum(piece * piece) for piece in shards))
    local_squares = (
        local_squares + (jnp.sum(embed_grad * embed_grad) + jnp.sum(head_grad * head_grad)) / 2
    )
    sft_local = -jnp.sum(own_logp * live * top_mask[..., None])
    sums = total_all(jnp.stack([local_squares, pro_value / 2, sft_local]))
    grad_norm = jnp.sqrt(sums[0])
    factor = jnp.minimum(1.0, CLIP_NORM / (grad_norm + 1e-06))
    embed_new = adam_update(embed_table, embed_first, embed_second, embed_grad, factor)
    head_new = adam_update(head_table, head_first, head_second, head_grad, factor)
    qkv_new = adam_update(qkv_weight, qkv_first, qkv_second, shards[0], factor)
    proj_new = adam_update(proj_weight, proj_first, proj_second, shards[1], factor)
    up_new = adam_update(up_weight, up_first, up_second, shards[2], factor)
    down_new = adam_update(down_weight, down_first, down_second, shards[3], factor)
    vector_first_new, vector_second_new = moments(vector_first, vector_second, shards[4], factor)
    loss_parts = jnp.stack([sums[1], sums[2], stats[3]])
    return (
        loss_parts,
        grad_norm,
        my_grad,
        embed_new[0],
        embed_new[1],
        embed_new[2],
        head_new[0],
        head_new[1],
        head_new[2],
        qkv_new[0],
        qkv_new[1],
        qkv_new[2],
        proj_new[0],
        proj_new[1],
        proj_new[2],
        up_new[0],
        up_new[1],
        up_new[2],
        down_new[0],
        down_new[1],
        down_new[2],
        vector_first_new,
        vector_second_new,
    )


def solution(mesh):
    fine = Mesh(mesh.devices.reshape(2, RING, RING, RING), ("cand", *AXES))
    in_specs = (
        P(AXES, "cand", None),
        P(AXES, "cand", None),
        P(AXES, "cand"),
        P(AXES),
        P(AXES, "cand"),
        P(AXES, "cand"),
        P(None, AXES),
        P(None, AXES),
        P(None, AXES),
        P(AXES, None),
        P(AXES, None),
        P(AXES, None),
        P(("cand", *AXES), None),
        P(("cand", *AXES), None),
        P(("cand", *AXES), None),
        P(("cand", *AXES), None),
        P(("cand", *AXES), None),
        P(("cand", *AXES), None),
        P(("cand", *AXES), None),
        P(("cand", *AXES), None),
        P(("cand", *AXES), None),
        P(("cand", *AXES), None),
        P(("cand", *AXES), None),
        P(("cand", *AXES), None),
        P(),
        P(("cand", *AXES)),
        P(("cand", *AXES)),
    )
    out_specs = (
        P(),
        P(),
        P(AXES, "cand"),
        P(None, AXES),
        P(None, AXES),
        P(None, AXES),
        P(AXES, None),
        P(AXES, None),
        P(AXES, None),
        P(("cand", *AXES), None),
        P(("cand", *AXES), None),
        P(("cand", *AXES), None),
        P(("cand", *AXES), None),
        P(("cand", *AXES), None),
        P(("cand", *AXES), None),
        P(("cand", *AXES), None),
        P(("cand", *AXES), None),
        P(("cand", *AXES), None),
        P(("cand", *AXES), None),
        P(("cand", *AXES), None),
        P(("cand", *AXES), None),
        P(("cand", *AXES)),
        P(("cand", *AXES)),
    )
    return jax.shard_map(body, mesh=fine, in_specs=in_specs, out_specs=out_specs, check_vma=False)
```

time: 3890 us -> 1000 us (0.26)
  waiting for transfers between devices: 2620 us -> 193 us
  blocking collectives: 729 us -> 0 us
  starting transfers between devices: 12.9 us -> 261 us
  other arithmetic: 154 us -> 214 us
    reduce_scatter x5 -> x0, waiting for transfers between devices: 2460 us -> none  [the longest x1 680 us: body(): lax.psum_scatter(grads[2], ('cand', 'dp'), scatter_dimension=0, tiled=True)]
    unnamed x4 -> x0, blocking collectives: 514 us -> none
    ppermute x0 -> x184, starting transfers between devices: none -> 249 us  [the longest x170 181 us: shift(): lax.ppermute(value, axis, [(i, (i + step) % RING) for i in range(RING)])]
    ppermute x0 -> x184, waiting for transfers between devices: none -> 187 us  [the longest x170 185 us: shift(): lax.ppermute(value, axis, [(i, (i + step) % RING) for i in range(RING)])]
    all_gather x1 -> x0, blocking collectives: 152 us -> none  [body(): group_ids = lax.all_gather(token_ids, 'dp', axis=0, tiled=True)]
    all_gather x8 -> x1, waiting for transfers between devices: 151 us -> 0.01 us  [body(): lax.all_gather(packed, ('cand', 'x', 'y', 'z'), axis=0, tiled=True)]
    dynamic_slice x134 -> x3, local copies, waits for them, and re-layouts: 68.9 us -> 1.36 us  [the longest x1 1.3 us: body(): lax.dynamic_slice_in_dim(head_low, core * (VOCAB_PAD // 2), VOCAB_PAD // 2)]
    psum x1 -> x0, blocking collectives: 63 us -> none  [body(): lax.psum((local_squares, pro_value / pair_count, sft_local), ('cand', 'dp'))]
  transfers between devices with their start and end apart: 16 -> 187, of which waited for: 9 -> 74; matrix products, arithmetic and copies ran while one was open for 5% -> 38% of each run, Pallas kernels for 0% -> 0%
where the time goes in v1:
time: 1000 us; the launch traced here: 986 us
  starting transfers between devices  261 us (26%)
  other arithmetic  214 us (21%)
  waiting for transfers between devices  193 us (19%)
  local copies, waits for them, and re-layouts  173 us (17%)
  matrix products  114 us (11%)
  between operations  31 us (3%)
    ppermute x170, waiting for transfers between devices, shift(): lax.ppermute(value, axis, [(i, (i + step) % RING) for i in range(RING)])  185 us
    ppermute x170, starting transfers between devices, shift(): lax.ppermute(value, axis, [(i, (i + step) % RING) for i in range(RING)])  181 us
    scatter-add x1, other arithmetic, body(): jax.ops.segment_sum(embed_rows, flat_ids, num_segments=embed_table.shape[0])  76.1 us
    ppermute x14, starting transfers between devices, swap(): return lax.ppermute(value, 'cand', [(0, 1), (1, 0)])  67.6 us
    gather x2, local copies, waits for them, and re-layouts, body(): looked = jnp.take(embed_table.astype(jnp.bfloat16), flat_ids, axis=0)  51.9 us
    dot_general x6, matrix products, matmul_nt(): lax.dot_general(left, right, (((1,), (1,)), ((), ())), preferred_element_...  40.6 us
    dot_general x6, matrix products, matmul(): return jnp.dot(left, right, preferred_element_type=jnp.float32)  32.5 us
    dot_general x6, matrix products, matmul_tn(): lax.dot_general(left, right, (((0,), (0,)), ((), ())), preferred_element_...  29.5 us
  transfers between devices with their start and end apart: 187, of which 74 were waited for; matrix products, arithmetic and copies ran while one was open for 38% of the time, Pallas kernels for 0%

profile of v1, /device:TPU:1, one launch (start us, length us, event | category | flops | bytes accessed | tf_op | source)
XLA Modules:
  0.0 986.1 jit_solution(5073067801636658555)
XLA Ops:
  35.2 8.6 copy.316
  55.1 48.4 %gather_fusion = bf16[12288,16]{1,0:T(8,128)(2,1)} fusion(bf16[50304,16]{1,0:T(8,128)(2,1)} %copy.316, s32[12288]{0:T(1024)S(1)} %broadcast_clamp_fusion), kind=kCustom, calls=%fused_computation | custom fusion | bytes 835584 | tf_op jit(solution)/shard_map/jit(_take)/gather | solution.py:385
  188.6 7.8 slice.876
  196.4 8.8 multiply_convert_fusion.1
  263.3 18.1 %fusion.199 = (f32[1536]{0:T(1024)S(1)}, f32[1536,3584]{1,0:T(8,128)}) fusion(bf16[1536,1024]{1,0:T(8,128)(2,1)} %bitcast.557, bf16[2688,1024]{1,0:T(8,128)(2,1)S(1)} %bitcast.543, bf16[896,1024]{1,0:T(8,128)(2,1)} %pad.11, pred[3584]{0:T(1024)(128)(4,1)S(1)} %copy-done.103), kind=kOutput, calls=%fused_computation.581 | convolution fusion | flops 11299977216 | bytes 32515584 | tf_op jit(solution)/shard_map/dot_general | solution.py:139
  281.5 11.6 %select_reduce_fusion = (f32[1536]{0:T(1024)S(1)}, f32[1536]{0:T(1024)S(1)}) fusion(f32[1536,3584]{1,0:T(8,128)} %get-tuple-element.369, s32[1536]{0:T(1024)S(1)} %fusion.101, f32[1536]{0:T(1024)S(1)} %get-tuple-element.368), kind=kLoop, calls=%fused_computation.4 | loop fusion | flops 27522048 | bytes 22044672 | tf_op jit(solution)/shard_map/reduce_sum | solution.py:443
  359.2 12.2 %multiply_convert_fusion = bf16[1536,3584]{1,0:T(8,128)(2,1)S(1)} fusion(f32[1536,3584]{1,0:T(8,128)} %get-tuple-element.369, f32[1536]{0:T(1024)S(1)} %sub.244, f32[1536]{0:T(1024)S(1)} %mul.1034, s32[1536]{0:T(1024)S(1)} %fusion.101), kind=kLoop, calls=%fused_computation.3 | loop fusion | flops 33030144 | bytes 33048576 | tf_op jit(solution)/shard_map/convert_element_type | solution.py:476
  371.5 13.0 %fusion.15 = bf16[1536,1024]{1,0:T(8,128)(2,1)} fusion(bf16[1536,3584]{1,0:T(8,128)(2,1)S(1)} %multiply_convert_fusion, bf16[2688,1024]{1,0:T(8,128)(2,1)S(1)} %bitcast.546, bf16[896,1024]{1,0:T(8,128)(2,1)S(1)} %copy-done.37), kind=kOutput, calls=%fused_computation.34 | convolution fusion | flops 11290542080 | bytes 21495808 | tf_op jit(solution)/shard_map/dot_general | solution.py:129
  384.4 13.4 %convolution_convert_fusion = bf16[3584,1024]{1,0:T(8,128)(2,1)S(1)} fusion(bf16[1536,3584]{1,0:T(8,128)(2,1)S(1)} %multiply_convert_fusion, bf16[1536,1024]{1,0:T(8,128)(2,1)} %bitcast.558), kind=kOutput, calls=%fused_computation.14 | convolution fusion | flops 11277959168 | bytes 21495808 | tf_op jit(solution)/shard_map/dot_general | solution.py:133
  407.0 7.6 collective-permute-done.71
  503.6 15.4 %collective-permute-start.155 = (f32[4,4,4,120]{3,2,1,0:T(4,128)S(1)}, f32[4,4,4,120]{3,2,1,0:T(4,128)S(1)}, u32[]{:S(2)}, u32[]{:S(2)}) collective-permute-start(f32[4,4,4,120]{3,2,1,0:T(4,128)S(1)} %dynamic-slice_bitcast_fusion.38), channel_id=1, source_target_pairs={{0,64},{64,0},{1,65},{65,1},{2,66},{66,2},{3,67},{67,3},{4,68},{68... | collective-permute-start | bytes 92168 | tf_op jit(solution)/shard_map/ppermute | solution.py:36
  520.5 7.9 all-to-all-start.1
  609.1 76.1 %scatter_custom_fusion = f32[50304,16]{1,0:T(8,128)} fusion(s32[12288]{0:T(1024)} %reshape.968, f32[12288,16]{1,0:T(8,128)} %bitcast.542, f32[]{:T(128)} %constant.628.clone.1), kind=kCustom, calls=%fused_computation.8 | custom fusion | flops 196608 | bytes 3219968 | tf_op jit(solution)/shard_map/scatter-add | solution.py:507
  685.1 14.9 %copy.361 = f32[50304,16]{0,1:T(8,128)} copy(f32[50304,16]{1,0:T(8,128)} %scatter_custom_fusion) | data formatting | bytes 6438912 | tf_op jit(solution)/shard_map/scatter-add | solution.py:507
  700.0 10.0 %collective-permute-start.117 = (bf16[512,4096]{1,0:T(8,128)(2,1)}, bf16[512,4096]{1,0:T(8,128)(2,1)}, u32[]{:S(2)}, u32[]{:S(2)}) collective-permute-start(bf16[512,4096]{1,0:T(8,128)(2,1)} %dynamic-slice_bitcast_fusion.1), channel_id=1, source_target_pairs={{0,64},{64,0},{1,65},{65,1},{2,66},{66,2},{3,67},{67,3},{4,68},{68... | collective-permute-start | bytes 12582920 | tf_op jit(solution)/shard_map/ppermute | solution.py:36
  724.1 12.8 %collective-permute-done.84 = bf16[4,4,8,1536]{3,2,1,0:T(8,128)(2,1)S(1)} collective-permute-done((bf16[4,4,8,1536]{3,2,1,0:T(8,128)(2,1)S(1)}, bf16[4,4,8,1536]{3,2,1,0:T(8,128)(2,1)S(1)}, u32[]{:S(2)}, u32[]{:S(2)}) %collective-permute-start.84) | collective-permute-done | bytes 393248 | tf_op jit(solution)/shard_map/ppermute | solution.py:32
  748.2 9.4 collective-permute-done.171
  776.8 8.7 collective-permute-done.170
  787.9 7.4 collective-permute-done.172
  819.1 13.3 %collective-permute-done.122 = bf16[4,4,8,2048]{3,2,1,0:T(8,128)(2,1)} collective-permute-done((bf16[4,4,8,2048]{3,2,1,0:T(8,128)(2,1)}, bf16[4,4,8,2048]{3,2,1,0:T(8,128)(2,1)}, u32[]{:S(2)}, u32[]{:S(2)}) %collective-permute-start.122) | collective-permute-done | bytes 524320 | tf_op jit(solution)/shard_map/ppermute | solution.py:32
  853.2 7.4 collective-permute-done.139
  863.3 11.2 %collective-permute-done.142 = bf16[4,4,32,512]{3,2,1,0:T(8,128)(2,1)S(1)} collective-permute-done((bf16[4,4,32,512]{3,2,1,0:T(8,128)(2,1)S(1)}, bf16[4,4,32,512]{3,2,1,0:T(8,128)(2,1)S(1)}, u32[]{:S(2)}, u32[]{:S(2)}) %collective-permute-start.142) | collective-permute-done | bytes 524320 | tf_op jit(solution)/shard_map/ppermute | solution.py:32
  931.9 7.8 collective-permute-start.174
  959.7 8.8 multiply_subtract_fusion.1
  (1012 shorter events, 594.7 us)
Async XLA Ops:
  7.2 137.7 %all-gather.2.cloned.1.call-start = ((), (), s32[]{:S(2)}) async-start(), calls=%async_computation.2 | async-start | bytes 25362432 | tf_op jit(solution)/shard_map/all_gather | solution.py:366
  22.9 102.0 %collective-permute-start.38 = (bf16[448,1024]{1,0:T(8,128)(2,1)}, bf16[448,1024]{1,0:T(8,128)(2,1)}, u32[]{:S(2)}, u32[]{:S(2)}) collective-permute-start(bf16[448,1024]{1,0:T(8,128)(2,1)} %constant_dynamic-slice_fusion.16), channel_id=1, source_target_pairs={{0,1},{1,2},{2,3},{3,0},{4,5},{5,6},{6,7},{7,4},{8,9},{9,10},{10,1... | collective-permute-start | bytes 2752520 | tf_op jit(solution)/shard_map/ppermute | solution.py:32
  23.7 102.8 %collective-permute-start.37 = (bf16[448,1024]{1,0:T(8,128)(2,1)}, bf16[448,1024]{1,0:T(8,128)(2,1)}, u32[]{:S(2)}, u32[]{:S(2)}) collective-permute-start(bf16[448,1024]{1,0:T(8,128)(2,1)} %constant_dynamic-slice_fusion.16), channel_id=1, source_target_pairs={{0,3},{1,0},{2,1},{3,2},{4,7},{5,4},{6,5},{7,6},{8,11},{9,8},{10,9... | collective-permute-start | bytes 2752520 | tf_op jit(solution)/shard_map/ppermute | solution.py:32
  139.1 101.7 %collective-permute-start.41 = (bf16[3,448,1024]{2,1,0:T(8,128)(2,1)}, bf16[3,448,1024]{2,1,0:T(8,128)(2,1)}, u32[]{:S(2)}, u32[]{:S(2)}) collective-permute-start(bf16[3,448,1024]{2,1,0:T(8,128)(2,1)} %get-tuple-element.208), channel_id=1, source_target_pairs={{0,64},{64,0},{1,65},{65,1},{2,66},{66,2},{3,67},{67,3},{4,68},{68... | collective-permute-start | bytes 8257544 | tf_op jit(solution)/shard_map/ppermute | solution.py:36
  231.3 108.8 %collective-permute-start.9 = (f32[3]{0:T(128)}, f32[3]{0:T(128)}, u32[]{:S(2)}, u32[]{:S(2)}) collective-permute-start(f32[3]{0:T(128)} %bitcast.623), channel_id=1, source_target_pairs={{0,64},{64,0},{1,65},{65,1},{2,66},{66,2},{3,67},{67,3},{4,68},{68... | collective-permute-start | bytes 44 | tf_op jit(solution)/shard_map/ppermute | solution.py:36
  246.5 65.6 %collective-permute-start.20 = (s32[3]{0:T(128)S(1)}, s32[3]{0:T(128)}, u32[]{:S(2)}, u32[]{:S(2)}) collective-permute-start(s32[3]{0:T(128)S(1)} %bitcast.603), channel_id=1, source_target_pairs={{0,64},{64,0},{1,65},{65,1},{2,66},{66,2},{3,67},{67,3},{4,68},{68... | collective-permute-start | bytes 44 | tf_op jit(solution)/shard_map/ppermute | solution.py:36
  503.6 53.4 %collective-permute-start.155 = (f32[4,4,4,120]{3,2,1,0:T(4,128)S(1)}, f32[4,4,4,120]{3,2,1,0:T(4,128)S(1)}, u32[]{:S(2)}, u32[]{:S(2)}) collective-permute-start(f32[4,4,4,120]{3,2,1,0:T(4,128)S(1)} %dynamic-slice_bitcast_fusion.38), channel_id=1, source_target_pairs={{0,64},{64,0},{1,65},{65,1},{2,66},{66,2},{3,67},{67,3},{4,68},{68... | collective-permute-start | bytes 92168 | tf_op jit(solution)/shard_map/ppermute | solution.py:36
  520.5 83.5 %all-to-all-start.1 = ((f32[192,64,16]{0,2,1:T(8,128)}), f32[192,64,16]{0,2,1:T(8,128)}, u32[]{:S(2)}, u32[]{:S(2)}) async-start(f32[192,64,16]{0,2,1:T(8,128)} %bitcast.547), calls=%async_computation.1 | async-start | bytes 2097152 | tf_op jit(solution)/shard_map/all_to_all | solution.py:506
  544.1 166.6 %collective-permute-start.79 = (bf16[512,3072]{1,0:T(8,128)(2,1)}, bf16[512,3072]{1,0:T(8,128)(2,1)}, u32[]{:S(2)}, u32[]{:S(2)}) collective-permute-start(bf16[512,3072]{1,0:T(8,128)(2,1)} %dynamic-slice_bitcast_fusion.3), channel_id=1, source_target_pairs={{0,64},{64,0},{1,65},{65,1},{2,66},{66,2},{3,67},{67,3},{4,68},{68... | collective-permute-start | bytes 9437192 | tf_op jit(solution)/shard_map/ppermute | solution.py:36
  571.6 146.4 %collective-permute-start.166 = (bf16[4,448,1024]{2,1,0:T(8,128)(2,1)}, bf16[4,448,1024]{2,1,0:T(8,128)(2,1)}, u32[]{:S(2)}, u32[]{:S(2)}) collective-permute-start(bf16[4,448,1024]{2,1,0:T(8,128)(2,1)} %dynamic-slice_bitcast_fusion.2), channel_id=1, source_target_pairs={{0,64},{64,0},{1,65},{65,1},{2,66},{66,2},{3,67},{67,3},{4,68},{68... | collective-permute-start | bytes 11010056 | tf_op jit(solution)/shard_map/ppermute | solution.py:36
  599.2 100.8 %collective-permute-start.113 = (bf16[8,512]{1,0:T(8,128)(2,1)S(1)}, bf16[8,512]{1,0:T(8,128)(2,1)S(1)}, u32[]{:S(2)}, u32[]{:S(2)}) collective-permute-start(bf16[8,512]{1,0:T(8,128)(2,1)S(1)} %slice.984), channel_id=1, source_target_pairs={{0,12},{4,0},{8,4},{12,8},{1,13},{5,1},{9,5},{13,9},{2,14},{6,2},{... | collective-permute-start | bytes 24584 | tf_op jit(solution)/shard_map/ppermute | solution.py:32
  601.9 108.1 %collective-permute-start.112 = (bf16[8,512]{1,0:T(8,128)(2,1)S(1)}, bf16[8,512]{1,0:T(8,128)(2,1)S(1)}, u32[]{:S(2)}, u32[]{:S(2)}) collective-permute-start(bf16[8,512]{1,0:T(8,128)(2,1)S(1)} %add_convert_fusion.40), channel_id=1, source_target_pairs={{0,12},{4,0},{8,4},{12,8},{1,13},{5,1},{9,5},{13,9},{2,14},{6,2},{... | collective-permute-start | bytes 24584 | tf_op jit(solution)/shard_map/ppermute | solution.py:32
  602.9 107.2 %collective-permute-start.116 = (bf16[8,512]{1,0:T(8,128)(2,1)S(1)}, bf16[8,512]{1,0:T(8,128)(2,1)S(1)}, u32[]{:S(2)}, u32[]{:S(2)}) collective-permute-start(bf16[8,512]{1,0:T(8,128)(2,1)S(1)} %add_convert_fusion.39), channel_id=1, source_target_pairs={{0,4},{4,8},{8,12},{12,0},{1,5},{5,9},{9,13},{13,1},{2,6},{6,10},{... | collective-permute-start | bytes 24584 | tf_op jit(solution)/shard_map/ppermute | solution.py:32
  700.0 102.6 %collective-permute-start.117 = (bf16[512,4096]{1,0:T(8,128)(2,1)}, bf16[512,4096]{1,0:T(8,128)(2,1)}, u32[]{:S(2)}, u32[]{:S(2)}) collective-permute-start(bf16[512,4096]{1,0:T(8,128)(2,1)} %dynamic-slice_bitcast_fusion.1), channel_id=1, source_target_pairs={{0,64},{64,0},{1,65},{65,1},{2,66},{66,2},{3,67},{67,3},{4,68},{68... | collective-permute-start | bytes 12582920 | tf_op jit(solution)/shard_map/ppermute | solution.py:36
  715.2 25.1 %collective-permute-start.82 = (bf16[4,4,8,1536]{3,2,1,0:T(8,128)(2,1)S(1)}, bf16[4,4,8,1536]{3,2,1,0:T(8,128)(2,1)S(1)}, u32[]{:S(2)}, u32[]{:S(2)}) collective-permute-start(bf16[4,4,8,1536]{3,2,1,0:T(8,128)(2,1)S(1)} %slice.954), channel_id=1, source_target_pairs={{0,3},{1,0},{2,1},{3,2},{4,7},{5,4},{6,5},{7,6},{8,11},{9,8},{10,9... | collective-permute-start | bytes 1179656 | tf_op jit(solution)/shard_map/ppermute | solution.py:32
  740.3 34.0 %collective-permute-start.169 = (bf16[448,512]{1,0:T(8,128)(2,1)S(1)}, bf16[448,512]{1,0:T(8,128)(2,1)S(1)}, u32[]{:S(2)}, u32[]{:S(2)}) collective-permute-start(bf16[448,512]{1,0:T(8,128)(2,1)S(1)} %slice.1029), channel_id=1, source_target_pairs={{0,3},{1,0},{2,1},{3,2},{4,7},{5,4},{6,5},{7,6},{8,11},{9,8},{10,9... | collective-permute-start | bytes 1376264 | tf_op jit(solution)/shard_map/ppermute | solution.py:32
  770.0 44.2 %collective-permute-start.136 = (bf16[2048,1024]{1,0:T(8,128)(2,1)}, bf16[2048,1024]{1,0:T(8,128)(2,1)}, u32[]{:S(2)}, u32[]{:S(2)}) collective-permute-start(bf16[2048,1024]{1,0:T(8,128)(2,1)} %dynamic-slice_bitcast_fusion), channel_id=1, source_target_pairs={{0,64},{64,0},{1,65},{65,1},{2,66},{66,2},{3,67},{67,3},{4,68},{68... | collective-permute-start | bytes 12582920 | tf_op jit(solution)/shard_map/ppermute | solution.py:36
  808.8 38.1 %collective-permute-start.120 = (bf16[4,4,8,2048]{3,2,1,0:T(8,128)(2,1)}, bf16[4,4,8,2048]{3,2,1,0:T(8,128)(2,1)S(1)}, u32[]{:S(2)}, u32[]{:S(2)}) collective-permute-start(bf16[4,4,8,2048]{3,2,1,0:T(8,128)(2,1)} %slice.990), channel_id=1, source_target_pairs={{0,12},{4,0},{8,4},{12,8},{1,13},{5,1},{9,5},{13,9},{2,14},{6,2},{... | collective-permute-start | bytes 1572872 | tf_op jit(solution)/shard_map/ppermute | solution.py:32
  810.2 38.6 %collective-permute-start.121 = (bf16[4,4,8,2048]{3,2,1,0:T(8,128)(2,1)}, bf16[4,4,8,2048]{3,2,1,0:T(8,128)(2,1)}, u32[]{:S(2)}, u32[]{:S(2)}) collective-permute-start(bf16[4,4,8,2048]{3,2,1,0:T(8,128)(2,1)} %slice.991), channel_id=1, source_target_pairs={{0,4},{4,8},{8,12},{12,0},{1,5},{5,9},{9,13},{13,1},{2,6},{6,10},{... | collective-permute-start | bytes 1572872 | tf_op jit(solution)/shard_map/ppermute | solution.py:32
  841.0 66.5 %collective-permute-start.165 = (f32[50304,16]{0,1:T(8,128)S(1)}, f32[50304,16]{0,1:T(8,128)S(1)}, u32[]{:S(2)}, u32[]{:S(2)}) collective-permute-start(f32[50304,16]{0,1:T(8,128)S(1)} %copy-done.4), channel_id=1, source_target_pairs={{0,64},{64,0},{1,65},{65,1},{2,66},{66,2},{3,67},{67,3},{4,68},{68... | collective-permute-start | bytes 9658376 | tf_op jit(solution)/shard_map/ppermute | solution.py:36
  848.8 25.7 %collective-permute-start.142 = (bf16[4,4,32,512]{3,2,1,0:T(8,128)(2,1)S(1)}, bf16[4,4,32,512]{3,2,1,0:T(8,128)(2,1)S(1)}, u32[]{:S(2)}, u32[]{:S(2)}) collective-permute-start(bf16[4,4,32,512]{3,2,1,0:T(8,128)(2,1)S(1)} %add_convert_fusion.2), channel_id=1, source_target_pairs={{0,16},{16,32},{32,48},{48,0},{1,17},{17,33},{33,49},{49,1},{2,18}... | collective-permute-start | bytes 1572872 | tf_op jit(solution)/shard_map/ppermute | solution.py:32
  848.9 25.6 %collective-permute-start.138 = (bf16[4,4,32,512]{3,2,1,0:T(8,128)(2,1)S(1)}, bf16[4,4,32,512]{3,2,1,0:T(8,128)(2,1)S(1)}, u32[]{:S(2)}, u32[]{:S(2)}) collective-permute-start(bf16[4,4,32,512]{3,2,1,0:T(8,128)(2,1)S(1)} %add_convert_fusion.3), channel_id=1, source_target_pairs={{0,48},{16,0},{32,16},{48,32},{1,49},{17,1},{33,17},{49,33},{2,50}... | collective-permute-start | bytes 1572872 | tf_op jit(solution)/shard_map/ppermute | solution.py:32
  860.6 27.0 %collective-permute-start.126 = (bf16[4,8,2048]{2,1,0:T(8,128)(2,1)S(1)}, bf16[4,8,2048]{2,1,0:T(8,128)(2,1)S(1)}, u32[]{:S(2)}, u32[]{:S(2)}) collective-permute-start(bf16[4,8,2048]{2,1,0:T(8,128)(2,1)S(1)} %slice.996), channel_id=1, source_target_pairs={{0,3},{1,0},{2,1},{3,2},{4,7},{5,4},{6,5},{7,6},{8,11},{9,8},{10,9... | collective-permute-start | bytes 393224 | tf_op jit(solution)/shard_map/ppermute | solution.py:32
  892.6 34.5 %collective-permute-start.173 = (f32[448,1024]{1,0:T(8,128)S(1)}, f32[448,1024]{1,0:T(8,128)}, u32[]{:S(2)}, u32[]{:S(2)}) collective-permute-start(f32[448,1024]{1,0:T(8,128)S(1)} %copy-done.2), channel_id=1, source_target_pairs={{0,64},{64,0},{1,65},{65,1},{2,66},{66,2},{3,67},{67,3},{4,68},{68... | collective-permute-start | bytes 5505032 | tf_op jit(solution)/shard_map/ppermute | solution.py:36
  (293 other events, 3022.4 us)
Sparse Core Ops, SparseCore 0:
  11.7 97.7 all-gather.1

commit v2 on v1

v2 whole, which is shorter than its diff:
```python
import jax
import jax.numpy as jnp
from jax import lax
from jax.experimental import pallas as pl
from jax.experimental.pallas import tpu as pltpu
from jax.sharding import Mesh
from jax.sharding import PartitionSpec as P

D = 1024
HEADS = 16
HEAD_DIM = 64
ROT = 16
FF = 4096
SEQ = 64
STEP = 10
RESP = 32


NORM_EPS = 1e-05
CLIP_NORM = 1.0
LEARN_RATE = 0.05
BETA_ONE = 0.9
BETA_TWO = 0.999
ADAM_EPS = 1e-08
DECAY = 0.1


RING = 4
PAD_HALF = 448
AXES = ("x", "y", "z")


def swap(value):
    return lax.ppermute(value, "cand", [(0, 1), (1, 0)])


def exchange(pieces, axes):
    return lax.all_to_all(pieces, axes, split_axis=0, concat_axis=0, tiled=True)


def spread(value, axes):
    count = lax.axis_size(axes)
    return exchange(jnp.broadcast_to(value[None], (count, *value.shape)), axes)


def core_sum(left, right, low=jnp.bfloat16):
    core = lax.axis_index("cand")
    half = left.shape[1] // 2
    kept = lax.dynamic_slice_in_dim(left, core * half, half, axis=1)
    given = lax.dynamic_slice_in_dim(left, (1 - core) * half, half, axis=1)
    return (
        matmul_tn(kept, right) + swap(matmul_tn(given, right).astype(low)).astype(jnp.float32)
    ).astype(low)


WIDE = 256
LOOK_BLOCK = 1024
FOLD_BLOCK = 2048


def look_kernel(high_ref, low_ref, table_ref, out_ref, left):
    spans = table_ref.shape[1] // WIDE
    rest = table_ref.shape[1] - spans * WIDE

    @pl.when(pl.program_id(0) == 0)
    def _():
        def fill(i, carry):
            span = table_ref[:, pl.ds(pl.multiple_of(i * WIDE, WIDE), WIDE)]
            left[pl.ds(pl.multiple_of(i * 16, 16), 16), :] = span.astype(jnp.bfloat16)
            return carry

        lax.fori_loop(0, spans, fill, 0)
        if rest:
            last = table_ref[:, spans * WIDE :].astype(jnp.bfloat16)
            left[spans * 16 :, :] = jnp.concatenate(
                [last, jnp.zeros((16, WIDE - rest), jnp.bfloat16)], axis=1
            )

    block = out_ref.shape[1]
    one_hot = jnp.where(
        lax.broadcasted_iota(jnp.int32, (WIDE, block), 0) == low_ref[...], 1.0, 0.0
    ).astype(jnp.bfloat16)
    high = jnp.broadcast_to(high_ref[...], (16, block))
    total = jnp.zeros((16, block), jnp.float32)
    rows = left.shape[0] // 16
    CH = 16
    for begin in range(0, rows, CH):
        count = min(CH, rows - begin)
        part = jnp.dot(
            left[begin * 16 : (begin + count) * 16, :], one_hot, preferred_element_type=jnp.float32
        )
        for k in range(count):
            total = total + jnp.where(high == begin + k, part[k * 16 : (k + 1) * 16], 0.0)
    out_ref[...] = total.astype(out_ref.dtype)


def look_up(table, ids):
    count = ids.shape[0]
    spans = -(-table.shape[1] // WIDE)
    high = (ids // WIDE).reshape(1, count)
    low = (ids % WIDE).reshape(1, count)
    row = pl.BlockSpec((1, LOOK_BLOCK), lambda i: (0, i))
    return pl.pallas_call(
        look_kernel,
        grid=(count // LOOK_BLOCK,),
        in_specs=[row, row, pl.BlockSpec(table.shape, lambda i: (0, 0))],
        out_specs=pl.BlockSpec((16, LOOK_BLOCK), lambda i: (0, i)),
        out_shape=jax.ShapeDtypeStruct((16, count), jnp.float32),
        scratch_shapes=[pltpu.VMEM((spans * 16, WIDE), jnp.bfloat16)],
        compiler_params=pltpu.CompilerParams(vmem_limit_bytes=40 << 20),
        cost_estimate=pl.CostEstimate(flops=2 * spans * 16 * WIDE * count, bytes_accessed=table.size * 4, transcendentals=0),
        name="look_up",
    )(high, low, table)


def fold_kernel(high_ref, low_ref, grad_ref, out_ref, left, total):
    step = pl.program_id(0)
    block = grad_ref.shape[1]
    rows = left.shape[0] // 16
    grad = grad_ref[...]
    high = jnp.broadcast_to(high_ref[...], (16, block))

    def place(i, carry):
        for k in range(4):
            at = i * 4 + k
            left[pl.ds(pl.multiple_of(at * 16, 16), 16), :] = jnp.where(
                high == at, grad, 0.0
            ).astype(jnp.bfloat16)
        return carry

    lax.fori_loop(0, rows // 4, place, 0)
    for at in range(rows // 4 * 4, rows):
        left[at * 16 : at * 16 + 16, :] = jnp.where(high == at, grad, 0.0).astype(jnp.bfloat16)
    one_hot = jnp.where(
        lax.broadcasted_iota(jnp.int32, (WIDE, block), 0) == low_ref[...], 1.0, 0.0
    ).astype(jnp.bfloat16)
    part = lax.dot_general(
        left[...], one_hot, (((1,), (1,)), ((), ())), preferred_element_type=jnp.float32
    )

    @pl.when(step == 0)
    def _():
        total[...] = part

    @pl.when(step > 0)
    def _():
        total[...] += part

    @pl.when(step == pl.num_programs(0) - 1)
    def _():
        spans = out_ref.shape[1] // WIDE
        rest = out_ref.shape[1] - spans * WIDE

        def drain(i, carry):
            out_ref[:, pl.ds(pl.multiple_of(i * WIDE, WIDE), WIDE)] = total[
                pl.ds(pl.multiple_of(i * 16, 16), 16), :
            ]
            return carry

        lax.fori_loop(0, spans, drain, 0)
        if rest:
            out_ref[:, spans * WIDE :] = total[spans * 16 :, :rest]


def fold(grads, ids, size):
    count = ids.shape[0]
    spans = -(-size // WIDE)
    high = (ids // WIDE).reshape(1, count)
    low = (ids % WIDE).reshape(1, count)
    row = pl.BlockSpec((1, FOLD_BLOCK), lambda i: (0, i))
    return pl.pallas_call(
        fold_kernel,
        grid=(count // FOLD_BLOCK,),
        in_specs=[row, row, pl.BlockSpec((16, FOLD_BLOCK), lambda i: (0, i))],
        out_specs=pl.BlockSpec((16, size), lambda i: (0, 0)),
        out_shape=jax.ShapeDtypeStruct((16, size), jnp.float32),
        scratch_shapes=[
            pltpu.VMEM((spans * 16, FOLD_BLOCK), jnp.bfloat16),
            pltpu.VMEM((spans * 16, WIDE), jnp.float32),
        ],
        compiler_params=pltpu.CompilerParams(vmem_limit_bytes=40 << 20),
        cost_estimate=pl.CostEstimate(flops=2 * spans * 16 * WIDE * count, bytes_accessed=size * 64, transcendentals=0),
        name="fold",
    )(high, low, grads)


def matmul(left, right):
    return jnp.dot(left, right, preferred_element_type=jnp.float32)


def matmul_tn(left, right):
    return lax.dot_general(
        left, right, (((0,), (0,)), ((), ())), preferred_element_type=jnp.float32
    )


def matmul_nt(left, right):
    return lax.dot_general(
        left, right, (((1,), (1,)), ((), ())), preferred_element_type=jnp.float32
    )


def layer_norm(inputs, gain, bias):
    mean = jnp.mean(inputs, -1, keepdims=True)
    centred = inputs - mean
    variance = jnp.mean(centred * centred, -1, keepdims=True)
    return centred * lax.rsqrt(variance + NORM_EPS) * gain + bias


def norm_back(inputs, gain, bias, grad):
    outputs, pullback = jax.vjp(layer_norm, inputs, gain, bias)
    return pullback(grad)


def split_params(vector):
    spans = [D, D, D, D, D, D, 3 * D, D, FF, D]
    pieces = []
    begin = 0
    for span_len in spans:
        pieces.append(vector[begin : begin + span_len])
        begin = begin + span_len
    return pieces


def gelu_exact(values):
    return jax.nn.gelu(values, approximate=False)


def rotary(inputs, places, sign):
    half = ROT // 2
    freq = 10000.0 ** (-jnp.arange(half).astype(jnp.float32) * (2.0 / ROT))
    angle = places.astype(jnp.float32)[:, None] * freq[None, :]
    cosine = jnp.cos(angle)[:, None, :]
    sine = sign * jnp.sin(angle)[:, None, :]
    first = inputs[..., :half]
    second = inputs[..., half:ROT]
    return jnp.concatenate(
        [first * cosine - second * sine, second * cosine + first * sine, inputs[..., ROT:]], axis=-1
    )


def key_places():
    return (jnp.arange(SEQ) + (SEQ - RESP - 1)) % SEQ


def attention_probs(query, keys):
    scores = jnp.einsum(
        "cqhd,ckhd->chqk", query, keys, preferred_element_type=jnp.float32
    ) * HEAD_DIM ** (-0.5)
    places = key_places()
    causal = places[:RESP, None] >= places[None, :]
    return jax.nn.softmax(jnp.where(causal, scores, -1e30), axis=-1)


def joined(rows, slots):
    cut = rows.reshape(2, slots, RESP, *rows.shape[1:])
    return jnp.concatenate([cut[0], cut[1]], axis=1)


def parted(rows):
    cut = jnp.stack([rows[:, :RESP], rows[:, RESP:]])
    return cut.reshape(-1, *rows.shape[2:])


def layer_forward(inputs, mats, pieces):
    query_w, kv_w, proj_w, up_w, down_w = mats
    live = inputs.shape[0] // 2
    slots = live // RESP
    first = inputs[:live]
    attn_in = layer_norm(inputs, pieces[0], pieces[1]).astype(jnp.bfloat16)
    mlp_in = layer_norm(first, pieces[2], pieces[3]).astype(jnp.bfloat16)
    query = matmul(attn_in[:live], query_w) + pieces[6][:D]
    both = matmul(attn_in, kv_w) + pieces[6][D:]
    query = rotary(query.reshape(slots, RESP, HEADS, HEAD_DIM), key_places()[:RESP], 1.0)
    keys = joined(both[:, :D], slots).reshape(slots, SEQ, HEADS, HEAD_DIM)
    keys = rotary(keys, key_places(), 1.0)
    values = joined(both[:, D:], slots).reshape(slots, SEQ, HEADS, HEAD_DIM)
    query, keys, values = [part.astype(jnp.bfloat16) for part in (query, keys, values)]
    probs_low = attention_probs(query, keys).astype(jnp.bfloat16)
    mixed = jnp.einsum("chqk,ckhd->cqhd", probs_low, values, preferred_element_type=jnp.float32)
    mixed = mixed.astype(jnp.bfloat16).reshape(-1, D)
    up_val = matmul(mlp_in, up_w) + pieces[8]
    act = gelu_exact(up_val).astype(jnp.bfloat16)
    mlp = sum(matmul(act[:, k * D : (k + 1) * D], part) for k, part in enumerate(down_w))
    hidden = first + (matmul(mixed, proj_w) + pieces[7]) + (mlp + pieces[9])
    return (hidden, (attn_in, mlp_in, query, keys, values, mixed, up_val, act))


def layer_backward(inputs, saved, mats, pieces, grad_hidden, ahead):
    query_w, kv_w, proj_w, up_w, down_w = mats
    attn_in, mlp_in, query, keys, values, mixed, up_val, act = saved
    live = inputs.shape[0] // 2
    slots = live // RESP
    first = inputs[:live]
    grad_low = grad_hidden.astype(jnp.bfloat16)
    grad_sum = jnp.sum(grad_low.astype(jnp.float32), 0)
    down_grad = core_sum(act, grad_low)
    act_grad = jnp.concatenate([matmul_nt(grad_low, part) for part in down_w], axis=1)
    gelu_out, gelu_pull = jax.vjp(gelu_exact, up_val)
    up_grad_low = gelu_pull(act_grad)[0].astype(jnp.bfloat16)
    up_w_grad = core_sum(mlp_in, up_grad_low)
    mlp_in_grad = matmul_nt(up_grad_low, up_w)
    proj_grad = core_sum(mixed, grad_low)
    mixed_grad = (
        matmul_nt(grad_low, proj_w).astype(jnp.bfloat16).reshape(slots, RESP, HEADS, HEAD_DIM)
    )
    probs = attention_probs(query, keys)
    probs_low = probs.astype(jnp.bfloat16)
    probs_grad = jnp.einsum(
        "cqhd,ckhd->chqk", mixed_grad, values, preferred_element_type=jnp.float32
    )
    value_grad = jnp.einsum(
        "chqk,cqhd->ckhd", probs_low, mixed_grad, preferred_element_type=jnp.float32
    )
    score_grad = probs * (probs_grad - jnp.sum(probs * probs_grad, -1, keepdims=True))
    score_grad = score_grad.astype(jnp.bfloat16)
    scale = HEAD_DIM ** (-0.5)
    query_grad = (
        jnp.einsum("chqk,ckhd->cqhd", score_grad, keys, preferred_element_type=jnp.float32) * scale
    )
    key_grad = (
        jnp.einsum("chqk,cqhd->ckhd", score_grad, query, preferred_element_type=jnp.float32) * scale
    )
    query_grad = rotary(query_grad, key_places()[:RESP], -1.0).reshape(live, D)
    key_grad = rotary(key_grad, key_places(), -1.0).reshape(slots, SEQ, D)
    value_grad = value_grad.reshape(slots, SEQ, D)
    query_grad = query_grad.astype(jnp.bfloat16)
    both_grad = jnp.concatenate([parted(key_grad), parted(value_grad)], axis=1).astype(jnp.bfloat16)
    qkv_w_grad = (core_sum(attn_in[:live], query_grad), core_sum(attn_in, both_grad))
    query_grad, both_grad, ahead = lax.optimization_barrier((query_grad, both_grad, ahead))
    attn_in_grad = matmul_nt(both_grad, kv_w)
    attn_in_grad = attn_in_grad + jnp.pad(matmul_nt(query_grad, query_w), ((0, live), (0, 0)))
    input_one, gain_one_grad, bias_one_grad = norm_back(inputs, pieces[0], pieces[1], attn_in_grad)
    input_two, gain_two_grad, bias_two_grad = norm_back(first, pieces[2], pieces[3], mlp_in_grad)
    input_grad = input_one + jnp.pad(grad_hidden + input_two, ((0, live), (0, 0)))
    vector_head = [gain_one_grad, bias_one_grad, gain_two_grad, bias_two_grad]
    vector_tail = [
        jnp.sum(query_grad.astype(jnp.float32), 0),
        jnp.sum(both_grad.astype(jnp.float32), 0),
        grad_sum,
        jnp.sum(up_grad_low.astype(jnp.float32), 0),
        grad_sum,
    ]
    mat_grads = (qkv_w_grad, proj_grad, up_w_grad, down_grad)
    return (input_grad, mat_grads, vector_head, vector_tail, ahead)


def pro_single(scores, weight, ranks, count):
    valid = ranks < count
    head = ranks < count - 1
    peak = jnp.max(jnp.where(valid, scores, -1e30))
    expo = jnp.where(valid, jnp.exp(scores - peak), 0.0)
    later = ranks[None, :] >= ranks[:, None]
    suffix = jnp.sum(jnp.where(later, expo[None, :], 0.0), -1)
    return jnp.sum(
        jnp.where(head, -weight * (scores - peak - jnp.log(jnp.where(head, suffix, 1.0))), 0.0)
    )


def moments(first, second, grad, factor):
    clipped = grad * factor
    first_new = BETA_ONE * first + (1.0 - BETA_ONE) * clipped
    second_new = BETA_TWO * second + (1.0 - BETA_TWO) * clipped * clipped
    return (first_new, second_new)


def adam_update(weight, first, second, grad, factor):
    first_new, second_new = moments(first, second, grad, factor)
    first_hat = first_new / (1.0 - BETA_ONE**STEP)
    second_hat = second_new / (1.0 - BETA_TWO**STEP)
    weight_new = weight - LEARN_RATE * (
        first_hat / (jnp.sqrt(second_hat) + ADAM_EPS) + DECAY * weight
    )
    return (first_new, second_new, weight_new)


def body(
    token_ids,
    token_mask,
    resp_lengths,
    cand_counts,
    cand_rank,
    rewards,
    embed_table,
    embed_first,
    embed_second,
    head_table,
    head_first,
    head_second,
    qkv_weight,
    qkv_first,
    qkv_second,
    proj_weight,
    proj_first,
    proj_second,
    up_weight,
    up_first,
    up_second,
    down_weight,
    down_first,
    down_second,
    vector_params,
    vector_first,
    vector_second,
):
    slots = token_ids.shape[1]
    rows_own = slots * RESP
    core = lax.axis_index("cand")
    here = [lax.axis_index(axis) for axis in AXES]
    vocab_local = head_table.shape[0]
    pieces = split_params(vector_params)

    everyone = ("cand", *AXES)
    me = lax.axis_index(everyone)
    quarter = me // 32
    down_low = down_weight.reshape(RING, 8, D)
    moved = []
    for step in range(RING):
        group = lax.dynamic_index_in_dim(down_low, (step + quarter) % RING, 0, False)
        moved.append(
            lax.ppermute(
                group.astype(jnp.bfloat16),
                everyone,
                [(d, RING * (d % 32) + (step + d // 32) % RING) for d in range(128)],
            ).astype(jnp.float32)
        )
    moved = jnp.stack(moved)
    down_rows = [
        lax.dynamic_index_in_dim(moved, (me - k) % RING, 0, False) for k in range(RING)
    ]
    packed = jnp.concatenate([qkv_weight, up_weight, proj_weight, *down_rows], axis=1)
    gathered = lax.all_gather(packed.astype(jnp.bfloat16), everyone, axis=0, tiled=True)
    mats = (
        gathered[:, :D],
        gathered[:, D : 3 * D],
        gathered[:, 7 * D : 8 * D],
        gathered[:, 3 * D : 7 * D],
        [gathered[:, (8 + k) * D : (9 + k) * D] for k in range(RING)],
    )

    live = (
        (jnp.arange(RESP)[None, None, :] < resp_lengths[:, :, None]) & (token_mask == 1)
    ).astype(jnp.float32)
    valid = (cand_rank < cand_counts[:, None]).astype(jnp.float32)
    top_mask = (cand_rank == 0).astype(jnp.float32)
    stats = jnp.stack(
        [
            jnp.sum(valid),
            jnp.sum(rewards * valid),
            jnp.sum(rewards * rewards * valid),
            jnp.sum(live * top_mask[..., None]),
        ]
    )

    turned = jnp.concatenate(
        [token_ids[0, :, SEQ - RESP - 1 :], token_ids[0, :, : SEQ - RESP - 1]], axis=1
    )
    posted = spread(
        jnp.concatenate([turned.reshape(-1).astype(jnp.float32), stats, jnp.zeros(60)]), AXES
    )
    all_ids = posted[:, : slots * SEQ].astype(jnp.int32)
    stats = jnp.sum(posted[:, slots * SEQ : slots * SEQ + 4], 0)
    group_ids = lax.dynamic_index_in_dim(all_ids.reshape(16, RING, slots, SEQ), here[2], 1, False)
    group_targets = group_ids[:, :, 1 : RESP + 1].reshape(-1)
    flat_ids = all_ids.reshape(64, slots, 2, RESP).transpose(0, 2, 1, 3).reshape(-1)
    looked = look_up(embed_table.T, flat_ids).astype(jnp.bfloat16)
    looked = looked.reshape(16, 64, slots * SEQ).swapaxes(0, 1)
    inputs = exchange(looked, AXES).reshape(D, slots * SEQ).T.astype(jnp.float32)

    head_low = jnp.pad(head_table.astype(jnp.bfloat16), ((0, 2 * PAD_HALF - vocab_local), (0, 0)))
    head_half = lax.dynamic_slice_in_dim(head_low, core * PAD_HALF, PAD_HALF)
    head_half, inputs = lax.optimization_barrier((head_half, inputs))
    mine = spread(head_half, "z").reshape(-1, D)

    other = swap(
        jnp.concatenate([stats, rewards.reshape(-1), cand_rank.reshape(-1).astype(jnp.float32)])
    )
    stats = stats + other[:4]
    mean = stats[1] / stats[0]
    variance = stats[2] / stats[0] - mean * mean

    def both(value, second):
        return jnp.where(
            core == 0, jnp.concatenate([value, second]), jnp.concatenate([second, value])
        )

    all_rank = both(cand_rank.reshape(-1), other[4 + slots :].astype(jnp.int32))
    all_rewards = both(rewards.reshape(-1), other[4 : 4 + slots])
    weight = jax.nn.softplus((all_rewards - mean) * lax.rsqrt(variance + NORM_EPS))

    hidden, saved = layer_forward(inputs, mats, pieces)
    rows_low = layer_norm(hidden, pieces[4], pieces[5]).astype(jnp.bfloat16)

    rows_low, mine = lax.optimization_barrier((rows_low, mine))
    group_rows = spread(rows_low, ("x", "y")).reshape(-1, D)
    head_group = jnp.concatenate([mine, swap(mine)], axis=0)

    shard = group_targets // vocab_local
    offset = group_targets % vocab_local
    part = jnp.where(offset // PAD_HALF == core, 0, 1)
    local = (shard // RING) == here[0] * RING + here[1]
    targets = jnp.where(
        local, (part * RING + shard % RING) * PAD_HALF + offset % PAD_HALF, -1
    )
    column = jnp.arange(2 * RING * PAD_HALF)[None, :]
    half = jnp.where(column < RING * PAD_HALF, core, 1 - core)
    real = half * PAD_HALF + column % PAD_HALF < vocab_local
    logits = jnp.where(real, matmul_nt(group_rows, head_group), -1e30)
    hits = column == targets[:, None]
    local_max = jnp.max(logits, -1)
    local_sum = jnp.sum(jnp.exp(logits - local_max[:, None]), -1)
    local_target = jnp.sum(jnp.where(hits, logits, 0.0), -1)

    held = jnp.stack([local_max, local_sum, local_target], axis=1).reshape(16, rows_own, 3)
    held = exchange(held.swapaxes(1, 2), ("x", "y"))
    biggest = jnp.max(held[:, 0], 0)
    held = (
        biggest,
        jnp.sum(held[:, 1] * jnp.exp(held[:, 0] - biggest), 0),
        jnp.sum(held[:, 2], 0),
    )
    row_lse = held[0] + jnp.log(held[1])
    own_logp = (held[2] - row_lse).reshape(1, slots, RESP)
    own_count = jnp.sum(live, -1)
    own_scores = jnp.sum(own_logp * live, -1) / jnp.maximum(own_count, 1.0)
    all_scores = both(own_scores.reshape(-1), swap(own_scores.reshape(-1)))
    pro_value, pro_grad = jax.value_and_grad(pro_single)(
        all_scores, weight, all_rank, cand_counts[0]
    )
    my_grad = lax.dynamic_slice_in_dim(pro_grad, core * slots, slots).reshape(1, slots)
    sft_scale = 64 / jnp.maximum(stats[3], 1.0)
    row_grad = (
        my_grad[..., None] / jnp.maximum(own_count, 1.0)[..., None]
        - sft_scale * top_mask[..., None]
    ) * live
    back = spread(jnp.stack([row_grad.reshape(-1), row_lse]), ("x", "y"))
    group_grad = back[:, 0].reshape(-1)
    group_lse = back[:, 1].reshape(-1)

    vocab_probs = jnp.exp(logits - group_lse[:, None])
    logit_grad = (group_grad[:, None] * (hits.astype(jnp.float32) - vocab_probs)).astype(
        jnp.bfloat16
    )
    rows_part = matmul(logit_grad, head_group).astype(jnp.bfloat16)
    rows_part = exchange(rows_part.reshape(16, rows_own, D), ("x", "y"))
    near = RING * PAD_HALF
    head_part = matmul_tn(logit_grad[:, :near], group_rows) + swap(
        matmul_tn(logit_grad[:, near:], group_rows).astype(jnp.bfloat16)
    ).astype(jnp.float32)
    head_part = head_part.astype(jnp.bfloat16).reshape(RING, PAD_HALF, D)
    rows_part, head_part = lax.optimization_barrier((rows_part, head_part))
    head_part = exchange(head_part, "z")
    rows_grad = jnp.sum(rows_part.astype(jnp.float32), 0)

    grad_hidden, gain_fin_grad, bias_fin_grad = norm_back(hidden, pieces[4], pieces[5], rows_grad)
    input_grad, mat_grads, vector_head, vector_tail, head_part = layer_backward(
        inputs, saved, mats, pieces, grad_hidden, head_part
    )
    head_own = jnp.sum(head_part.astype(jnp.float32), 0)

    head_grad = both(head_own, swap(head_own))[:vocab_local]

    (query_g, kv_g), proj_g, up_g, down_g = mat_grads
    vector_grad = jnp.concatenate(vector_head + [gain_fin_grad, bias_fin_grad] + vector_tail)
    vector_high = vector_grad.astype(jnp.bfloat16)
    vector_low = (vector_grad - vector_high.astype(jnp.float32)).astype(jnp.bfloat16)
    vector_both = jnp.stack([vector_high, vector_low]).reshape(4, 64, 120).swapaxes(0, 1)
    vector_both = jnp.pad(vector_both, ((0, 0), (0, 4), (0, slots * SEQ - 120)))
    turned_grad = input_grad.astype(jnp.bfloat16).T.reshape(64, 16, slots * SEQ)
    turned_grad = jnp.concatenate([turned_grad, vector_both], axis=1)
    rest = jnp.concatenate([up_g, proj_g, query_g, kv_g], axis=1).reshape(64, 8, 8 * D)
    down_g = down_g.reshape(64, 32, D)
    down_g, head_own = lax.optimization_barrier((down_g, head_own))
    down_g = exchange(down_g, AXES)
    turned_grad, down_g, rest = lax.optimization_barrier((turned_grad, down_g, rest))
    turned_grad = exchange(turned_grad, AXES)
    embed_rows = turned_grad[:, :16].astype(jnp.float32).swapaxes(0, 1).reshape(16, -1)
    vector_both = jnp.sum(turned_grad[:, 16:20, :120].astype(jnp.float32), 0).reshape(2, 2, 120)
    vector_both = vector_both[0] + vector_both[1]
    vector_grad = lax.dynamic_index_in_dim(vector_both, core, 0, False) + swap(
        lax.dynamic_index_in_dim(vector_both, 1 - core, 0, False)
    )

    rest, embed_rows = lax.optimization_barrier((rest, embed_rows))
    rest = exchange(rest, AXES)
    embed_grad = fold(embed_rows, flat_ids, embed_table.shape[0])
    embed_grad = (embed_grad + swap(embed_grad)).T
    rest = jnp.sum(rest.astype(jnp.float32), 0)

    down_g = jnp.sum(down_g.astype(jnp.float32), 0)
    shards = (rest[:, 5 * D :], rest[:, 4 * D : 5 * D], rest[:, : 4 * D], down_g, vector_grad)
    local_squares = sum((jnp.sum(piece * piece) for piece in shards))
    local_squares = (
        local_squares + (jnp.sum(embed_grad * embed_grad) + jnp.sum(head_grad * head_grad)) / 2
    )
    sft_local = -jnp.sum(own_logp * live * top_mask[..., None])
    sums = jnp.sum(
        spread(jnp.stack([local_squares, pro_value / 2, sft_local]), ("cand", *AXES)), 0
    )
    grad_norm = jnp.sqrt(sums[0])
    factor = jnp.minimum(1.0, CLIP_NORM / (grad_norm + 1e-06))
    embed_new = adam_update(embed_table, embed_first, embed_second, embed_grad, factor)
    head_new = adam_update(head_table, head_first, head_second, head_grad, factor)
    qkv_new = adam_update(qkv_weight, qkv_first, qkv_second, shards[0], factor)
    proj_new = adam_update(proj_weight, proj_first, proj_second, shards[1], factor)
    up_new = adam_update(up_weight, up_first, up_second, shards[2], factor)
    down_new = adam_update(down_weight, down_first, down_second, shards[3], factor)
    vector_first_new, vector_second_new = moments(vector_first, vector_second, shards[4], factor)
    loss_parts = jnp.stack([sums[1], sums[2], stats[3]])
    return (
        loss_parts,
        grad_norm,
        my_grad,
        embed_new[0],
        embed_new[1],
        embed_new[2],
        head_new[0],
        head_new[1],
        head_new[2],
        qkv_new[0],
        qkv_new[1],
        qkv_new[2],
        proj_new[0],
        proj_new[1],
        proj_new[2],
        up_new[0],
        up_new[1],
        up_new[2],
        down_new[0],
        down_new[1],
        down_new[2],
        vector_first_new,
        vector_second_new,
    )


def solution(mesh):
    fine = Mesh(mesh.devices.reshape(2, RING, RING, RING), ("cand", *AXES))
    in_specs = (
        P(AXES, "cand", None),
        P(AXES, "cand", None),
        P(AXES, "cand"),
        P(AXES),
        P(AXES, "cand"),
        P(AXES, "cand"),
        P(None, AXES),
        P(None, AXES),
        P(None, AXES),
        P(AXES, None),
        P(AXES, None),
        P(AXES, None),
        P(("cand", *AXES), None),
        P(("cand", *AXES), None),
        P(("cand", *AXES), None),
        P(("cand", *AXES), None),
        P(("cand", *AXES), None),
        P(("cand", *AXES), None),
        P(("cand", *AXES), None),
        P(("cand", *AXES), None),
        P(("cand", *AXES), None),
        P(("cand", *AXES), None),
        P(("cand", *AXES), None),
        P(("cand", *AXES), None),
        P(),
        P(("cand", *AXES)),
        P(("cand", *AXES)),
    )
    out_specs = (
        P(),
        P(),
        P(AXES, "cand"),
        P(None, AXES),
        P(None, AXES),
        P(None, AXES),
        P(AXES, None),
        P(AXES, None),
        P(AXES, None),
        P(("cand", *AXES), None),
        P(("cand", *AXES), None),
        P(("cand", *AXES), None),
        P(("cand", *AXES), None),
        P(("cand", *AXES), None),
        P(("cand", *AXES), None),
        P(("cand", *AXES), None),
        P(("cand", *AXES), None),
        P(("cand", *AXES), None),
        P(("cand", *AXES), None),
        P(("cand", *AXES), None),
        P(("cand", *AXES), None),
        P(("cand", *AXES)),
        P(("cand", *AXES)),
    )
    return jax.shard_map(body, mesh=fine, in_specs=in_specs, out_specs=out_specs, check_vma=False)
```

time: 1000 us -> 771 us (0.77)
  starting transfers between devices: 261 us -> 104 us
  local copies, waits for them, and re-layouts: 173 us -> 63.7 us
  other arithmetic: 214 us -> 117 us
  blocking collectives: 0 us -> 68 us
  Pallas kernels: 0 us -> 64.2 us
  matrix products: 114 us -> 141 us
  waiting for transfers between devices: 193 us -> 174 us
    ppermute x170 -> x4, waiting for transfers between devices: 185 us -> 0.01 us  [body(): lax.ppermute(group.astype(jnp.bfloat16), everyone, [(d, RING * (d % 32) +...]
    ppermute x170 -> x4, starting transfers between devices: 181 us -> 18.9 us  [body(): lax.ppermute(group.astype(jnp.bfloat16), everyone, [(d, RING * (d % 32) +...]
    all_to_all x2 -> x9, waiting for transfers between devices: 5.24 us -> 155 us  [exchange(): return lax.all_to_all(pieces, axes, split_axis=0, concat_axis=0, tiled=True)]
    scatter-add x1 -> x0, other arithmetic: 76.1 us -> none  [body(): jax.ops.segment_sum(embed_rows, flat_ids, num_segments=embed_table.shape[0])]
    all_to_all x0 -> x3, blocking collectives: none -> 68 us  [exchange(): return lax.all_to_all(pieces, axes, split_axis=0, concat_axis=0, tiled=True)]
    pallas_call x0 -> x2, Pallas kernels: none -> 64.2 us  [the longest x1 39.9 us: fold(): pl.pallas_call(fold_kernel, grid=(count // FOLD_BLOCK,), in_specs=[row, r...]
    all_to_all x2 -> x9, starting transfers between devices: 12.5 us -> 73.2 us  [exchange(): return lax.all_to_all(pieces, axes, split_axis=0, concat_axis=0, tiled=True)]
    ppermute x14 -> x12, starting transfers between devices: 67.6 us -> 12 us  [swap(): return lax.ppermute(value, 'cand', [(0, 1), (1, 0)])]
  transfers between devices with their start and end apart: 187 -> 26, of which waited for: 74 -> 14; matrix products, arithmetic and copies ran while one was open for 38% -> 25% of each run, Pallas kernels for 0% -> 8%
where the time goes in v2:
time: 771 us; the launch traced here: 761 us
  waiting for transfers between devices  174 us (23%)
  matrix products  141 us (18%)
  other arithmetic  117 us (15%)
  starting transfers between devices  104 us (13%)
  blocking collectives  68 us (9%)
  Pallas kernels  64.2 us (8%)
  local copies, waits for them, and re-layouts  63.7 us (8%)
  between operations  29.7 us (4%)
    all_to_all x9, waiting for transfers between devices, exchange(): return lax.all_to_all(pieces, axes, split_axis=0, concat_axis=0, tiled=True)  155 us
    all_to_all x9, starting transfers between devices, exchange(): return lax.all_to_all(pieces, axes, split_axis=0, concat_axis=0, tiled=True)  73.2 us
    all_to_all x3, blocking collectives, exchange(): return lax.all_to_all(pieces, axes, split_axis=0, concat_axis=0, tiled=True)  68 us
    dot_general x9, matrix products, matmul_nt(): lax.dot_general(left, right, (((1,), (1,)), ((), ())), preferred_element_...  45.5 us
    dot_general x12, matrix products, matmul_tn(): lax.dot_general(left, right, (((0,), (0,)), ((), ())), preferred_element_...  43.7 us
    dot_general x9, matrix products, matmul(): return jnp.dot(left, right, preferred_element_type=jnp.float32)  41.1 us
    pallas_call x1, Pallas kernels, fold(): pl.pallas_call(fold_kernel, grid=(count // FOLD_BLOCK,), in_specs=[row, r...  39.9 us
    pallas_call x1, Pallas kernels, look_up(): pl.pallas_call(look_kernel, grid=(count // LOOK_BLOCK,), in_specs=[row, r...  24.2 us
  transfers between devices with their start and end apart: 26, of which 14 were waited for; matrix products, arithmetic and copies ran while one was open for 25% of the time, Pallas kernels for 8%

profile of v2, /device:TPU:1, one launch (start us, length us, event | category | flops | bytes accessed | tf_op | source)
XLA Modules:
  0.0 761.0 jit_solution(2426176058247357193)
XLA Ops:
  15.7 8.4 %collective-permute-start.1 = (bf16[8,1024]{1,0:T(8,128)(2,1)S(1)}, bf16[8,1024]{1,0:T(8,128)(2,1)S(1)}, u32[]{:S(2)}, u32[]{:S(2)}) collective-permute-start(bf16[8,1024]{1,0:T(8,128)(2,1)S(1)} %get-tuple-element.145), channel_id=1, source_target_pairs={{0,1},{1,5},{2,9},{3,13},{4,17},{5,21},{6,25},{7,29},{8,33},{9,37}... | collective-permute-start | bytes 49160 | tf_op jit(solution)/shard_map/ppermute | solution.py:421
  39.9 12.2 %all-to-all-start = ((f32[64,1,256]{2,1,0:T(1,128)}), f32[64,1,256]{2,1,0:T(1,128)S(1)}, u32[]{:S(2)}, u32[]{:S(2)}) async-start(f32[64,1,256]{2,1,0:T(1,128)} %broadcast_in_dim.92), calls=%async_computation | async-start | bytes 131072 | tf_op jit(solution)/shard_map/all_to_all | solution.py:38
  64.0 24.2 %look_up.1 = f32[16,12288]{1,0:T(8,128)S(1)} custom-call(s32[1,12288]{1,0:T(1,128)S(1)} %and_select_fusion.1.high_ref, s32[1,12288]{1,0:T(1,128)S(1)} %get-tuple-element.120.low_ref, f32[16,50304]{1,0:T(8,128)S(1)} %bitcast.179), custom_call_target="tpu_custom_call" | custom-call | flops 19830669312 | bytes 3219456 | tf_op jit(solution)/shard_map/look_up/pallas_call | solution.py:103
  106.9 10.7 %all-to-all-done.1 = bf16[64,16,192]{2,1,0:T(8,128)(2,1)} async-done(((bf16[64,16,192]{2,1,0:T(8,128)(2,1)}), bf16[64,16,192]{2,1,0:T(8,128)(2,1)}, u32[]{:S(2)}, u32[]{:S(2)}) %all-to-all-start.1) | async-done | bytes 393248 | tf_op jit(solution)/shard_map/all_to_all | solution.py:38
  155.1 8.9 %multiply_convert_fusion.1 = (bf16[96,4096]{1,0:T(8,128)(2,1)}, f32[96,4096]{1,0:T(8,128)}, f32[96,4096]{1,0:T(8,128)}) fusion(f32[4096]{0:T(1024)} %slice.309, bf16[96,1024]{1,0:T(8,128)(2,1)} %add_convert_fusion.13, bf16[1024,12288]{1,0:T(8,128)(2,1)} %all-gather.2.cloned.1.call-done), kind=kOutput, calls=%fused_computation.88 | convolution fusion | flops 831258624 | bytes 12533760 | tf_op jit(solution)/shard_map/dot_general | solution.py:188
  178.9 10.0 %all-to-all-start.3 = ((bf16[16,96,1024]{2,1,0:T(8,128)(2,1)}), bf16[16,96,1024]{2,1,0:T(8,128)(2,1)}, u32[]{:S(2)}, u32[]{:S(2)}) async-start(bf16[16,96,1024]{2,1,0:T(8,128)(2,1)} %broadcast_in_dim.99), calls=%async_computation.3 | async-start | bytes 6291456 | tf_op jit(solution)/shard_map/all_to_all | solution.py:38
  200.0 29.8 %all-to-all-done.3 = bf16[16,96,1024]{2,1,0:T(8,128)(2,1)} async-done(((bf16[16,96,1024]{2,1,0:T(8,128)(2,1)}), bf16[16,96,1024]{2,1,0:T(8,128)(2,1)}, u32[]{:S(2)}, u32[]{:S(2)}) %all-to-all-start.3) | async-done | bytes 3145760 | tf_op jit(solution)/shard_map/all_to_all | solution.py:38
  229.7 19.4 %fusion.219 = (f32[1536]{0:T(1024)S(1)}, f32[1536,3584]{1,0:T(8,128)}) fusion(bf16[1536,1024]{1,0:T(8,128)(2,1)} %bitcast.33, bf16[3584,1024]{1,0:T(8,128)(2,1)} %constant_dynamic-update-slice_fusion.6, pred[3584]{0:T(1024)(128)(4,1)S(1)} %fusion.135), kind=kOutput, calls=%fused_computation.433 | convolution fusion | flops 11285297152 | bytes 32515584 | tf_op jit(solution)/shard_map/dot_general | solution.py:198
  249.2 10.7 %exponential_reduce_fusion = (f32[1536]{0:T(1024)S(1)}, f32[1536]{0:T(1024)S(1)}) fusion(f32[1536,3584]{1,0:T(8,128)} %get-tuple-element.190, f32[1536]{0:T(1024)S(1)} %get-tuple-element.189, s32[1536]{0:T(1024)S(1)} %fusion.152), kind=kLoop, calls=%fused_computation.4 | loop fusion | flops 27522048 | bytes 22044672 | tf_op jit(solution)/shard_map/reduce_sum | solution.py:511
  260.7 11.1 %all-to-all-start.4 = ((f32[16,3,96]{2,1,0:T(4,128)}), f32[16,3,96]{2,1,0:T(4,128)S(1)}, u32[]{:S(2)}, u32[]{:S(2)}) async-start(f32[16,3,96]{2,1,0:T(4,128)} %copy.235), calls=%async_computation.4 | async-start | bytes 65536 | tf_op jit(solution)/shard_map/all_to_all | solution.py:38
  289.3 9.6 %all_to_all.65 = f32[16,2,96]{2,1,0:T(2,128)S(1)} all-to-all(f32[16,2,96]{2,1,0:T(2,128)S(1)} %broadcast_in_dim.107), channel_id=1, replica_groups=mesh['cand'=2,'x'=4,'y'=4,'z'=4] {'x','y'}, dimensions={0} | all-to-all | bytes 24576 | tf_op jit(solution)/shard_map/all_to_all | solution.py:38
  299.1 11.7 %multiply_convert_fusion = bf16[1536,3584]{1,0:T(8,128)(2,1)S(1)} fusion(f32[1536,3584]{1,0:T(8,128)} %get-tuple-element.190, f32[1536]{0:T(1024)S(1)} %sub.245, f32[1536]{0:T(1024)S(1)} %mul.1081, s32[1536]{0:T(1024)S(1)} %fusion.152), kind=kLoop, calls=%fused_computation.1 | loop fusion | flops 33030144 | bytes 33048576 | tf_op jit(solution)/shard_map/convert_element_type | solution.py:541
  310.8 11.7 %fusion.12 = bf16[1792,1024]{1,0:T(8,128)(2,1)} fusion(bf16[1536,1024]{1,0:T(8,128)(2,1)} %bitcast.33, bf16[1536,3584]{1,0:T(8,128)(2,1)S(1)} %multiply_convert_fusion), kind=kOutput, calls=%fused_computation.29 | convolution fusion | flops 5638979584 | bytes 12320768 | tf_op jit(solution)/shard_map/dot_general | solution.py:192
  324.2 15.4 %convolution_convert_fusion.1 = bf16[1536,1024]{1,0:T(8,128)(2,1)} fusion(bf16[1536,3584]{1,0:T(8,128)(2,1)S(1)} %multiply_convert_fusion, bf16[3584,1024]{1,0:T(8,128)(2,1)} %constant_dynamic-update-slice_fusion.6), kind=kOutput, calls=%fused_computation.28 | convolution fusion | flops 11275862016 | bytes 21495808 | tf_op jit(solution)/shard_map/dot_general | solution.py:188
  345.7 10.8 %add_convert_fusion.2 = bf16[1792,1024]{1,0:T(8,128)(2,1)} fusion(bf16[1792,1024]{1,0:T(8,128)(2,1)} %collective-permute-done.7, bf16[1536,1024]{1,0:T(8,128)(2,1)} %bitcast.33, bf16[1536,3584]{1,0:T(8,128)(2,1)} %copy-done.9), kind=kOutput, calls=%fused_computation.18 | convolution fusion | flops 5642649600 | bytes 15990784 | tf_op jit(solution)/shard_map/dot_general | solution.py:192
  356.5 30.5 %all-to-all-done.6 = bf16[16,96,1024]{2,1,0:T(8,128)(2,1)} async-done(((bf16[16,96,1024]{2,1,0:T(8,128)(2,1)}), bf16[16,96,1024]{2,1,0:T(8,128)(2,1)}, u32[]{:S(2)}, u32[]{:S(2)}) %all-to-all-start.6) | async-done | bytes 3145760 | tf_op jit(solution)/shard_map/all_to_all | solution.py:38
  481.0 13.0 %all-to-all-start.8 = ((bf16[64,32,1024]{2,1,0:T(8,128)(2,1)}), bf16[64,32,1024]{2,1,0:T(8,128)(2,1)}, u32[]{:S(2)}, u32[]{:S(2)}) async-start(bf16[64,32,1024]{2,1,0:T(8,128)(2,1)} %bitcast.191), calls=%async_computation.8 | async-start | bytes 8388608 | tf_op jit(solution)/shard_map/all_to_all | solution.py:38
  500.4 7.5 maximum_bitcast_fusion
  507.9 34.5 %all-to-all-done.8 = bf16[64,32,1024]{2,1,0:T(8,128)(2,1)} async-done(((bf16[64,32,1024]{2,1,0:T(8,128)(2,1)}), bf16[64,32,1024]{2,1,0:T(8,128)(2,1)}, u32[]{:S(2)}, u32[]{:S(2)}) %all-to-all-start.8) | async-done | bytes 4194336 | tf_op jit(solution)/shard_map/all_to_all | solution.py:38
  542.4 27.2 %all_to_all.66 = bf16[64,24,192]{2,1,0:T(8,128)(2,1)S(1)} all-to-all(bf16[64,24,192]{2,1,0:T(8,128)(2,1)S(1)} %fusion.94), channel_id=1, replica_groups=mesh['cand'=2,'x'=4,'y'=4,'z'=4] {'x','y','z'}, dimensions={0} | all-to-all | bytes 1179648 | tf_op jit(solution)/shard_map/all_to_all | solution.py:38
  580.6 39.9 %fold.1 = f32[16,50304]{1,0:T(8,128)S(1)} custom-call(s32[1,12288]{1,0:T(1,128)S(1)} %copy-done.6, s32[1,12288]{1,0:T(1,128)S(1)} %copy-done.4, f32[16,12288]{1,0:T(8,128)S(1)} %copy-done.2), custom_call_target="tpu_custom_call" | custom-call | flops 19830669312 | bytes 3219456 | tf_op jit(solution)/shard_map/fold/pallas_call | solution.py:171
  648.3 38.0 %all-to-all-done.10 = bf16[64,8,8192]{2,1,0:T(8,128)(2,1)} async-done(((bf16[64,8,8192]{2,1,0:T(8,128)(2,1)}), bf16[64,8,8192]{2,1,0:T(8,128)(2,1)}, u32[]{:S(2)}, u32[]{:S(2)}) %all-to-all-start.10) | async-done | bytes 8388640 | tf_op jit(solution)/shard_map/all_to_all | solution.py:38
  696.2 31.3 %all_to_all.67 = f32[128,1,3]{2,1,0:T(1,128)S(1)} all-to-all(f32[128,1,3]{2,1,0:T(1,128)S(1)} %broadcast_in_dim.114), channel_id=1, replica_groups=mesh['cand'=2,'x'=4,'y'=4,'z'=4] {'cand','x','y','z'}, dimensions={0} | all-to-all | bytes 3072 | tf_op jit(solution)/shard_map/all_to_all | solution.py:38
  736.0 7.8 %multiply_subtract_fusion.1 = (f32[50304,16]{0,1:T(8,128)}, f32[50304,16]{0,1:T(8,128)}, f32[50304,16]{0,1:T(8,128)}) fusion(f32[50304,16]{0,1:T(8,128)S(1)} %copy-done.1, f32[16,50304]{1,0:T(8,128)} %get-tuple-element.98, f32[]{:T(128)S(6)} %min.3, f32[50304,16]{0,1:T(8,128)} %param.35, f32[50304,16]{0,1:T(8,128)} %param.34), kind=kLoop, calls=%fused_computation.45 | loop fusion | flops 12877824 | bytes 22536196 | tf_op jit(solution)/shard_map/sub | solution.py:371
  (481 shorter events, 297.2 us)
Async XLA Ops:
  7.2 126.8 %all-gather.2.cloned.1.call-start = ((), (), s32[]{:S(2)}) async-start(), calls=%async_computation.12 | async-start | bytes 25362432 | tf_op jit(solution)/shard_map/all_gather | solution.py:432
  8.2 21.5 %collective-permute-start.3 = (bf16[8,1024]{1,0:T(8,128)(2,1)S(1)}, bf16[8,1024]{1,0:T(8,128)(2,1)S(1)}, u32[]{:S(2)}, u32[]{:S(2)}) collective-permute-start(bf16[8,1024]{1,0:T(8,128)(2,1)S(1)} %get-tuple-element.143), channel_id=1, source_target_pairs={{0,3},{1,7},{2,11},{3,15},{4,19},{5,23},{6,27},{7,31},{8,35},{9,39... | collective-permute-start | bytes 49160 | tf_op jit(solution)/shard_map/ppermute | solution.py:421
  13.1 16.5 %collective-permute-start.2 = (bf16[8,1024]{1,0:T(8,128)(2,1)S(1)}, bf16[8,1024]{1,0:T(8,128)(2,1)S(1)}, u32[]{:S(2)}, u32[]{:S(2)}) collective-permute-start(bf16[8,1024]{1,0:T(8,128)(2,1)S(1)} %get-tuple-element.144), channel_id=1, source_target_pairs={{0,2},{1,6},{2,10},{3,14},{4,18},{5,22},{6,26},{7,30},{8,34},{9,38... | collective-permute-start | bytes 49160 | tf_op jit(solution)/shard_map/ppermute | solution.py:421
  15.7 13.9 %collective-permute-start.1 = (bf16[8,1024]{1,0:T(8,128)(2,1)S(1)}, bf16[8,1024]{1,0:T(8,128)(2,1)S(1)}, u32[]{:S(2)}, u32[]{:S(2)}) collective-permute-start(bf16[8,1024]{1,0:T(8,128)(2,1)S(1)} %get-tuple-element.145), channel_id=1, source_target_pairs={{0,1},{1,5},{2,9},{3,13},{4,17},{5,21},{6,25},{7,29},{8,33},{9,37}... | collective-permute-start | bytes 49160 | tf_op jit(solution)/shard_map/ppermute | solution.py:421
  24.1 5.6 collective-permute-start
  39.9 20.7 %all-to-all-start = ((f32[64,1,256]{2,1,0:T(1,128)}), f32[64,1,256]{2,1,0:T(1,128)S(1)}, u32[]{:S(2)}, u32[]{:S(2)}) async-start(f32[64,1,256]{2,1,0:T(1,128)} %broadcast_in_dim.92), calls=%async_computation | async-start | bytes 131072 | tf_op jit(solution)/shard_map/all_to_all | solution.py:38
  95.1 22.5 %all-to-all-start.1 = ((bf16[64,16,192]{2,1,0:T(8,128)(2,1)}), bf16[64,16,192]{2,1,0:T(8,128)(2,1)}, u32[]{:S(2)}, u32[]{:S(2)}) async-start(bf16[64,16,192]{2,1,0:T(8,128)(2,1)} %bitcast.202), calls=%async_computation.1 | async-start | bytes 1048576 | tf_op jit(solution)/shard_map/all_to_all | solution.py:38
  121.5 55.0 %all-to-all-start.2 = ((bf16[4,448,1024]{2,1,0:T(8,128)(2,1)}), bf16[4,448,1024]{2,1,0:T(8,128)(2,1)}, u32[]{:S(2)}, u32[]{:S(2)}) async-start(bf16[4,448,1024]{2,1,0:T(8,128)(2,1)} %broadcast_in_dim.98), calls=%async_computation.2 | async-start | bytes 7340032 | tf_op jit(solution)/shard_map/all_to_all | solution.py:38
  176.5 19.1 %collective-permute-start.5 = (bf16[1792,1024]{1,0:T(8,128)(2,1)}, bf16[1792,1024]{1,0:T(8,128)(2,1)}, u32[]{:S(2)}, u32[]{:S(2)}) collective-permute-start(bf16[1792,1024]{1,0:T(8,128)(2,1)} %bitcast.32), channel_id=1, source_target_pairs={{0,64},{64,0},{1,65},{65,1},{2,66},{66,2},{3,67},{67,3},{4,68},{68... | collective-permute-start | bytes 11010056 | tf_op jit(solution)/shard_map/ppermute | solution.py:34
  178.9 50.8 %all-to-all-start.3 = ((bf16[16,96,1024]{2,1,0:T(8,128)(2,1)}), bf16[16,96,1024]{2,1,0:T(8,128)(2,1)}, u32[]{:S(2)}, u32[]{:S(2)}) async-start(bf16[16,96,1024]{2,1,0:T(8,128)(2,1)} %broadcast_in_dim.99), calls=%async_computation.3 | async-start | bytes 6291456 | tf_op jit(solution)/shard_map/all_to_all | solution.py:38
  260.7 17.6 %all-to-all-start.4 = ((f32[16,3,96]{2,1,0:T(4,128)}), f32[16,3,96]{2,1,0:T(4,128)S(1)}, u32[]{:S(2)}, u32[]{:S(2)}) async-start(f32[16,3,96]{2,1,0:T(4,128)} %copy.235), calls=%async_computation.4 | async-start | bytes 65536 | tf_op jit(solution)/shard_map/all_to_all | solution.py:38
  279.2 3.8 collective-permute-start.6
  322.5 23.2 %collective-permute-start.7 = (bf16[1792,1024]{1,0:T(8,128)(2,1)}, bf16[1792,1024]{1,0:T(8,128)(2,1)}, u32[]{:S(2)}, u32[]{:S(2)}) collective-permute-start(bf16[1792,1024]{1,0:T(8,128)(2,1)} %fusion.12), channel_id=1, source_target_pairs={{0,64},{64,0},{1,65},{65,1},{2,66},{66,2},{3,67},{67,3},{4,68},{68... | collective-permute-start | bytes 11010056 | tf_op jit(solution)/shard_map/ppermute | solution.py:34
  339.7 47.3 %all-to-all-start.6 = ((bf16[16,96,1024]{2,1,0:T(8,128)(2,1)}), bf16[16,96,1024]{2,1,0:T(8,128)(2,1)}, u32[]{:S(2)}, u32[]{:S(2)}) async-start(bf16[16,96,1024]{2,1,0:T(8,128)(2,1)} %bitcast.199), calls=%async_computation.6 | async-start | bytes 6291456 | tf_op jit(solution)/shard_map/all_to_all | solution.py:38
  415.1 46.9 %all-to-all-start.7 = ((bf16[4,448,1024]{2,1,0:T(8,128)(2,1)}), bf16[4,448,1024]{2,1,0:T(8,128)(2,1)}, u32[]{:S(2)}, u32[]{:S(2)}) async-start(bf16[4,448,1024]{2,1,0:T(8,128)(2,1)} %bitcast.198), calls=%async_computation.7 | async-start | bytes 7340032 | tf_op jit(solution)/shard_map/all_to_all | solution.py:38
  421.3 36.6 %collective-permute-start.12 = (bf16[512,2048]{1,0:T(8,128)(2,1)S(1)}, bf16[512,2048]{1,0:T(8,128)(2,1)S(1)}, u32[]{:S(2)}, u32[]{:S(2)}) collective-permute-start(bf16[512,2048]{1,0:T(8,128)(2,1)S(1)} %convolution_convert_fusion.3), channel_id=1, source_target_pairs={{0,64},{64,0},{1,65},{65,1},{2,66},{66,2},{3,67},{67,3},{4,68},{68... | collective-permute-start | bytes 6291464 | tf_op jit(solution)/shard_map/ppermute | solution.py:34
  423.6 27.1 %collective-permute-start.11 = (bf16[512,1024]{1,0:T(8,128)(2,1)S(1)}, bf16[512,1024]{1,0:T(8,128)(2,1)S(1)}, u32[]{:S(2)}, u32[]{:S(2)}) collective-permute-start(bf16[512,1024]{1,0:T(8,128)(2,1)S(1)} %convolution_convert_fusion.4), channel_id=1, source_target_pairs={{0,64},{64,0},{1,65},{65,1},{2,66},{66,2},{3,67},{67,3},{4,68},{68... | collective-permute-start | bytes 3145736 | tf_op jit(solution)/shard_map/ppermute | solution.py:34
  447.4 28.1 %collective-permute-start.8 = (bf16[2048,1024]{1,0:T(8,128)(2,1)}, bf16[2048,1024]{1,0:T(8,128)(2,1)}, u32[]{:S(2)}, u32[]{:S(2)}) collective-permute-start(bf16[2048,1024]{1,0:T(8,128)(2,1)} %convolution_convert_fusion.2), channel_id=1, source_target_pairs={{0,64},{64,0},{1,65},{65,1},{2,66},{66,2},{3,67},{67,3},{4,68},{68... | collective-permute-start | bytes 12582920 | tf_op jit(solution)/shard_map/ppermute | solution.py:34
  448.0 8.6 %collective-permute-start.10 = (bf16[512,1024]{1,0:T(8,128)(2,1)S(1)}, bf16[512,1024]{1,0:T(8,128)(2,1)S(1)}, u32[]{:S(2)}, u32[]{:S(2)}) collective-permute-start(bf16[512,1024]{1,0:T(8,128)(2,1)S(1)} %convolution_convert_fusion.5), channel_id=1, source_target_pairs={{0,64},{64,0},{1,65},{65,1},{2,66},{66,2},{3,67},{67,3},{4,68},{68... | collective-permute-start | bytes 3145736 | tf_op jit(solution)/shard_map/ppermute | solution.py:34
  448.1 48.4 %collective-permute-start.9 = (bf16[512,4096]{1,0:T(8,128)(2,1)}, bf16[512,4096]{1,0:T(8,128)(2,1)}, u32[]{:S(2)}, u32[]{:S(2)}) collective-permute-start(bf16[512,4096]{1,0:T(8,128)(2,1)} %convolution_convert_fusion), channel_id=1, source_target_pairs={{0,64},{64,0},{1,65},{65,1},{2,66},{66,2},{3,67},{67,3},{4,68},{68... | collective-permute-start | bytes 12582920 | tf_op jit(solution)/shard_map/ppermute | solution.py:34
  481.0 61.4 %all-to-all-start.8 = ((bf16[64,32,1024]{2,1,0:T(8,128)(2,1)}), bf16[64,32,1024]{2,1,0:T(8,128)(2,1)}, u32[]{:S(2)}, u32[]{:S(2)}) async-start(bf16[64,32,1024]{2,1,0:T(8,128)(2,1)} %bitcast.191), calls=%async_computation.8 | async-start | bytes 8388608 | tf_op jit(solution)/shard_map/all_to_all | solution.py:38
  572.5 113.8 %all-to-all-start.10 = ((bf16[64,8,8192]{2,1,0:T(8,128)(2,1)}), bf16[64,8,8192]{2,1,0:T(8,128)(2,1)}, u32[]{:S(2)}, u32[]{:S(2)}) async-start(bf16[64,8,8192]{2,1,0:T(8,128)(2,1)} %maximum_bitcast_fusion), calls=%async_computation.10 | async-start | bytes 16777216 | tf_op jit(solution)/shard_map/all_to_all | solution.py:38
  620.5 21.5 %collective-permute-start.14 = (f32[16,50304]{1,0:T(8,128)S(1)}, f32[16,50304]{1,0:T(8,128)}, u32[]{:S(2)}, u32[]{:S(2)}) collective-permute-start(f32[16,50304]{1,0:T(8,128)S(1)} %fold.1), channel_id=1, source_target_pairs={{0,64},{64,0},{1,65},{65,1},{2,66},{66,2},{3,67},{67,3},{4,68},{68... | collective-permute-start | bytes 9658376 | tf_op jit(solution)/shard_map/ppermute | solution.py:34
  623.5 8.2 %collective-permute-start.15 = (f32[448,1024]{1,0:T(8,128)}, f32[448,1024]{1,0:T(8,128)}, u32[]{:S(2)}, u32[]{:S(2)}) collective-permute-start(f32[448,1024]{1,0:T(8,128)} %convert_reduce_fusion.4), channel_id=1, source_target_pairs={{0,64},{64,0},{1,65},{65,1},{2,66},{66,2},{3,67},{67,3},{4,68},{68... | collective-permute-start | bytes 5505032 | tf_op jit(solution)/shard_map/ppermute | solution.py:34
  (103 other events, 864.9 us)
Sparse Core Ops, SparseCore 0:
  30.6 103.3 all-gather.1

commit v3 on v2

--- a/solution.py
+++ b/solution.py
@@ -1,5 +1,8 @@
+import math
+
 import jax
 import jax.numpy as jnp
+import numpy as np
 from jax import lax
 from jax.experimental import pallas as pl
 from jax.experimental.pallas import tpu as pltpu
@@ -26,6 +29,7 @@
 
 
 RING = 4
+SLOTS = 3
 PAD_HALF = 448
 AXES = ("x", "y", "z")
 
@@ -43,14 +47,30 @@
     return exchange(jnp.broadcast_to(value[None], (count, *value.shape)), axes)
 
 
-def core_sum(left, right, low=jnp.bfloat16):
+def shift(value, axis, step):
+    return lax.ppermute(value, axis, [(i, (i + step) % RING) for i in range(RING)])
+
+
+def ring_sum(pieces, axis):
+    me = lax.axis_index(axis)
+
+    def piece(step):
+        return lax.dynamic_index_in_dim(pieces, (me + step) % RING, 0, False)
+
+    got = [shift(piece(step), axis, step).astype(jnp.float32) for step in (1, 2, 3)]
+    return piece(0).astype(jnp.float32) + got[1] + (got[0] + got[2])
+
+
+def of_both(value):
+    return jnp.concatenate([value, swap(value)], axis=0)
+
+
+def half_of_both(value):
     core = lax.axis_index("cand")
-    half = left.shape[1] // 2
-    kept = lax.dynamic_slice_in_dim(left, core * half, half, axis=1)
-    given = lax.dynamic_slice_in_dim(left, (1 - core) * half, half, axis=1)
-    return (
-        matmul_tn(kept, right) + swap(matmul_tn(given, right).astype(low)).astype(jnp.float32)
-    ).astype(low)
+    half = value.shape[1] // 2
+    kept = lax.dynamic_slice_in_dim(value, core * half, half, axis=1)
+    given = lax.dynamic_slice_in_dim(value, (1 - core) * half, half, axis=1)
+    return jnp.concatenate([kept, swap(given)], axis=0)
 
 
 WIDE = 256
@@ -222,127 +242,293 @@
     return pieces
 
 
-def gelu_exact(values):
-    return jax.nn.gelu(values, approximate=False)
-
-
-def rotary(inputs, places, sign):
+def turn(values, tables, sign):
+    cosine, low, high = tables
+    return (
+        values * cosine
+        + sign * (pltpu.roll(values, 120, axis=1) * low + pltpu.roll(values, 8, axis=1) * high)
+    )
+
+
+def dot_nn(left, right):
+    return jnp.dot(left, right, preferred_element_type=jnp.float32)
+
+
+def dot_nt(left, right):
+    return lax.dot_general(
+        left, right, (((1,), (1,)), ((), ())), preferred_element_type=jnp.float32
+    )
+
+
+def dot_tn(left, right):
+    return lax.dot_general(
+        left, right, (((0,), (0,)), ((), ())), preferred_element_type=jnp.float32
+    )
+
+
+def pair_of(values):
+    lanes = lax.broadcasted_iota(jnp.int32, values.shape, 1)
+    zero = jnp.zeros_like(values)
+    return (jnp.where(lanes < HEAD_DIM, values, zero), jnp.where(lanes < HEAD_DIM, zero, values))
+
+
+def row_places(rows, width, axis):
+    row = lax.broadcasted_iota(jnp.int32, (rows, width), axis)
+    live = SLOTS * RESP
+    late = row >= live
+    row = jnp.where(late, row - live, row)
+    inside = row % RESP
+    place = jnp.where(
+        late, jnp.where(inside == 0, SEQ - 1, inside - 1), inside + (SEQ - RESP - 1)
+    )
+    return row // RESP, place
+
+
+def softmax_rows(query, keys):
+    rows, width = query.shape[0], keys.shape[0]
+    scores = dot_nt(query, keys) * HEAD_DIM ** (-0.5)
+    query_slot, query_place = row_places(rows, width, 0)
+    key_slot, key_place = row_places(rows, width, 1)
+    seen = (query_slot == key_slot) & (query_place >= key_place)
+    scores = jnp.where(seen, scores, -1e30)
+    scores = jnp.exp(scores - jnp.max(scores, axis=1, keepdims=True))
+    return scores / jnp.sum(scores, axis=1, keepdims=True)
+
+
+def forward_kernel(
+    attn_ref, mlp_ref, query_w, key_w, value_w, proj_w, up_w, down_w,
+    query_b, key_b, value_b, up_b, regroup, cosine, low, high,
+    query_ref, key_ref, value_ref, mixed_ref, up_ref, act_ref, out_ref,
+):
+    live = query_ref.shape[0]
+    tables = (cosine[...], low[...], high[...])
+    firsts = tuple(table[:live] for table in tables)
+    attn = attn_ref[...]
+    query = turn(dot_nn(attn[:live], query_w[...]) + query_b[...], firsts, 1.0).astype(jnp.bfloat16)
+    keys = turn(dot_nn(attn, key_w[...]) + key_b[...], tables, 1.0).astype(jnp.bfloat16)
+    values = (dot_nn(attn, value_w[...]) + value_b[...]).astype(jnp.bfloat16)
+    query_ref[...] = query
+    key_ref[...] = keys
+    value_ref[...] = values
+    mixed = 0.0
+    for part, held in zip(pair_of(query), pair_of(values)):
+        probs = softmax_rows(part, keys).astype(jnp.bfloat16)
+        mixed = mixed + dot_nn(probs, held)
+    mixed = mixed.astype(jnp.bfloat16)
+    mixed_ref[...] = mixed
+    up_val = dot_nn(mlp_ref[...], up_w[...]) + up_b[...]
+    act = (0.5 * up_val * (1.0 + lax.erf(up_val * 0.5**0.5))).astype(jnp.bfloat16)
+    up_ref[...] = up_val
+    act_ref[...] = act
+    part = dot_nn(mixed, proj_w[...])
+    act = dot_nn(act, regroup[...]).astype(jnp.bfloat16)
+    for k in range(4):
+        part = part + dot_nn(act[:, 128 * k : 128 * k + 128], down_w[:, D * k : D * k + D])
+
+    @pl.when(pl.program_id(0) == 0)
+    def _():
+        out_ref[...] = part
+
+    @pl.when(pl.program_id(0) > 0)
+    def _():
+        out_ref[...] += part
+
+
+def backward_kernel(
+    grad_ref, query_ref, key_ref, value_ref, up_ref, query_w, key_w, value_w, proj_w, up_w, down_w,
+    regroup, cosine, low, high,
+    query_g, key_g, value_g, up_g, attn_g, mlp_g, query_s, key_s, value_s, up_s,
+):
+    live = query_ref.shape[0]
+    tables = (cosine[...], low[...], high[...])
+    firsts = tuple(table[:live] for table in tables)
+    grad = grad_ref[...]
+    query, keys, values = query_ref[...], key_ref[...], value_ref[...]
+    mixed_grad = dot_nt(grad, proj_w[...]).astype(jnp.bfloat16)
+    query_grad, key_grad, value_grad = 0.0, 0.0, 0.0
+    for part, held, given in zip(pair_of(query), pair_of(keys), pair_of(mixed_grad)):
+        probs = softmax_rows(part, keys)
+        probs_grad = dot_nt(given, values)
+        value_grad = value_grad + dot_tn(probs.astype(jnp.bfloat16), given)
+        score_grad = probs * (probs_grad - jnp.sum(probs * probs_grad, axis=1, keepdims=True))
+        score_grad = score_grad.astype(jnp.bfloat16)
+        query_grad = query_grad + dot_nn(score_grad, held)
+        key_grad = key_grad + dot_tn(score_grad, part)
+    scale = HEAD_DIM ** (-0.5)
+    query_grad = turn(query_grad * scale, firsts, -1.0).astype(jnp.bfloat16)
+    key_grad = turn(key_grad * scale, tables, -1.0).astype(jnp.bfloat16)
+    value_grad = value_grad.astype(jnp.bfloat16)
+    act_grad = jnp.concatenate(
+        [dot_nt(grad, down_w[:, D * k : D * k + D]) for k in range(4)], axis=1
+    )
+    act_high = act_grad.astype(jnp.bfloat16)
+    act_low = (act_grad - act_high.astype(jnp.float32)).astype(jnp.bfloat16)
+    act_grad = dot_nt(act_high, regroup[...]) + dot_nt(act_low, regroup[...])
+    up_val = up_ref[...]
+    slope = 0.5 * (1.0 + lax.erf(up_val * 0.5**0.5)) + up_val * (
+        jnp.exp(-0.5 * up_val * up_val) * (2.0 * math.pi) ** (-0.5)
+    )
+    up_grad = (act_grad * slope).astype(jnp.bfloat16)
+    for ref, sums, value in (
+        (query_g, query_s, query_grad),
+        (key_g, key_s, key_grad),
+        (value_g, value_s, value_grad),
+        (up_g, up_s, up_grad),
+    ):
+        ref[...] = value
+        sums[...] = jnp.sum(value.astype(jnp.float32), axis=0, keepdims=True)
+    first = dot_nt(query_grad, query_w[...])
+    both = dot_nt(key_grad, key_w[...]) + dot_nt(value_grad, value_w[...])
+    mlp = dot_nt(up_grad, up_w[...])
+
+    @pl.when(pl.program_id(0) == 0)
+    def _():
+        attn_g[...] = both
+        attn_g[:live] += first
+        mlp_g[...] = mlp
+
+    @pl.when(pl.program_id(0) > 0)
+    def _():
+        attn_g[...] += both
+        attn_g[:live] += first
+        mlp_g[...] += mlp
+
+
+def turn_tables(slots):
     half = ROT // 2
-    freq = 10000.0 ** (-jnp.arange(half).astype(jnp.float32) * (2.0 / ROT))
-    angle = places.astype(jnp.float32)[:, None] * freq[None, :]
-    cosine = jnp.cos(angle)[:, None, :]
-    sine = sign * jnp.sin(angle)[:, None, :]
-    first = inputs[..., :half]
-    second = inputs[..., half:ROT]
-    return jnp.concatenate(
-        [first * cosine - second * sine, second * cosine + first * sine, inputs[..., ROT:]], axis=-1
-    )
-
-
-def key_places():
-    return (jnp.arange(SEQ) + (SEQ - RESP - 1)) % SEQ
-
-
-def attention_probs(query, keys):
-    scores = jnp.einsum(
-        "cqhd,ckhd->chqk", query, keys, preferred_element_type=jnp.float32
-    ) * HEAD_DIM ** (-0.5)
-    places = key_places()
-    causal = places[:RESP, None] >= places[None, :]
-    return jax.nn.softmax(jnp.where(causal, scores, -1e30), axis=-1)
-
-
-def joined(rows, slots):
-    cut = rows.reshape(2, slots, RESP, *rows.shape[1:])
-    return jnp.concatenate([cut[0], cut[1]], axis=1)
-
-
-def parted(rows):
-    cut = jnp.stack([rows[:, :RESP], rows[:, RESP:]])
-    return cut.reshape(-1, *rows.shape[2:])
-
-
-def layer_forward(inputs, mats, pieces):
-    query_w, kv_w, proj_w, up_w, down_w = mats
-    live = inputs.shape[0] // 2
-    slots = live // RESP
-    first = inputs[:live]
-    attn_in = layer_norm(inputs, pieces[0], pieces[1]).astype(jnp.bfloat16)
-    mlp_in = layer_norm(first, pieces[2], pieces[3]).astype(jnp.bfloat16)
-    query = matmul(attn_in[:live], query_w) + pieces[6][:D]
-    both = matmul(attn_in, kv_w) + pieces[6][D:]
-    query = rotary(query.reshape(slots, RESP, HEADS, HEAD_DIM), key_places()[:RESP], 1.0)
-    keys = joined(both[:, :D], slots).reshape(slots, SEQ, HEADS, HEAD_DIM)
-    keys = rotary(keys, key_places(), 1.0)
-    values = joined(both[:, D:], slots).reshape(slots, SEQ, HEADS, HEAD_DIM)
-    query, keys, values = [part.astype(jnp.bfloat16) for part in (query, keys, values)]
-    probs_low = attention_probs(query, keys).astype(jnp.bfloat16)
-    mixed = jnp.einsum("chqk,ckhd->cqhd", probs_low, values, preferred_element_type=jnp.float32)
-    mixed = mixed.astype(jnp.bfloat16).reshape(-1, D)
-    up_val = matmul(mlp_in, up_w) + pieces[8]
-    act = gelu_exact(up_val).astype(jnp.bfloat16)
-    mlp = sum(matmul(act[:, k * D : (k + 1) * D], part) for k, part in enumerate(down_w))
-    hidden = first + (matmul(mixed, proj_w) + pieces[7]) + (mlp + pieces[9])
-    return (hidden, (attn_in, mlp_in, query, keys, values, mixed, up_val, act))
-
-
-def layer_backward(inputs, saved, mats, pieces, grad_hidden, ahead):
-    query_w, kv_w, proj_w, up_w, down_w = mats
-    attn_in, mlp_in, query, keys, values, mixed, up_val, act = saved
-    live = inputs.shape[0] // 2
-    slots = live // RESP
-    first = inputs[:live]
-    grad_low = grad_hidden.astype(jnp.bfloat16)
-    grad_sum = jnp.sum(grad_low.astype(jnp.float32), 0)
-    down_grad = core_sum(act, grad_low)
-    act_grad = jnp.concatenate([matmul_nt(grad_low, part) for part in down_w], axis=1)
-    gelu_out, gelu_pull = jax.vjp(gelu_exact, up_val)
-    up_grad_low = gelu_pull(act_grad)[0].astype(jnp.bfloat16)
-    up_w_grad = core_sum(mlp_in, up_grad_low)
-    mlp_in_grad = matmul_nt(up_grad_low, up_w)
-    proj_grad = core_sum(mixed, grad_low)
-    mixed_grad = (
-        matmul_nt(grad_low, proj_w).astype(jnp.bfloat16).reshape(slots, RESP, HEADS, HEAD_DIM)
-    )
-    probs = attention_probs(query, keys)
-    probs_low = probs.astype(jnp.bfloat16)
-    probs_grad = jnp.einsum(
-        "cqhd,ckhd->chqk", mixed_grad, values, preferred_element_type=jnp.float32
-    )
-    value_grad = jnp.einsum(
-        "chqk,cqhd->ckhd", probs_low, mixed_grad, preferred_element_type=jnp.float32
-    )
-    score_grad = probs * (probs_grad - jnp.sum(probs * probs_grad, -1, keepdims=True))
-    score_grad = score_grad.astype(jnp.bfloat16)
-    scale = HEAD_DIM ** (-0.5)
-    query_grad = (
-        jnp.einsum("chqk,ckhd->cqhd", score_grad, keys, preferred_element_type=jnp.float32) * scale
-    )
-    key_grad = (
-        jnp.einsum("chqk,cqhd->ckhd", score_grad, query, preferred_element_type=jnp.float32) * scale
-    )
-    query_grad = rotary(query_grad, key_places()[:RESP], -1.0).reshape(live, D)
-    key_grad = rotary(key_grad, key_places(), -1.0).reshape(slots, SEQ, D)
-    value_grad = value_grad.reshape(slots, SEQ, D)
-    query_grad = query_grad.astype(jnp.bfloat16)
-    both_grad = jnp.concatenate([parted(key_grad), parted(value_grad)], axis=1).astype(jnp.bfloat16)
-    qkv_w_grad = (core_sum(attn_in[:live], query_grad), core_sum(attn_in, both_grad))
-    query_grad, both_grad, ahead = lax.optimization_barrier((query_grad, both_grad, ahead))
-    attn_in_grad = matmul_nt(both_grad, kv_w)
-    attn_in_grad = attn_in_grad + jnp.pad(matmul_nt(query_grad, query_w), ((0, live), (0, 0)))
-    input_one, gain_one_grad, bias_one_grad = norm_back(inputs, pieces[0], pieces[1], attn_in_grad)
-    input_two, gain_two_grad, bias_two_grad = norm_back(first, pieces[2], pieces[3], mlp_in_grad)
-    input_grad = input_one + jnp.pad(grad_hidden + input_two, ((0, live), (0, 0)))
-    vector_head = [gain_one_grad, bias_one_grad, gain_two_grad, bias_two_grad]
-    vector_tail = [
-        jnp.sum(query_grad.astype(jnp.float32), 0),
-        jnp.sum(both_grad.astype(jnp.float32), 0),
-        grad_sum,
-        jnp.sum(up_grad_low.astype(jnp.float32), 0),
-        grad_sum,
+    row = np.arange(2 * slots * RESP)
+    inside = row % RESP
+    place = np.where(row < slots * RESP, inside + SEQ - RESP - 1, (inside - 1) % SEQ)
+    lane = np.arange(2 * HEAD_DIM) % HEAD_DIM
+    freq = np.float32(10000.0) ** (-(np.arange(half) * np.float32(2.0 / ROT)).astype(np.float32))
+    angle = place.astype(np.float32)[:, None] * freq.astype(np.float32)[lane % half][None, :]
+    cosine = np.where(lane < ROT, np.cos(angle), 1.0).astype(np.float32)
+    sine = np.sin(angle)
+    low = np.where(lane < half, -sine, 0.0).astype(np.float32)
+    high = np.where((lane >= half) & (lane < ROT), sine, 0.0).astype(np.float32)
+    return cosine, low, high
+
+
+def regroup_table():
+    at = np.arange(512)
+    to = (at // 8 % 4) * 128 + (at // 32) * 8 + at % 8
+    table = np.zeros((512, 512), np.float32)
+    table[at, to] = 1.0
+    return jnp.asarray(table, jnp.bfloat16)
+
+
+def weight_specs():
+    wide = 2 * HEAD_DIM
+    return [
+        pl.BlockSpec((D, wide), lambda j: (0, j)),
+        pl.BlockSpec((D, wide), lambda j: (0, 8 + j)),
+        pl.BlockSpec((D, wide), lambda j: (0, 16 + j)),
+        pl.BlockSpec((wide, D), lambda j: (j, 7)),
+        pl.BlockSpec((D, 512), lambda j: (0, 6 + j)),
+        pl.BlockSpec((128, 4 * D), lambda j: (j, 2)),
     ]
-    mat_grads = (qkv_w_grad, proj_grad, up_w_grad, down_grad)
-    return (input_grad, mat_grads, vector_head, vector_tail, ahead)
+
+
+def whole(*shape):
+    return pl.BlockSpec(shape, lambda j: (0, 0))
+
+
+def columns(rows, width):
+    return pl.BlockSpec((rows, width), lambda j: (0, j))
+
+
+def layer_forward(attn_in, mlp_in, gathered, pieces, tables):
+    rows, live = attn_in.shape[0], mlp_in.shape[0]
+    wide = 2 * HEAD_DIM
+    bias = pieces[6].reshape(1, 3 * D)
+    shape = jax.ShapeDtypeStruct
+    return pl.pallas_call(
+        forward_kernel,
+        grid=(HEADS // 2,),
+        in_specs=[whole(rows, D), whole(live, D)]
+        + weight_specs()
+        + [
+            pl.BlockSpec((1, wide), lambda j: (0, j)),
+            pl.BlockSpec((1, wide), lambda j: (0, 8 + j)),
+            pl.BlockSpec((1, wide), lambda j: (0, 16 + j)),
+            columns(1, 512),
+        ]
+        + [whole(512, 512)]
+        + [whole(rows, wide)] * 3,
+        out_specs=[
+            columns(live, wide),
+            columns(rows, wide),
+            columns(rows, wide),
+            columns(live, wide),
+            columns(live, 512),
+            columns(live, 512),
+            whole(live, D),
+        ],
+        out_shape=[
+            shape((live, D), jnp.bfloat16),
+            shape((rows, D), jnp.bfloat16),
+            shape((rows, D), jnp.bfloat16),
+            shape((live, D), jnp.bfloat16),
+            shape((live, FF), jnp.float32),
+            shape((live, FF), jnp.bfloat16),
+            shape((live, D), jnp.float32),
+        ],
+        compiler_params=pltpu.CompilerParams(vmem_limit_bytes=40 << 20),
+        cost_estimate=pl.CostEstimate(
+            flops=2 * live * 16 * D * D, bytes_accessed=64 * D * D, transcendentals=0
+        ),
+        name="layer_forward",
+    )(attn_in, mlp_in, *[gathered] * 6, bias, bias, bias, pieces[8].reshape(1, FF), regroup_table(), *tables)
+
+
+def layer_backward(grad_low, saved, gathered, tables):
+    query, keys, values, up_val = saved
+    rows, live = keys.shape[0], query.shape[0]
+    wide = 2 * HEAD_DIM
+    shape = jax.ShapeDtypeStruct
+    return pl.pallas_call(
+        backward_kernel,
+        grid=(HEADS // 2,),
+        in_specs=[
+            whole(live, D),
+            columns(live, wide),
+            columns(rows, wide),
+            columns(rows, wide),
+            columns(live, 512),
+        ]
+        + weight_specs()
+        + [whole(512, 512)]
+        + [whole(rows, wide)] * 3,
+        out_specs=[
+            columns(live, wide),
+            columns(rows, wide),
+            columns(rows, wide),
+            columns(live, 512),
+            whole(rows, D),
+            whole(live, D),
+            columns(1, wide),
+            columns(1, wide),
+            columns(1, wide),
+            columns(1, 512),
+        ],
+        out_shape=[
+            shape((live, D), jnp.bfloat16),
+            shape((rows, D), jnp.bfloat16),
+            shape((rows, D), jnp.bfloat16),
+            shape((live, FF), jnp.bfloat16),
+            shape((rows, D), jnp.float32),
+            shape((live, D), jnp.float32),
+            shape((1, D), jnp.float32),
+            shape((1, D), jnp.float32),
+            shape((1, D), jnp.float32),
+            shape((1, FF), jnp.float32),
+        ],
+        compiler_params=pltpu.CompilerParams(vmem_limit_bytes=40 << 20),
+        cost_estimate=pl.CostEstimate(
+            flops=2 * live * 16 * D * D, bytes_accessed=64 * D * D, transcendentals=0
+        ),
+        name="layer_backward",
+    )(grad_low, query, keys, values, up_val, *[gathered] * 6, regroup_table(), *tables)
 
 
 def pro_single(scores, weight, ranks, count):
@@ -410,32 +596,12 @@
     vocab_local = head_table.shape[0]
     pieces = split_params(vector_params)
 
-    everyone = ("cand", *AXES)
-    me = lax.axis_index(everyone)
-    quarter = me // 32
-    down_low = down_weight.reshape(RING, 8, D)
-    moved = []
-    for step in range(RING):
-        group = lax.dynamic_index_in_dim(down_low, (step + quarter) % RING, 0, False)
-        moved.append(
-            lax.ppermute(
-                group.astype(jnp.bfloat16),
-                everyone,
-                [(d, RING * (d % 32) + (step + d // 32) % RING) for d in range(128)],
-            ).astype(jnp.float32)
-        )
-    moved = jnp.stack(moved)
-    down_rows = [
-        lax.dynamic_index_in_dim(moved, (me - k) % RING, 0, False) for k in range(RING)
-    ]
-    packed = jnp.concatenate([qkv_weight, up_weight, proj_weight, *down_rows], axis=1)
-    gathered = lax.all_gather(packed.astype(jnp.bfloat16), everyone, axis=0, tiled=True)
-    mats = (
-        gathered[:, :D],
-        gathered[:, D : 3 * D],
-        gathered[:, 7 * D : 8 * D],
-        gathered[:, 3 * D : 7 * D],
-        [gathered[:, (8 + k) * D : (9 + k) * D] for k in range(RING)],
+    packed = jnp.concatenate(
+        [qkv_weight, up_weight, proj_weight, *[down_weight[8 * k : 8 * k + 8] for k in range(4)]],
+        axis=1,
+    )
+    gathered = lax.all_gather(
+        packed.astype(jnp.bfloat16), ("cand", *AXES), axis=0, tiled=True
     )
 
     live = (
@@ -488,7 +654,15 @@
     all_rewards = both(rewards.reshape(-1), other[4 : 4 + slots])
     weight = jax.nn.softplus((all_rewards - mean) * lax.rsqrt(variance + NORM_EPS))
 
-    hidden, saved = layer_forward(inputs, mats, pieces)
+    live_rows = slots * RESP
+    first_rows = inputs[:live_rows]
+    attn_in = layer_norm(inputs, pieces[0], pieces[1]).astype(jnp.bfloat16)
+    mlp_in = layer_norm(first_rows, pieces[2], pieces[3]).astype(jnp.bfloat16)
+    tables = turn_tables(slots)
+    query, keys, values, mixed, up_val, act, added = layer_forward(
+        attn_in, mlp_in, gathered, pieces, tables
+    )
+    hidden = first_rows + added + (pieces[7] + pieces[9])
     rows_low = layer_norm(hidden, pieces[4], pieces[5]).astype(jnp.bfloat16)
 
     rows_low, mine = lax.optimization_barrier((rows_low, mine))
@@ -549,18 +723,36 @@
     ).astype(jnp.float32)
     head_part = head_part.astype(jnp.bfloat16).reshape(RING, PAD_HALF, D)
     rows_part, head_part = lax.optimization_barrier((rows_part, head_part))
-    head_part = exchange(head_part, "z")
+    head_own = ring_sum(head_part, "z")
     rows_grad = jnp.sum(rows_part.astype(jnp.float32), 0)
 
     grad_hidden, gain_fin_grad, bias_fin_grad = norm_back(hidden, pieces[4], pieces[5], rows_grad)
-    input_grad, mat_grads, vector_head, vector_tail, head_part = layer_backward(
-        inputs, saved, mats, pieces, grad_hidden, head_part
-    )
-    head_own = jnp.sum(head_part.astype(jnp.float32), 0)
+    grad_low = grad_hidden.astype(jnp.bfloat16)
+    grad_sum = jnp.sum(grad_low.astype(jnp.float32), 0)
+    grad_both = of_both(grad_low)
+    down_g = matmul_tn(half_of_both(act), grad_both).astype(jnp.bfloat16).reshape(64, 32, D)
+    down_g = exchange(down_g, AXES)
+    query_grad, key_grad, value_grad, up_grad, attn_grad, mlp_grad, *sums = layer_backward(
+        grad_low, (query, keys, values, up_val), gathered, tables
+    )
+    attn_grad, mlp_grad, down_g = lax.optimization_barrier((attn_grad, mlp_grad, down_g))
+    input_one, gain_one_grad, bias_one_grad = norm_back(inputs, pieces[0], pieces[1], attn_grad)
+    input_two, gain_two_grad, bias_two_grad = norm_back(first_rows, pieces[2], pieces[3], mlp_grad)
+    input_grad = input_one + jnp.pad(grad_hidden + input_two, ((0, live_rows), (0, 0)))
+    attn_both = half_of_both(attn_in)
+    first_both = jnp.concatenate(
+        [attn_both[:live_rows], attn_both[2 * live_rows : 3 * live_rows]], axis=0
+    )
+    up_g = matmul_tn(half_of_both(mlp_in), of_both(up_grad)).astype(jnp.bfloat16)
+    proj_g = matmul_tn(half_of_both(mixed), grad_both).astype(jnp.bfloat16)
+    query_g = matmul_tn(first_both, of_both(query_grad)).astype(jnp.bfloat16)
+    key_g = matmul_tn(attn_both, of_both(key_grad)).astype(jnp.bfloat16)
+    value_g = matmul_tn(attn_both, of_both(value_grad)).astype(jnp.bfloat16)
+    vector_head = [gain_one_grad, bias_one_grad, gain_two_grad, bias_two_grad]
+    vector_tail = [*[part[0] for part in sums[:3]], grad_sum, sums[3][0], grad_sum]
 
     head_grad = both(head_own, swap(head_own))[:vocab_local]
 
-    (query_g, kv_g), proj_g, up_g, down_g = mat_grads
     vector_grad = jnp.concatenate(vector_head + [gain_fin_grad, bias_fin_grad] + vector_tail)
     vector_high = vector_grad.astype(jnp.bfloat16)
     vector_low = (vector_grad - vector_high.astype(jnp.float32)).astype(jnp.bfloat16)
@@ -568,11 +760,7 @@
     vector_both = jnp.pad(vector_both, ((0, 0), (0, 4), (0, slots * SEQ - 120)))
     turned_grad = input_grad.astype(jnp.bfloat16).T.reshape(64, 16, slots * SEQ)
     turned_grad = jnp.concatenate([turned_grad, vector_both], axis=1)
-    rest = jnp.concatenate([up_g, proj_g, query_g, kv_g], axis=1).reshape(64, 8, 8 * D)
-    down_g = down_g.reshape(64, 32, D)
-    down_g, head_own = lax.optimization_barrier((down_g, head_own))
-    down_g = exchange(down_g, AXES)
-    turned_grad, down_g, rest = lax.optimization_barrier((turned_grad, down_g, rest))
+    rest = jnp.concatenate([up_g, proj_g, query_g, key_g, value_g], axis=1).reshape(64, 8, 8 * D)
     turned_grad = exchange(turned_grad, AXES)
     embed_rows = turned_grad[:, :16].astype(jnp.float32).swapaxes(0, 1).reshape(16, -1)
     vector_both = jnp.sum(turned_grad[:, 16:20, :120].astype(jnp.float32), 0).reshape(2, 2, 120)
@@ -583,6 +771,7 @@
 
     rest, embed_rows = lax.optimization_barrier((rest, embed_rows))
     rest = exchange(rest, AXES)
+    embed_rows, head_own = lax.optimization_barrier((embed_rows, head_own))
     embed_grad = fold(embed_rows, flat_ids, embed_table.shape[0])
     embed_grad = (embed_grad + swap(embed_grad)).T
     rest = jnp.sum(rest.astype(jnp.float32), 0)

time: 771 us -> 768 us (level)
  waiting for transfers between devices: 174 us -> 261 us
  matrix products: 141 us -> 75.8 us
  Pallas kernels: 64.2 us -> 104 us
  starting transfers between devices: 104 us -> 84.3 us
  other arithmetic: 117 us -> 98.2 us
  blocking collectives: 68 us -> 53.1 us
  local copies, waits for them, and re-layouts: 63.7 us -> 52.3 us
    ppermute x4 -> x3, waiting for transfers between devices: 0.01 us -> 130 us  [shift(): lax.ppermute(value, axis, [(i, (i + step) % RING) for i in range(RING)])]
    all_to_all x9 -> x8, waiting for transfers between devices: 155 us -> 104 us  [exchange(): return lax.all_to_all(pieces, axes, split_axis=0, concat_axis=0, tiled=True)]
    pallas_call x0 -> x2, Pallas kernels: none -> 40.1 us  [the longest x1 22.7 us: layer_backward(): pl.pallas_call(backward_kernel, grid=(HEADS // 2,), in_specs=[whole(live,...]
    dot_general x9 -> x1, matrix products: 45.5 us -> 19.4 us  [matmul_nt(): lax.dot_general(left, right, (((1,), (1,)), ((), ())), preferred_element_...]
    dot_general x9 -> x1, matrix products: 41.1 us -> 15.4 us  [matmul(): return jnp.dot(left, right, preferred_element_type=jnp.float32)]
    all_to_all x3, blocking collectives: 68 us -> 53.1 us  [exchange(): return lax.all_to_all(pieces, axes, split_axis=0, concat_axis=0, tiled=True)]
    ppermute x4 -> x3, starting transfers between devices: 18.9 us -> 4.21 us  [shift(): lax.ppermute(value, axis, [(i, (i + step) % RING) for i in range(RING)])]
    all_gather x1, waiting for transfers between devices: 5.73 us -> 18.2 us  [body(): lax.all_gather(packed.astype(jnp.bfloat16), ('cand', *AXES), axis=0, tile...]
  transfers between devices with their start and end apart: 26 -> 28, of which waited for: 14 -> 14; matrix products, arithmetic and copies ran while one was open for 25% -> 15% of each run, Pallas kernels for 8% -> 14%
where the time goes in v3:
time: 768 us; the launch traced here: 758 us
  waiting for transfers between devices  261 us (34%)
  Pallas kernels  104 us (14%)
  other arithmetic  98.2 us (13%)
  starting transfers between devices  84.3 us (11%)
  matrix products  75.8 us (10%)
  blocking collectives  53.1 us (7%)
  local copies, waits for them, and re-layouts  52.3 us (7%)
  between operations  28.9 us (4%)
    ppermute x3, waiting for transfers between devices, shift(): lax.ppermute(value, axis, [(i, (i + step) % RING) for i in range(RING)])  130 us
    all_to_all x8, waiting for transfers between devices, exchange(): return lax.all_to_all(pieces, axes, split_axis=0, concat_axis=0, tiled=True)  104 us
    all_to_all x8, starting transfers between devices, exchange(): return lax.all_to_all(pieces, axes, split_axis=0, concat_axis=0, tiled=True)  66.7 us
    all_to_all x3, blocking collectives, exchange(): return lax.all_to_all(pieces, axes, split_axis=0, concat_axis=0, tiled=True)  53.1 us
    dot_general x8, matrix products, matmul_tn(): lax.dot_general(left, right, (((0,), (0,)), ((), ())), preferred_element_...  40.9 us
    pallas_call x1, Pallas kernels, fold(): pl.pallas_call(fold_kernel, grid=(count // FOLD_BLOCK,), in_specs=[row, r...  39.9 us
    pallas_call x1, Pallas kernels, look_up(): pl.pallas_call(look_kernel, grid=(count // LOOK_BLOCK,), in_specs=[row, r...  24.2 us
    pallas_call x1, Pallas kernels, layer_backward(): pl.pallas_call(backward_kernel, grid=(HEADS // 2,), in_specs=[whole(live,...  22.7 us
  transfers between devices with their start and end apart: 28, of which 14 were waited for; matrix products, arithmetic and copies ran while one was open for 15% of the time, Pallas kernels for 14%

profile of v3, /device:TPU:1, one launch (start us, length us, event | category | flops | bytes accessed | tf_op | source)
XLA Modules:
  0.0 757.9 jit_solution(4402775226204355203)
XLA Ops:
  19.7 20.3 %all_to_all.60 = f32[64,1,256]{2,1,0:T(1,128)S(1)} all-to-all(f32[64,1,256]{2,1,0:T(1,128)S(1)} %broadcast_in_dim.82), channel_id=1, replica_groups=mesh['cand'=2,'x'=4,'y'=4,'z'=4] {'x','y','z'}, dimensions={0} | all-to-all | bytes 131072 | tf_op jit(solution)/shard_map/all_to_all | solution.py:42
  42.8 24.2 %look_up.1 = f32[16,12288]{1,0:T(8,128)S(1)} custom-call(s32[1,12288]{1,0:T(1,128)S(1)} %and_select_fusion.1.high_ref, s32[1,12288]{1,0:T(1,128)S(1)} %get-tuple-element.146.low_ref, f32[16,50304]{1,0:T(8,128)S(1)} %bitcast.111), custom_call_target="tpu_custom_call" | custom-call | flops 19830669312 | bytes 3219456 | tf_op jit(solution)/shard_map/look_up/pallas_call | solution.py:123
  77.3 13.7 %all-to-all-done.1 = bf16[64,16,192]{2,1,0:T(8,128)(2,1)S(1)} async-done(((bf16[64,16,192]{2,1,0:T(8,128)(2,1)}), bf16[64,16,192]{2,1,0:T(8,128)(2,1)S(1)}, u32[]{:S(2)}, u32[]{:S(2)}) %all-to-all-start.1) | async-done | bytes 393248 | tf_op jit(solution)/shard_map/all_to_all | solution.py:42
  101.7 18.2 %all-gather.2.cloned.1.call-done.query_w.key_w.value_w.proj_w.up_w.down_w = bf16[1024,12288]{1,0:T(8,128)(2,1)} async-done(((bf16[8,12288]{1,0:T(8,128)(2,1)}), bf16[1024,12288]{1,0:T(8,128)(2,1)}) %all-gather.2.cloned.1.call-update) | async-done | bytes 25165840 | tf_op jit(solution)/shard_map/all_gather | solution.py:603
  119.9 17.4 %layer_forward.1 = (bf16[96,1024]{1,0:T(8,128)(2,1)S(1)}, bf16[192,1024]{1,0:T(8,128)(2,1)S(1)}, bf16[192,1024]{1,0:T(8,128)(2,1)S(1)}, bf16[96,1024]{1,0:T(8,12...) custom-call(bf16[192,1024]{1,0:T(8,128)(2,1)S(1)} %add_convert_fusion.2.attn_ref, ...), custom_call_target="tpu_custom_call" | custom-call | flops 3221225472 | bytes 67108864 | tf_op jit(solution)/shard_map/layer_forward/pallas_call | solution.py:445
  172.6 30.2 %all-to-all-done.3 = bf16[16,96,1024]{2,1,0:T(8,128)(2,1)} async-done(((bf16[16,96,1024]{2,1,0:T(8,128)(2,1)}), bf16[16,96,1024]{2,1,0:T(8,128)(2,1)}, u32[]{:S(2)}, u32[]{:S(2)}) %all-to-all-start.3) | async-done | bytes 3145760 | tf_op jit(solution)/shard_map/all_to_all | solution.py:42
  202.8 19.4 %fusion.113 = (f32[1536]{0:T(1024)S(1)}, f32[1536,3584]{1,0:T(8,128)}) fusion(bf16[1536,1024]{1,0:T(8,128)(2,1)} %bitcast.21, bf16[3584,1024]{1,0:T(8,128)(2,1)} %constant_dynamic-update-slice_fusion.6, pred[3584]{0:T(1024)(128)(4,1)S(1)} %fusion.51), kind=kOutput, calls=%fused_computation.306 | convolution fusion | flops 11285297152 | bytes 32515584 | tf_op jit(solution)/shard_map/dot_general | solution.py:218
  222.2 10.7 %exponential_reduce_fusion = (f32[1536]{0:T(1024)S(1)}, f32[1536]{0:T(1024)S(1)}) fusion(f32[1536,3584]{1,0:T(8,128)} %get-tuple-element.188, f32[1536]{0:T(1024)S(1)} %get-tuple-element.187, s32[1536]{0:T(1024)S(1)} %fusion.60), kind=kLoop, calls=%fused_computation.3 | loop fusion | flops 27522048 | bytes 22044672 | tf_op jit(solution)/shard_map/reduce_sum | solution.py:685
  233.7 11.4 %all-to-all-start.4 = ((f32[16,3,96]{2,1,0:T(4,128)}), f32[16,3,96]{2,1,0:T(4,128)S(1)}, u32[]{:S(2)}, u32[]{:S(2)}) async-start(f32[16,3,96]{2,1,0:T(4,128)} %copy.110), calls=%async_computation.4 | async-start | bytes 65536 | tf_op jit(solution)/shard_map/all_to_all | solution.py:42
  272.4 11.7 %multiply_convert_fusion = bf16[1536,3584]{1,0:T(8,128)(2,1)S(1)} fusion(f32[1536,3584]{1,0:T(8,128)} %get-tuple-element.188, f32[1536]{0:T(1024)S(1)} %sub.191, f32[1536]{0:T(1024)S(1)} %mul.644, s32[1536]{0:T(1024)S(1)} %fusion.60), kind=kLoop, calls=%fused_computation | loop fusion | flops 33030144 | bytes 33048576 | tf_op jit(solution)/shard_map/convert_element_type | solution.py:715
  284.1 11.7 %fusion.5 = bf16[1792,1024]{1,0:T(8,128)(2,1)} fusion(bf16[1536,1024]{1,0:T(8,128)(2,1)} %bitcast.21, bf16[1536,3584]{1,0:T(8,128)(2,1)S(1)} %multiply_convert_fusion), kind=kOutput, calls=%fused_computation.19 | convolution fusion | flops 5638979584 | bytes 12320768 | tf_op jit(solution)/shard_map/dot_general | solution.py:212
  297.6 15.4 %convolution_convert_fusion.1 = bf16[1536,1024]{1,0:T(8,128)(2,1)} fusion(bf16[1536,3584]{1,0:T(8,128)(2,1)S(1)} %multiply_convert_fusion, bf16[3584,1024]{1,0:T(8,128)(2,1)} %constant_dynamic-update-slice_fusion.6), kind=kOutput, calls=%fused_computation.18 | convolution fusion | flops 11275862016 | bytes 21495808 | tf_op jit(solution)/shard_map/dot_general | solution.py:208
  319.7 10.7 %add_convert_fusion = bf16[1792,1024]{1,0:T(8,128)(2,1)} fusion(bf16[1792,1024]{1,0:T(8,128)(2,1)} %collective-permute-done.4, bf16[1536,1024]{1,0:T(8,128)(2,1)} %bitcast.21, bf16[1536,3584]{1,0:T(8,128)(2,1)} %copy-done.27), kind=kOutput, calls=%fused_computation.9 | convolution fusion | flops 5642649600 | bytes 15990784 | tf_op jit(solution)/shard_map/dot_general | solution.py:212
  330.4 29.8 %all-to-all-done.6 = bf16[16,96,1024]{2,1,0:T(8,128)(2,1)} async-done(((bf16[16,96,1024]{2,1,0:T(8,128)(2,1)}), bf16[16,96,1024]{2,1,0:T(8,128)(2,1)}, u32[]{:S(2)}, u32[]{:S(2)}) %all-to-all-start.6) | async-done | bytes 3145760 | tf_op jit(solution)/shard_map/all_to_all | solution.py:42
  370.7 11.7 %all-to-all-start.7 = ((bf16[64,32,1024]{2,1,0:T(8,128)(2,1)}), bf16[64,32,1024]{2,1,0:T(8,128)(2,1)}, u32[]{:S(2)}, u32[]{:S(2)}) async-start(bf16[64,32,1024]{2,1,0:T(8,128)(2,1)} %bitcast.127), calls=%async_computation.7 | async-start | bytes 8388608 | tf_op jit(solution)/shard_map/all_to_all | solution.py:42
  392.0 22.7 %layer_backward.1 = (bf16[96,1024]{1,0:T(8,128)(2,1)}, bf16[192,1024]{1,0:T(8,128)(2,1)}, bf16[192,1024]{1,0:T(8,128)(2,1)S(1)}, bf16[96,4096]{1,0:T(8,128)(2,1)...) custom-call(bf16[96,1024]{1,0:T(8,128)(2,1)S(1)} %get-tuple-element., ...), custom_call_target="tpu_custom_call" | custom-call | flops 3221225472 | bytes 67108864 | tf_op jit(solution)/shard_map/layer_backward/pallas_call | solution.py:489
  416.2 19.3 %all-to-all-done.7 = bf16[64,32,1024]{2,1,0:T(8,128)(2,1)} async-done(((bf16[64,32,1024]{2,1,0:T(8,128)(2,1)}), bf16[64,32,1024]{2,1,0:T(8,128)(2,1)}, u32[]{:S(2)}, u32[]{:S(2)}) %all-to-all-start.7) | async-done | bytes 4194336 | tf_op jit(solution)/shard_map/all_to_all | solution.py:42
  442.5 12.1 %all-to-all-start.8 = ((bf16[64,24,192]{2,1,0:T(8,128)(2,1)}), bf16[64,24,192]{2,1,0:T(8,128)(2,1)S(1)}, u32[]{:S(2)}, u32[]{:S(2)}) async-start(bf16[64,24,192]{2,1,0:T(8,128)(2,1)} %fusion.23), calls=%async_computation.8 | async-start | bytes 1572864 | tf_op jit(solution)/shard_map/all_to_all | solution.py:42
  474.0 10.3 %all-to-all-start.9 = ((bf16[64,8,8192]{2,1,0:T(8,128)(2,1)}), bf16[64,8,8192]{2,1,0:T(8,128)(2,1)}, u32[]{:S(2)}, u32[]{:S(2)}) async-start(bf16[64,8,8192]{2,1,0:T(8,128)(2,1)} %bitcast.31), calls=%async_computation.9 | async-start | bytes 16777216 | tf_op jit(solution)/shard_map/all_to_all | solution.py:42
  490.6 92.9 %collective-permute-done.16 = bf16[448,1024]{1,0:T(8,128)(2,1)} collective-permute-done((bf16[448,1024]{1,0:T(8,128)(2,1)S(1)}, bf16[448,1024]{1,0:T(8,128)(2,1)}, u32[]{:S(2)}, u32[]{:S(2)}) %collective-permute-start.16) | collective-permute-done | bytes 917536 | tf_op jit(solution)/shard_map/ppermute | solution.py:51
  583.5 12.8 %collective-permute-done.15 = bf16[448,1024]{1,0:T(8,128)(2,1)} collective-permute-done((bf16[448,1024]{1,0:T(8,128)(2,1)S(1)}, bf16[448,1024]{1,0:T(8,128)(2,1)}, u32[]{:S(2)}, u32[]{:S(2)}) %collective-permute-start.15) | collective-permute-done | bytes 917536 | tf_op jit(solution)/shard_map/ppermute | solution.py:51
  596.4 24.1 %collective-permute-done.14 = bf16[448,1024]{1,0:T(8,128)(2,1)} collective-permute-done((bf16[448,1024]{1,0:T(8,128)(2,1)S(1)}, bf16[448,1024]{1,0:T(8,128)(2,1)}, u32[]{:S(2)}, u32[]{:S(2)}) %collective-permute-start.14) | collective-permute-done | bytes 917536 | tf_op jit(solution)/shard_map/ppermute | solution.py:51
  625.5 39.9 %fold.1 = f32[16,50304]{1,0:T(8,128)S(1)} custom-call(s32[1,12288]{1,0:T(1,128)S(1)} %copy-done.20, s32[1,12288]{1,0:T(1,128)S(1)} %copy-done.18, f32[16,12288]{1,0:T(8,128)S(1)} %copy-done.3), custom_call_target="tpu_custom_call" | custom-call | flops 19830669312 | bytes 3219456 | tf_op jit(solution)/shard_map/fold/pallas_call | solution.py:191
  701.4 22.8 %all_to_all.62 = f32[128,1,3]{2,1,0:T(1,128)S(1)} all-to-all(f32[128,1,3]{2,1,0:T(1,128)S(1)} %broadcast_in_dim.167), channel_id=1, replica_groups=mesh['cand'=2,'x'=4,'y'=4,'z'=4] {'cand','x','y','z'}, dimensions={0} | all-to-all | bytes 3072 | tf_op jit(solution)/shard_map/all_to_all | solution.py:42
  (351 shorter events, 215.5 us)
Async XLA Ops:
  7.2 112.6 %all-gather.2.cloned.1.call-start = ((), (), s32[]{:S(2)}) async-start(), calls=%async_computation.11 | async-start | bytes 25362432 | tf_op jit(solution)/shard_map/all_gather | solution.py:603
  68.9 22.1 %all-to-all-start.1 = ((bf16[64,16,192]{2,1,0:T(8,128)(2,1)}), bf16[64,16,192]{2,1,0:T(8,128)(2,1)S(1)}, u32[]{:S(2)}, u32[]{:S(2)}) async-start(bf16[64,16,192]{2,1,0:T(8,128)(2,1)} %bitcast.102), calls=%async_computation.1 | async-start | bytes 1048576 | tf_op jit(solution)/shard_map/all_to_all | solution.py:42
  95.5 54.3 %all-to-all-start.2 = ((bf16[4,448,1024]{2,1,0:T(8,128)(2,1)}), bf16[4,448,1024]{2,1,0:T(8,128)(2,1)}, u32[]{:S(2)}, u32[]{:S(2)}) async-start(bf16[4,448,1024]{2,1,0:T(8,128)(2,1)} %broadcast_in_dim.86), calls=%async_computation.2 | async-start | bytes 7340032 | tf_op jit(solution)/shard_map/all_to_all | solution.py:42
  149.8 18.5 %collective-permute-start.2 = (bf16[1792,1024]{1,0:T(8,128)(2,1)}, bf16[1792,1024]{1,0:T(8,128)(2,1)}, u32[]{:S(2)}, u32[]{:S(2)}) collective-permute-start(bf16[1792,1024]{1,0:T(8,128)(2,1)} %bitcast.20), channel_id=1, source_target_pairs={{0,64},{64,0},{1,65},{65,1},{2,66},{66,2},{3,67},{67,3},{4,68},{68... | collective-permute-start | bytes 11010056 | tf_op jit(solution)/shard_map/ppermute | solution.py:38
  154.3 48.5 %all-to-all-start.3 = ((bf16[16,96,1024]{2,1,0:T(8,128)(2,1)}), bf16[16,96,1024]{2,1,0:T(8,128)(2,1)}, u32[]{:S(2)}, u32[]{:S(2)}) async-start(bf16[16,96,1024]{2,1,0:T(8,128)(2,1)} %broadcast_in_dim.87), calls=%async_computation.3 | async-start | bytes 6291456 | tf_op jit(solution)/shard_map/all_to_all | solution.py:42
  233.7 17.9 %all-to-all-start.4 = ((f32[16,3,96]{2,1,0:T(4,128)}), f32[16,3,96]{2,1,0:T(4,128)S(1)}, u32[]{:S(2)}, u32[]{:S(2)}) async-start(f32[16,3,96]{2,1,0:T(4,128)} %copy.110), calls=%async_computation.4 | async-start | bytes 65536 | tf_op jit(solution)/shard_map/all_to_all | solution.py:42
  252.5 3.4 collective-permute-start.3
  295.8 23.9 %collective-permute-start.4 = (bf16[1792,1024]{1,0:T(8,128)(2,1)}, bf16[1792,1024]{1,0:T(8,128)(2,1)}, u32[]{:S(2)}, u32[]{:S(2)}) collective-permute-start(bf16[1792,1024]{1,0:T(8,128)(2,1)} %fusion.5), channel_id=1, source_target_pairs={{0,64},{64,0},{1,65},{65,1},{2,66},{66,2},{3,67},{67,3},{4,68},{68... | collective-permute-start | bytes 11010056 | tf_op jit(solution)/shard_map/ppermute | solution.py:38
  313.0 47.2 %all-to-all-start.6 = ((bf16[16,96,1024]{2,1,0:T(8,128)(2,1)}), bf16[16,96,1024]{2,1,0:T(8,128)(2,1)}, u32[]{:S(2)}, u32[]{:S(2)}) async-start(bf16[16,96,1024]{2,1,0:T(8,128)(2,1)} %bitcast.130), calls=%async_computation.6 | async-start | bytes 6291456 | tf_op jit(solution)/shard_map/all_to_all | solution.py:42
  319.6 45.8 %collective-permute-start.12 = (bf16[96,2048]{1,0:T(8,128)(2,1)}, bf16[96,2048]{1,0:T(8,128)(2,1)}, u32[]{:S(2)}, u32[]{:S(2)}) collective-permute-start(bf16[96,2048]{1,0:T(8,128)(2,1)} %get-tuple-element.154), channel_id=1, source_target_pairs={{0,64},{64,0},{1,65},{65,1},{2,66},{66,2},{3,67},{67,3},{4,68},{68... | collective-permute-start | bytes 1179656 | tf_op jit(solution)/shard_map/ppermute | solution.py:38
  370.7 64.7 %all-to-all-start.7 = ((bf16[64,32,1024]{2,1,0:T(8,128)(2,1)}), bf16[64,32,1024]{2,1,0:T(8,128)(2,1)}, u32[]{:S(2)}, u32[]{:S(2)}) async-start(bf16[64,32,1024]{2,1,0:T(8,128)(2,1)} %bitcast.127), calls=%async_computation.7 | async-start | bytes 8388608 | tf_op jit(solution)/shard_map/all_to_all | solution.py:42
  384.5 70.1 %collective-permute-start = (bf16[96,512]{1,0:T(8,128)(2,1)}, bf16[96,512]{1,0:T(8,128)(2,1)}, u32[]{:S(2)}, u32[]{:S(2)}) collective-permute-start(bf16[96,512]{1,0:T(8,128)(2,1)} %get-tuple-element.160), channel_id=1, source_target_pairs={{0,64},{64,0},{1,65},{65,1},{2,66},{66,2},{3,67},{67,3},{4,68},{68... | collective-permute-start | bytes 294920 | tf_op jit(solution)/shard_map/ppermute | solution.py:38
  385.8 75.7 %collective-permute-start.6 = (bf16[96,512]{1,0:T(8,128)(2,1)}, bf16[96,512]{1,0:T(8,128)(2,1)}, u32[]{:S(2)}, u32[]{:S(2)}) collective-permute-start(bf16[96,512]{1,0:T(8,128)(2,1)} %get-tuple-element.158), channel_id=1, source_target_pairs={{0,64},{64,0},{1,65},{65,1},{2,66},{66,2},{3,67},{67,3},{4,68},{68... | collective-permute-start | bytes 294920 | tf_op jit(solution)/shard_map/ppermute | solution.py:38
  415.4 41.3 %collective-permute-start.5 = (bf16[96,4096]{1,0:T(8,128)(2,1)}, bf16[96,4096]{1,0:T(8,128)(2,1)}, u32[]{:S(2)}, u32[]{:S(2)}) collective-permute-start(bf16[96,4096]{1,0:T(8,128)(2,1)} %get-tuple-element.62), channel_id=1, source_target_pairs={{0,64},{64,0},{1,65},{65,1},{2,66},{66,2},{3,67},{67,3},{4,68},{68... | collective-permute-start | bytes 2359304 | tf_op jit(solution)/shard_map/ppermute | solution.py:38
  415.5 48.5 %collective-permute-start.9 = (bf16[96,1024]{1,0:T(8,128)(2,1)}, bf16[96,1024]{1,0:T(8,128)(2,1)}, u32[]{:S(2)}, u32[]{:S(2)}) collective-permute-start(bf16[96,1024]{1,0:T(8,128)(2,1)} %get-tuple-element.64), channel_id=1, source_target_pairs={{0,64},{64,0},{1,65},{65,1},{2,66},{66,2},{3,67},{67,3},{4,68},{68... | collective-permute-start | bytes 589832 | tf_op jit(solution)/shard_map/ppermute | solution.py:38
  416.0 50.5 %collective-permute-start.10 = (bf16[192,1024]{1,0:T(8,128)(2,1)}, bf16[192,1024]{1,0:T(8,128)(2,1)}, u32[]{:S(2)}, u32[]{:S(2)}) collective-permute-start(bf16[192,1024]{1,0:T(8,128)(2,1)} %get-tuple-element.65), channel_id=1, source_target_pairs={{0,64},{64,0},{1,65},{65,1},{2,66},{66,2},{3,67},{67,3},{4,68},{68... | collective-permute-start | bytes 1179656 | tf_op jit(solution)/shard_map/ppermute | solution.py:38
  442.5 28.6 %all-to-all-start.8 = ((bf16[64,24,192]{2,1,0:T(8,128)(2,1)}), bf16[64,24,192]{2,1,0:T(8,128)(2,1)S(1)}, u32[]{:S(2)}, u32[]{:S(2)}) async-start(bf16[64,24,192]{2,1,0:T(8,128)(2,1)} %fusion.23), calls=%async_computation.8 | async-start | bytes 1572864 | tf_op jit(solution)/shard_map/all_to_all | solution.py:42
  454.6 14.7 %collective-permute-start.11 = (bf16[192,1024]{1,0:T(8,128)(2,1)S(1)}, bf16[192,1024]{1,0:T(8,128)(2,1)S(1)}, u32[]{:S(2)}, u32[]{:S(2)}) collective-permute-start(bf16[192,1024]{1,0:T(8,128)(2,1)S(1)} %copy-done.22), channel_id=1, source_target_pairs={{0,64},{64,0},{1,65},{65,1},{2,66},{66,2},{3,67},{67,3},{4,68},{68... | collective-permute-start | bytes 1179656 | tf_op jit(solution)/shard_map/ppermute | solution.py:38
  474.0 217.4 %all-to-all-start.9 = ((bf16[64,8,8192]{2,1,0:T(8,128)(2,1)}), bf16[64,8,8192]{2,1,0:T(8,128)(2,1)}, u32[]{:S(2)}, u32[]{:S(2)}) async-start(bf16[64,8,8192]{2,1,0:T(8,128)(2,1)} %bitcast.31), calls=%async_computation.9 | async-start | bytes 16777216 | tf_op jit(solution)/shard_map/all_to_all | solution.py:42
  486.4 97.1 %collective-permute-start.16 = (bf16[448,1024]{1,0:T(8,128)(2,1)S(1)}, bf16[448,1024]{1,0:T(8,128)(2,1)}, u32[]{:S(2)}, u32[]{:S(2)}) collective-permute-start(bf16[448,1024]{1,0:T(8,128)(2,1)S(1)} %get-tuple-element.151), channel_id=1, source_target_pairs={{0,3},{1,0},{2,1},{3,2},{4,7},{5,4},{6,5},{7,6},{8,11},{9,8},{10,9... | collective-permute-start | bytes 2752520 | tf_op jit(solution)/shard_map/ppermute | solution.py:51
  488.6 107.7 %collective-permute-start.15 = (bf16[448,1024]{1,0:T(8,128)(2,1)S(1)}, bf16[448,1024]{1,0:T(8,128)(2,1)}, u32[]{:S(2)}, u32[]{:S(2)}) collective-permute-start(bf16[448,1024]{1,0:T(8,128)(2,1)S(1)} %get-tuple-element.152), channel_id=1, source_target_pairs={{0,1},{1,2},{2,3},{3,0},{4,5},{5,6},{6,7},{7,4},{8,9},{9,10},{10,1... | collective-permute-start | bytes 2752520 | tf_op jit(solution)/shard_map/ppermute | solution.py:51
  488.6 131.8 %collective-permute-start.14 = (bf16[448,1024]{1,0:T(8,128)(2,1)S(1)}, bf16[448,1024]{1,0:T(8,128)(2,1)}, u32[]{:S(2)}, u32[]{:S(2)}) collective-permute-start(bf16[448,1024]{1,0:T(8,128)(2,1)S(1)} %get-tuple-element.150), channel_id=1, source_target_pairs={{0,2},{1,3},{2,0},{3,1},{4,6},{5,7},{6,4},{7,5},{8,10},{9,11},{10,... | collective-permute-start | bytes 2752520 | tf_op jit(solution)/shard_map/ppermute | solution.py:51
  665.5 19.8 %collective-permute-start.17 = (f32[16,50304]{1,0:T(8,128)S(1)}, f32[16,50304]{1,0:T(8,128)}, u32[]{:S(2)}, u32[]{:S(2)}) collective-permute-start(f32[16,50304]{1,0:T(8,128)S(1)} %fold.1), channel_id=1, source_target_pairs={{0,64},{64,0},{1,65},{65,1},{2,66},{66,2},{3,67},{67,3},{4,68},{68... | collective-permute-start | bytes 9658376 | tf_op jit(solution)/shard_map/ppermute | solution.py:38
  666.7 8.2 %collective-permute-start.18 = (f32[448,1024]{1,0:T(8,128)}, f32[448,1024]{1,0:T(8,128)}, u32[]{:S(2)}, u32[]{:S(2)}) collective-permute-start(f32[448,1024]{1,0:T(8,128)} %fusion.14), channel_id=1, source_target_pairs={{0,64},{64,0},{1,65},{65,1},{2,66},{66,2},{3,67},{67,3},{4,68},{68... | collective-permute-start | bytes 5505032 | tf_op jit(solution)/shard_map/ppermute | solution.py:38
  (71 other events, 1248.5 us)
Sparse Core Ops, SparseCore 0:
  11.7 108.0 all-gather.1

commit v4 on v3

--- a/solution.py
+++ b/solution.py
@@ -716,6 +716,7 @@
         jnp.bfloat16
     )
     rows_part = matmul(logit_grad, head_group).astype(jnp.bfloat16)
+    rows_part, logit_grad = lax.optimization_barrier((rows_part, logit_grad))
     rows_part = exchange(rows_part.reshape(16, rows_own, D), ("x", "y"))
     near = RING * PAD_HALF
     head_part = matmul_tn(logit_grad[:, :near], group_rows) + swap(
@@ -769,9 +770,8 @@
         lax.dynamic_index_in_dim(vector_both, 1 - core, 0, False)
     )
 
-    rest, embed_rows = lax.optimization_barrier((rest, embed_rows))
+    rest, embed_rows, head_own = lax.optimization_barrier((rest, embed_rows, head_own))
     rest = exchange(rest, AXES)
-    embed_rows, head_own = lax.optimization_barrier((embed_rows, head_own))
     embed_grad = fold(embed_rows, flat_ids, embed_table.shape[0])
     embed_grad = (embed_grad + swap(embed_grad)).T
     rest = jnp.sum(rest.astype(jnp.float32), 0)

time: 768 us -> 698 us (0.909)
  waiting for transfers between devices: 261 us -> 169 us
  local copies, waits for them, and re-layouts: 52.3 us -> 62.8 us
  other arithmetic: 98.2 us -> 106 us
    ppermute x3, waiting for transfers between devices: 130 us -> 27.1 us  [shift(): lax.ppermute(value, axis, [(i, (i + step) % RING) for i in range(RING)])]
    all_to_all x8, waiting for transfers between devices: 104 us -> 124 us  [exchange(): return lax.all_to_all(pieces, axes, split_axis=0, concat_axis=0, tiled=True)]
    all_gather x1, waiting for transfers between devices: 18.2 us -> 6.81 us  [body(): lax.all_gather(packed.astype(jnp.bfloat16), ('cand', *AXES), axis=0, tile...]
    unnamed x149 -> x187, local copies, waits for them, and re-layouts: 20.7 us -> 27.8 us
  transfers between devices with their start and end apart: 28 -> 28, of which waited for: 14 -> 15; matrix products, arithmetic and copies ran while one was open for 15% -> 15% of each run, Pallas kernels for 14% -> 15%
where the time goes in v4:
time: 698 us; the launch traced here: 687 us
  waiting for transfers between devices  169 us (24%)
  other arithmetic  106 us (15%)
  Pallas kernels  104 us (15%)
  starting transfers between devices  82.7 us (12%)
  matrix products  75.1 us (11%)
  local copies, waits for them, and re-layouts  62.8 us (9%)
  blocking collectives  57.8 us (8%)
  between operations  28.9 us (4%)
    all_to_all x8, waiting for transfers between devices, exchange(): return lax.all_to_all(pieces, axes, split_axis=0, concat_axis=0, tiled=True)  124 us
    all_to_all x8, starting transfers between devices, exchange(): return lax.all_to_all(pieces, axes, split_axis=0, concat_axis=0, tiled=True)  65.5 us
    all_to_all x3, blocking collectives, exchange(): return lax.all_to_all(pieces, axes, split_axis=0, concat_axis=0, tiled=True)  57.8 us
    pallas_call x1, Pallas kernels, fold(): pl.pallas_call(fold_kernel, grid=(count // FOLD_BLOCK,), in_specs=[row, r...  39.9 us
    dot_general x8, matrix products, matmul_tn(): lax.dot_general(left, right, (((0,), (0,)), ((), ())), preferred_element_...  37.5 us
    unnamed x187, local copies, waits for them, and re-layouts  27.8 us
    ppermute x3, waiting for transfers between devices, shift(): lax.ppermute(value, axis, [(i, (i + step) % RING) for i in range(RING)])  27.1 us
    pallas_call x1, Pallas kernels, look_up(): pl.pallas_call(look_kernel, grid=(count // LOOK_BLOCK,), in_specs=[row, r...  24.2 us
  transfers between devices with their start and end apart: 28, of which 15 were waited for; matrix products, arithmetic and copies ran while one was open for 15% of the time, Pallas kernels for 15%

profile of v4, /device:TPU:1, one launch (start us, length us, event | category | flops | bytes accessed | tf_op | source)
XLA Modules:
  0.0 686.9 jit_solution(6700349639604283373)
XLA Ops:
  20.2 20.3 %all_to_all.60 = f32[64,1,256]{2,1,0:T(1,128)S(1)} all-to-all(f32[64,1,256]{2,1,0:T(1,128)S(1)} %broadcast_in_dim.82), channel_id=1, replica_groups=mesh['cand'=2,'x'=4,'y'=4,'z'=4] {'x','y','z'}, dimensions={0} | all-to-all | bytes 131072 | tf_op jit(solution)/shard_map/all_to_all | solution.py:42
  44.0 24.2 %look_up.1 = f32[16,12288]{1,0:T(8,128)S(1)} custom-call(s32[1,12288]{1,0:T(1,128)S(1)} %and_select_fusion.1.high_ref, s32[1,12288]{1,0:T(1,128)S(1)} %get-tuple-element.148.low_ref, f32[16,50304]{1,0:T(8,128)S(1)} %bitcast.111), custom_call_target="tpu_custom_call" | custom-call | flops 19830669312 | bytes 3219456 | tf_op jit(solution)/shard_map/look_up/pallas_call | solution.py:123
  83.5 14.1 %all-to-all-done.1 = bf16[64,16,192]{2,1,0:T(8,128)(2,1)} async-done(((bf16[64,16,192]{2,1,0:T(8,128)(2,1)}), bf16[64,16,192]{2,1,0:T(8,128)(2,1)}, u32[]{:S(2)}, u32[]{:S(2)}) %all-to-all-start.1) | async-done | bytes 393248 | tf_op jit(solution)/shard_map/all_to_all | solution.py:42
  117.2 17.4 %layer_forward.1 = (bf16[96,1024]{1,0:T(8,128)(2,1)S(1)}, bf16[192,1024]{1,0:T(8,128)(2,1)S(1)}, bf16[192,1024]{1,0:T(8,128)(2,1)S(1)}, bf16[96,1024]{1,0:T(8,12...) custom-call(bf16[192,1024]{1,0:T(8,128)(2,1)S(1)} %add_convert_fusion.2.attn_ref, ...), custom_call_target="tpu_custom_call" | custom-call | flops 3221225472 | bytes 67108864 | tf_op jit(solution)/shard_map/layer_forward/pallas_call | solution.py:445
  138.4 10.1 %all-to-all-done.2 = bf16[4,448,1024]{2,1,0:T(8,128)(2,1)} async-done(((bf16[4,448,1024]{2,1,0:T(8,128)(2,1)}), bf16[4,448,1024]{2,1,0:T(8,128)(2,1)}, u32[]{:S(2)}, u32[]{:S(2)}) %all-to-all-start.2) | async-done | bytes 3670048 | tf_op jit(solution)/shard_map/all_to_all | solution.py:42
  181.0 21.8 %all-to-all-done.3 = bf16[16,96,1024]{2,1,0:T(8,128)(2,1)} async-done(((bf16[16,96,1024]{2,1,0:T(8,128)(2,1)}), bf16[16,96,1024]{2,1,0:T(8,128)(2,1)}, u32[]{:S(2)}, u32[]{:S(2)}) %all-to-all-start.3) | async-done | bytes 3145760 | tf_op jit(solution)/shard_map/all_to_all | solution.py:42
  202.7 19.4 %fusion.113 = (f32[1536]{0:T(1024)S(1)}, f32[1536,3584]{1,0:T(8,128)}) fusion(bf16[1536,1024]{1,0:T(8,128)(2,1)} %bitcast.21, bf16[3584,1024]{1,0:T(8,128)(2,1)} %constant_dynamic-update-slice_fusion.6, pred[3584]{0:T(1024)(128)(4,1)S(1)} %copy-done.73), kind=kOutput, calls=%fused_computation.306 | convolution fusion | flops 11285297152 | bytes 32515584 | tf_op jit(solution)/shard_map/dot_general | solution.py:218
  222.2 10.7 %exponential_reduce_fusion = (f32[1536]{0:T(1024)S(1)}, f32[1536]{0:T(1024)S(1)}) fusion(f32[1536,3584]{1,0:T(8,128)} %get-tuple-element.190, f32[1536]{0:T(1024)S(1)} %get-tuple-element.189, s32[1536]{0:T(1024)S(1)} %fusion.60), kind=kLoop, calls=%fused_computation.3 | loop fusion | flops 27522048 | bytes 22044672 | tf_op jit(solution)/shard_map/reduce_sum | solution.py:685
  233.7 11.5 %all-to-all-start.4 = ((f32[16,3,96]{2,1,0:T(4,128)}), f32[16,3,96]{2,1,0:T(4,128)S(1)}, u32[]{:S(2)}, u32[]{:S(2)}) async-start(f32[16,3,96]{2,1,0:T(4,128)} %copy.110), calls=%async_computation.4 | async-start | bytes 65536 | tf_op jit(solution)/shard_map/all_to_all | solution.py:42
  265.6 10.0 %all_to_all.61 = f32[16,2,96]{2,1,0:T(2,128)S(1)} all-to-all(f32[16,2,96]{2,1,0:T(2,128)S(1)} %broadcast_in_dim.95), channel_id=1, replica_groups=mesh['cand'=2,'x'=4,'y'=4,'z'=4] {'x','y'}, dimensions={0} | all-to-all | bytes 24576 | tf_op jit(solution)/shard_map/all_to_all | solution.py:42
  275.7 11.7 %multiply_convert_fusion = bf16[1536,3584]{1,0:T(8,128)(2,1)S(1)} fusion(f32[1536,3584]{1,0:T(8,128)} %get-tuple-element.190, f32[1536]{0:T(1024)S(1)} %sub.191, f32[1536]{0:T(1024)S(1)} %mul.644, s32[1536]{0:T(1024)S(1)} %fusion.60), kind=kLoop, calls=%fused_computation | loop fusion | flops 33030144 | bytes 33048576 | tf_op jit(solution)/shard_map/convert_element_type | solution.py:715
  287.4 18.2 %convolution_convert_fusion.1 = bf16[1536,1024]{1,0:T(8,128)(2,1)} fusion(bf16[1536,3584]{1,0:T(8,128)(2,1)S(1)} %multiply_convert_fusion, bf16[3584,1024]{1,0:T(8,128)(2,1)} %constant_dynamic-update-slice_fusion.6), kind=kOutput, calls=%fused_computation.18 | convolution fusion | flops 11275862016 | bytes 21495808 | tf_op jit(solution)/shard_map/dot_general | solution.py:208
  305.7 9.3 %fusion.5 = bf16[1792,1024]{1,0:T(8,128)(2,1)} fusion(bf16[1536,1024]{1,0:T(8,128)(2,1)} %bitcast.21, bf16[1536,3584]{1,0:T(8,128)(2,1)S(1)} %multiply_convert_fusion), kind=kOutput, calls=%fused_computation.19 | convolution fusion | flops 5638979584 | bytes 12320768 | tf_op jit(solution)/shard_map/dot_general | solution.py:212
  323.1 10.7 %add_convert_fusion = bf16[1792,1024]{1,0:T(8,128)(2,1)} fusion(bf16[1792,1024]{1,0:T(8,128)(2,1)} %collective-permute-done.4, bf16[1536,1024]{1,0:T(8,128)(2,1)} %bitcast.21, bf16[1536,3584]{1,0:T(8,128)(2,1)} %copy-done.37), kind=kOutput, calls=%fused_computation.9 | convolution fusion | flops 5642649600 | bytes 15990784 | tf_op jit(solution)/shard_map/dot_general | solution.py:212
  333.8 30.2 %all-to-all-done.6 = bf16[16,96,1024]{2,1,0:T(8,128)(2,1)} async-done(((bf16[16,96,1024]{2,1,0:T(8,128)(2,1)}), bf16[16,96,1024]{2,1,0:T(8,128)(2,1)}, u32[]{:S(2)}, u32[]{:S(2)}) %all-to-all-start.6) | async-done | bytes 3145760 | tf_op jit(solution)/shard_map/all_to_all | solution.py:42
  374.4 11.7 %all-to-all-start.7 = ((bf16[64,32,1024]{2,1,0:T(8,128)(2,1)}), bf16[64,32,1024]{2,1,0:T(8,128)(2,1)}, u32[]{:S(2)}, u32[]{:S(2)}) async-start(bf16[64,32,1024]{2,1,0:T(8,128)(2,1)} %bitcast.127), calls=%async_computation.7 | async-start | bytes 8388608 | tf_op jit(solution)/shard_map/all_to_all | solution.py:42
  392.6 22.8 %layer_backward.1 = (bf16[96,1024]{1,0:T(8,128)(2,1)S(1)}, bf16[192,1024]{1,0:T(8,128)(2,1)S(1)}, bf16[192,1024]{1,0:T(8,128)(2,1)S(1)}, bf16[96,4096]{1,0:T(8,1...) custom-call(bf16[96,1024]{1,0:T(8,128)(2,1)S(1)} %copy-done.6, ...), custom_call_target="tpu_custom_call" | custom-call | flops 3221225472 | bytes 67108864 | tf_op jit(solution)/shard_map/layer_backward/pallas_call | solution.py:489
  443.1 11.6 %all-to-all-start.8 = ((bf16[64,24,192]{2,1,0:T(8,128)(2,1)}), bf16[64,24,192]{2,1,0:T(8,128)(2,1)S(1)}, u32[]{:S(2)}, u32[]{:S(2)}) async-start(bf16[64,24,192]{2,1,0:T(8,128)(2,1)} %fusion.23), calls=%async_computation.8 | async-start | bytes 1572864 | tf_op jit(solution)/shard_map/all_to_all | solution.py:42
  460.2 26.2 %collective-permute-done.15 = bf16[448,1024]{1,0:T(8,128)(2,1)} collective-permute-done((bf16[448,1024]{1,0:T(8,128)(2,1)}, bf16[448,1024]{1,0:T(8,128)(2,1)}, u32[]{:S(2)}, u32[]{:S(2)}) %collective-permute-start.15) | collective-permute-done | bytes 917536 | tf_op jit(solution)/shard_map/ppermute | solution.py:51
  494.2 9.2 %all-to-all-start.9 = ((bf16[64,8,8192]{2,1,0:T(8,128)(2,1)}), bf16[64,8,8192]{2,1,0:T(8,128)(2,1)}, u32[]{:S(2)}, u32[]{:S(2)}) async-start(bf16[64,8,8192]{2,1,0:T(8,128)(2,1)} %bitcast.31), calls=%async_computation.9 | async-start | bytes 16777216 | tf_op jit(solution)/shard_map/all_to_all | solution.py:42
  504.6 39.9 %fold.1 = f32[16,50304]{1,0:T(8,128)S(1)} custom-call(s32[1,12288]{1,0:T(1,128)S(1)} %copy-done.25, s32[1,12288]{1,0:T(1,128)S(1)} %copy-done.23, f32[16,12288]{1,0:T(8,128)S(1)} %copy-done.8), custom_call_target="tpu_custom_call" | custom-call | flops 19830669312 | bytes 3219456 | tf_op jit(solution)/shard_map/fold/pallas_call | solution.py:191
  570.2 45.4 %all-to-all-done.9 = bf16[64,8,8192]{2,1,0:T(8,128)(2,1)} async-done(((bf16[64,8,8192]{2,1,0:T(8,128)(2,1)}), bf16[64,8,8192]{2,1,0:T(8,128)(2,1)}, u32[]{:S(2)}, u32[]{:S(2)}) %all-to-all-start.9) | async-done | bytes 8388640 | tf_op jit(solution)/shard_map/all_to_all | solution.py:42
  625.6 27.6 %all_to_all.62 = f32[128,1,3]{2,1,0:T(1,128)S(1)} all-to-all(f32[128,1,3]{2,1,0:T(1,128)S(1)} %broadcast_in_dim.167), channel_id=1, replica_groups=mesh['cand'=2,'x'=4,'y'=4,'z'=4] {'cand','x','y','z'}, dimensions={0} | all-to-all | bytes 3072 | tf_op jit(solution)/shard_map/all_to_all | solution.py:42
  661.7 7.8 %multiply_subtract_fusion.1 = (f32[50304,16]{0,1:T(8,128)}, f32[50304,16]{0,1:T(8,128)}, f32[50304,16]{0,1:T(8,128)}) fusion(f32[50304,16]{0,1:T(8,128)S(1)} %copy-done.1, f32[16,50304]{1,0:T(8,128)} %get-tuple-element.128, f32[]{:T(128)S(6)} %min.3, f32[50304,16]{0,1:T(8,128)} %param.40, f32[50304,16]{0,1:T(8,128)} %param.39), kind=kLoop, calls=%fused_computation.31 | loop fusion | flops 12877824 | bytes 22536196 | tf_op jit(solution)/shard_map/sub | solution.py:557
  (388 shorter events, 216.2 us)
Async XLA Ops:
  7.2 107.4 %all-gather.2.cloned.1.call-start = ((), (), s32[]{:S(2)}) async-start(), calls=%async_computation.11 | async-start | bytes 25362432 | tf_op jit(solution)/shard_map/all_gather | solution.py:603
  75.0 22.7 %all-to-all-start.1 = ((bf16[64,16,192]{2,1,0:T(8,128)(2,1)}), bf16[64,16,192]{2,1,0:T(8,128)(2,1)}, u32[]{:S(2)}, u32[]{:S(2)}) async-start(bf16[64,16,192]{2,1,0:T(8,128)(2,1)} %bitcast.132), calls=%async_computation.1 | async-start | bytes 1048576 | tf_op jit(solution)/shard_map/all_to_all | solution.py:42
  101.6 46.9 %all-to-all-start.2 = ((bf16[4,448,1024]{2,1,0:T(8,128)(2,1)}), bf16[4,448,1024]{2,1,0:T(8,128)(2,1)}, u32[]{:S(2)}, u32[]{:S(2)}) async-start(bf16[4,448,1024]{2,1,0:T(8,128)(2,1)} %broadcast_in_dim.86), calls=%async_computation.2 | async-start | bytes 7340032 | tf_op jit(solution)/shard_map/all_to_all | solution.py:42
  148.5 28.1 %collective-permute-start.2 = (bf16[1792,1024]{1,0:T(8,128)(2,1)}, bf16[1792,1024]{1,0:T(8,128)(2,1)}, u32[]{:S(2)}, u32[]{:S(2)}) collective-permute-start(bf16[1792,1024]{1,0:T(8,128)(2,1)} %bitcast.20), channel_id=1, source_target_pairs={{0,64},{64,0},{1,65},{65,1},{2,66},{66,2},{3,67},{67,3},{4,68},{68... | collective-permute-start | bytes 11010056 | tf_op jit(solution)/shard_map/ppermute | solution.py:38
  154.3 48.4 %all-to-all-start.3 = ((bf16[16,96,1024]{2,1,0:T(8,128)(2,1)}), bf16[16,96,1024]{2,1,0:T(8,128)(2,1)}, u32[]{:S(2)}, u32[]{:S(2)}) async-start(bf16[16,96,1024]{2,1,0:T(8,128)(2,1)} %broadcast_in_dim.87), calls=%async_computation.3 | async-start | bytes 6291456 | tf_op jit(solution)/shard_map/all_to_all | solution.py:42
  165.2 5.2 collective-permute-start.1
  233.7 17.9 %all-to-all-start.4 = ((f32[16,3,96]{2,1,0:T(4,128)}), f32[16,3,96]{2,1,0:T(4,128)S(1)}, u32[]{:S(2)}, u32[]{:S(2)}) async-start(f32[16,3,96]{2,1,0:T(4,128)} %copy.110), calls=%async_computation.4 | async-start | bytes 65536 | tf_op jit(solution)/shard_map/all_to_all | solution.py:42
  315.0 8.1 %collective-permute-start.4 = (bf16[1792,1024]{1,0:T(8,128)(2,1)}, bf16[1792,1024]{1,0:T(8,128)(2,1)}, u32[]{:S(2)}, u32[]{:S(2)}) collective-permute-start(bf16[1792,1024]{1,0:T(8,128)(2,1)} %fusion.5), channel_id=1, source_target_pairs={{0,64},{64,0},{1,65},{65,1},{2,66},{66,2},{3,67},{67,3},{4,68},{68... | collective-permute-start | bytes 11010056 | tf_op jit(solution)/shard_map/ppermute | solution.py:38
  316.7 47.2 %all-to-all-start.6 = ((bf16[16,96,1024]{2,1,0:T(8,128)(2,1)}), bf16[16,96,1024]{2,1,0:T(8,128)(2,1)}, u32[]{:S(2)}, u32[]{:S(2)}) async-start(bf16[16,96,1024]{2,1,0:T(8,128)(2,1)} %bitcast.130), calls=%async_computation.6 | async-start | bytes 6291456 | tf_op jit(solution)/shard_map/all_to_all | solution.py:42
  322.2 46.9 %collective-permute-start.12 = (bf16[96,2048]{1,0:T(8,128)(2,1)}, bf16[96,2048]{1,0:T(8,128)(2,1)}, u32[]{:S(2)}, u32[]{:S(2)}) collective-permute-start(bf16[96,2048]{1,0:T(8,128)(2,1)} %get-tuple-element.156), channel_id=1, source_target_pairs={{0,64},{64,0},{1,65},{65,1},{2,66},{66,2},{3,67},{67,3},{4,68},{68... | collective-permute-start | bytes 1179656 | tf_op jit(solution)/shard_map/ppermute | solution.py:38
  374.4 65.2 %all-to-all-start.7 = ((bf16[64,32,1024]{2,1,0:T(8,128)(2,1)}), bf16[64,32,1024]{2,1,0:T(8,128)(2,1)}, u32[]{:S(2)}, u32[]{:S(2)}) async-start(bf16[64,32,1024]{2,1,0:T(8,128)(2,1)} %bitcast.127), calls=%async_computation.7 | async-start | bytes 8388608 | tf_op jit(solution)/shard_map/all_to_all | solution.py:42
  418.3 8.9 %collective-permute-start.5 = (bf16[96,4096]{1,0:T(8,128)(2,1)}, bf16[96,4096]{1,0:T(8,128)(2,1)S(1)}, u32[]{:S(2)}, u32[]{:S(2)}) collective-permute-start(bf16[96,4096]{1,0:T(8,128)(2,1)} %get-tuple-element.65), channel_id=1, source_target_pairs={{0,64},{64,0},{1,65},{65,1},{2,66},{66,2},{3,67},{67,3},{4,68},{68... | collective-permute-start | bytes 2359304 | tf_op jit(solution)/shard_map/ppermute | solution.py:38
  419.1 8.0 %collective-permute-start = (bf16[96,512]{1,0:T(8,128)(2,1)S(1)}, bf16[96,512]{1,0:T(8,128)(2,1)S(1)}, u32[]{:S(2)}, u32[]{:S(2)}) collective-permute-start(bf16[96,512]{1,0:T(8,128)(2,1)S(1)} %get-tuple-element.162), channel_id=1, source_target_pairs={{0,64},{64,0},{1,65},{65,1},{2,66},{66,2},{3,67},{67,3},{4,68},{68... | collective-permute-start | bytes 294920 | tf_op jit(solution)/shard_map/ppermute | solution.py:38
  422.8 11.9 %collective-permute-start.6 = (bf16[96,512]{1,0:T(8,128)(2,1)S(1)}, bf16[96,512]{1,0:T(8,128)(2,1)S(1)}, u32[]{:S(2)}, u32[]{:S(2)}) collective-permute-start(bf16[96,512]{1,0:T(8,128)(2,1)S(1)} %get-tuple-element.160), channel_id=1, source_target_pairs={{0,64},{64,0},{1,65},{65,1},{2,66},{66,2},{3,67},{67,3},{4,68},{68... | collective-permute-start | bytes 294920 | tf_op jit(solution)/shard_map/ppermute | solution.py:38
  423.2 13.1 %collective-permute-start.9 = (bf16[96,1024]{1,0:T(8,128)(2,1)}, bf16[96,1024]{1,0:T(8,128)(2,1)S(1)}, u32[]{:S(2)}, u32[]{:S(2)}) collective-permute-start(bf16[96,1024]{1,0:T(8,128)(2,1)} %copy-done.30), channel_id=1, source_target_pairs={{0,64},{64,0},{1,65},{65,1},{2,66},{66,2},{3,67},{67,3},{4,68},{68... | collective-permute-start | bytes 589832 | tf_op jit(solution)/shard_map/ppermute | solution.py:38
  423.4 31.4 %collective-permute-start.10 = (bf16[192,1024]{1,0:T(8,128)(2,1)}, bf16[192,1024]{1,0:T(8,128)(2,1)}, u32[]{:S(2)}, u32[]{:S(2)}) collective-permute-start(bf16[192,1024]{1,0:T(8,128)(2,1)} %copy-done.28), channel_id=1, source_target_pairs={{0,64},{64,0},{1,65},{65,1},{2,66},{66,2},{3,67},{67,3},{4,68},{68... | collective-permute-start | bytes 1179656 | tf_op jit(solution)/shard_map/ppermute | solution.py:38
  427.1 30.4 %collective-permute-start.11 = (bf16[192,1024]{1,0:T(8,128)(2,1)S(1)}, bf16[192,1024]{1,0:T(8,128)(2,1)}, u32[]{:S(2)}, u32[]{:S(2)}) collective-permute-start(bf16[192,1024]{1,0:T(8,128)(2,1)S(1)} %copy-done.27), channel_id=1, source_target_pairs={{0,64},{64,0},{1,65},{65,1},{2,66},{66,2},{3,67},{67,3},{4,68},{68... | collective-permute-start | bytes 1179656 | tf_op jit(solution)/shard_map/ppermute | solution.py:38
  427.2 59.2 %collective-permute-start.15 = (bf16[448,1024]{1,0:T(8,128)(2,1)}, bf16[448,1024]{1,0:T(8,128)(2,1)}, u32[]{:S(2)}, u32[]{:S(2)}) collective-permute-start(bf16[448,1024]{1,0:T(8,128)(2,1)} %get-tuple-element.153), channel_id=1, source_target_pairs={{0,3},{1,0},{2,1},{3,2},{4,7},{5,4},{6,5},{7,6},{8,11},{9,8},{10,9... | collective-permute-start | bytes 2752520 | tf_op jit(solution)/shard_map/ppermute | solution.py:51
  434.6 51.8 %collective-permute-start.14 = (bf16[448,1024]{1,0:T(8,128)(2,1)}, bf16[448,1024]{1,0:T(8,128)(2,1)}, u32[]{:S(2)}, u32[]{:S(2)}) collective-permute-start(bf16[448,1024]{1,0:T(8,128)(2,1)} %get-tuple-element.154), channel_id=1, source_target_pairs={{0,1},{1,2},{2,3},{3,0},{4,5},{5,6},{6,7},{7,4},{8,9},{9,10},{10,1... | collective-permute-start | bytes 2752520 | tf_op jit(solution)/shard_map/ppermute | solution.py:51
  436.3 51.0 %collective-permute-start.13 = (bf16[448,1024]{1,0:T(8,128)(2,1)}, bf16[448,1024]{1,0:T(8,128)(2,1)}, u32[]{:S(2)}, u32[]{:S(2)}) collective-permute-start(bf16[448,1024]{1,0:T(8,128)(2,1)} %get-tuple-element.152), channel_id=1, source_target_pairs={{0,2},{1,3},{2,0},{3,1},{4,6},{5,7},{6,4},{7,5},{8,10},{9,11},{10,... | collective-permute-start | bytes 2752520 | tf_op jit(solution)/shard_map/ppermute | solution.py:51
  443.1 48.2 %all-to-all-start.8 = ((bf16[64,24,192]{2,1,0:T(8,128)(2,1)}), bf16[64,24,192]{2,1,0:T(8,128)(2,1)S(1)}, u32[]{:S(2)}, u32[]{:S(2)}) async-start(bf16[64,24,192]{2,1,0:T(8,128)(2,1)} %fusion.23), calls=%async_computation.8 | async-start | bytes 1572864 | tf_op jit(solution)/shard_map/all_to_all | solution.py:42
  494.2 121.5 %all-to-all-start.9 = ((bf16[64,8,8192]{2,1,0:T(8,128)(2,1)}), bf16[64,8,8192]{2,1,0:T(8,128)(2,1)}, u32[]{:S(2)}, u32[]{:S(2)}) async-start(bf16[64,8,8192]{2,1,0:T(8,128)(2,1)} %bitcast.31), calls=%async_computation.9 | async-start | bytes 16777216 | tf_op jit(solution)/shard_map/all_to_all | solution.py:42
  544.5 19.4 %collective-permute-start.17 = (f32[16,50304]{1,0:T(8,128)S(1)}, f32[16,50304]{1,0:T(8,128)}, u32[]{:S(2)}, u32[]{:S(2)}) collective-permute-start(f32[16,50304]{1,0:T(8,128)S(1)} %fold.1), channel_id=1, source_target_pairs={{0,64},{64,0},{1,65},{65,1},{2,66},{66,2},{3,67},{67,3},{4,68},{68... | collective-permute-start | bytes 9658376 | tf_op jit(solution)/shard_map/ppermute | solution.py:38
  545.5 8.2 %collective-permute-start.18 = (f32[448,1024]{1,0:T(8,128)}, f32[448,1024]{1,0:T(8,128)}, u32[]{:S(2)}, u32[]{:S(2)}) collective-permute-start(f32[448,1024]{1,0:T(8,128)} %fusion.14), channel_id=1, source_target_pairs={{0,64},{64,0},{1,65},{65,1},{2,66},{66,2},{3,67},{67,3},{4,68},{68... | collective-permute-start | bytes 5505032 | tf_op jit(solution)/shard_map/ppermute | solution.py:38
  (89 other events, 855.8 us)
Sparse Core Ops, SparseCore 0:
  11.7 102.8 all-gather.1

commit v5 on v4

--- a/solution.py
+++ b/solution.py
@@ -57,8 +57,16 @@
     def piece(step):
         return lax.dynamic_index_in_dim(pieces, (me + step) % RING, 0, False)
 
-    got = [shift(piece(step), axis, step).astype(jnp.float32) for step in (1, 2, 3)]
-    return piece(0).astype(jnp.float32) + got[1] + (got[0] + got[2])
+    def added(first, second):
+        return (first.astype(jnp.float32) + second.astype(jnp.float32)).astype(first.dtype)
+
+    own, after, far, before = (piece(step) for step in range(RING))
+    mid = far.shape[0] // 2
+    back, onward = shift(far[:mid], axis, -1), shift(far[mid:], axis, 1)
+    before = jnp.concatenate([added(before[:mid], back), before[mid:]], axis=0)
+    after = jnp.concatenate([after[:mid], added(after[mid:], onward)], axis=0)
+    got = shift(before, axis, -1).astype(jnp.float32) + shift(after, axis, 1).astype(jnp.float32)
+    return own.astype(jnp.float32) + got
 
 
 def of_both(value):
@@ -732,11 +740,12 @@
     grad_sum = jnp.sum(grad_low.astype(jnp.float32), 0)
     grad_both = of_both(grad_low)
     down_g = matmul_tn(half_of_both(act), grad_both).astype(jnp.bfloat16).reshape(64, 32, D)
-    down_g = exchange(down_g, AXES)
+    proj_g = matmul_tn(half_of_both(mixed), grad_both).astype(jnp.bfloat16).reshape(64, 8, D)
+    early = exchange(jnp.concatenate([down_g, proj_g], axis=1), AXES)
     query_grad, key_grad, value_grad, up_grad, attn_grad, mlp_grad, *sums = layer_backward(
         grad_low, (query, keys, values, up_val), gathered, tables
     )
-    attn_grad, mlp_grad, down_g = lax.optimization_barrier((attn_grad, mlp_grad, down_g))
+    attn_grad, mlp_grad, early = lax.optimization_barrier((attn_grad, mlp_grad, early))
     input_one, gain_one_grad, bias_one_grad = norm_back(inputs, pieces[0], pieces[1], attn_grad)
     input_two, gain_two_grad, bias_two_grad = norm_back(first_rows, pieces[2], pieces[3], mlp_grad)
     input_grad = input_one + jnp.pad(grad_hidden + input_two, ((0, live_rows), (0, 0)))
@@ -745,7 +754,6 @@
         [attn_both[:live_rows], attn_both[2 * live_rows : 3 * live_rows]], axis=0
     )
     up_g = matmul_tn(half_of_both(mlp_in), of_both(up_grad)).astype(jnp.bfloat16)
-    proj_g = matmul_tn(half_of_both(mixed), grad_both).astype(jnp.bfloat16)
     query_g = matmul_tn(first_both, of_both(query_grad)).astype(jnp.bfloat16)
     key_g = matmul_tn(attn_both, of_both(key_grad)).astype(jnp.bfloat16)
     value_g = matmul_tn(attn_both, of_both(value_grad)).astype(jnp.bfloat16)
@@ -761,7 +769,7 @@
     vector_both = jnp.pad(vector_both, ((0, 0), (0, 4), (0, slots * SEQ - 120)))
     turned_grad = input_grad.astype(jnp.bfloat16).T.reshape(64, 16, slots * SEQ)
     turned_grad = jnp.concatenate([turned_grad, vector_both], axis=1)
-    rest = jnp.concatenate([up_g, proj_g, query_g, key_g, value_g], axis=1).reshape(64, 8, 8 * D)
+    rest = jnp.concatenate([up_g, query_g, key_g, value_g], axis=1).reshape(64, 8, 7 * D)
     turned_grad = exchange(turned_grad, AXES)
     embed_rows = turned_grad[:, :16].astype(jnp.float32).swapaxes(0, 1).reshape(16, -1)
     vector_both = jnp.sum(turned_grad[:, 16:20, :120].astype(jnp.float32), 0).reshape(2, 2, 120)
@@ -776,8 +784,8 @@
     embed_grad = (embed_grad + swap(embed_grad)).T
     rest = jnp.sum(rest.astype(jnp.float32), 0)
 
-    down_g = jnp.sum(down_g.astype(jnp.float32), 0)
-    shards = (rest[:, 5 * D :], rest[:, 4 * D : 5 * D], rest[:, : 4 * D], down_g, vector_grad)
+    early = jnp.sum(early.astype(jnp.float32), 0)
+    shards = (rest[:, 4 * D :], early[32:], rest[:, : 4 * D], early[:32], vector_grad)
     local_squares = sum((jnp.sum(piece * piece) for piece in shards))
     local_squares = (
         local_squares + (jnp.sum(embed_grad * embed_grad) + jnp.sum(head_grad * head_grad)) / 2

time: 698 us -> 683 us (0.979)
  local copies, waits for them, and re-layouts: 62.8 us -> 45.7 us
  blocking collectives: 57.8 us -> 65.9 us
  matrix products: 75.1 us -> 67.6 us
    all_gather x1, waiting for transfers between devices: 6.81 us -> 17.3 us  [body(): lax.all_gather(packed.astype(jnp.bfloat16), ('cand', *AXES), axis=0, tile...]
    ppermute x16, waiting for transfers between devices: 11.3 us -> 2.54 us  [swap(): return lax.ppermute(value, 'cand', [(0, 1), (1, 0)])]
    ppermute x3 -> x4, waiting for transfers between devices: 27.1 us -> 35.7 us  [shift(): lax.ppermute(value, axis, [(i, (i + step) % RING) for i in range(RING)])]
    all_to_all x8, waiting for transfers between devices: 124 us -> 116 us  [exchange(): return lax.all_to_all(pieces, axes, split_axis=0, concat_axis=0, tiled=True)]
    all_to_all x3, blocking collectives: 57.8 us -> 65.9 us  [exchange(): return lax.all_to_all(pieces, axes, split_axis=0, concat_axis=0, tiled=True)]
    all_to_all x8, starting transfers between devices: 65.5 us -> 57.7 us  [exchange(): return lax.all_to_all(pieces, axes, split_axis=0, concat_axis=0, tiled=True)]
    dot_general x8, matrix products: 37.5 us -> 30 us  [matmul_tn(): lax.dot_general(left, right, (((0,), (0,)), ((), ())), preferred_element_...]
    unnamed x187 -> x149, local copies, waits for them, and re-layouts: 27.8 us -> 21.2 us
  transfers between devices with their start and end apart: 28 -> 29, of which waited for: 15 -> 13; matrix products, arithmetic and copies ran while one was open for 15% -> 14% of each run, Pallas kernels for 15% -> 15%
where the time goes in v5:
time: 683 us; the launch traced here: 673 us
  waiting for transfers between devices  171 us (25%)
  other arithmetic  111 us (16%)
  Pallas kernels  104 us (15%)
  starting transfers between devices  78.1 us (11%)
  matrix products  67.6 us (10%)
  blocking collectives  65.9 us (10%)
  local copies, waits for them, and re-layouts  45.7 us (7%)
  between operations  28.9 us (4%)
    all_to_all x8, waiting for transfers between devices, exchange(): return lax.all_to_all(pieces, axes, split_axis=0, concat_axis=0, tiled=True)  116 us
    all_to_all x3, blocking collectives, exchange(): return lax.all_to_all(pieces, axes, split_axis=0, concat_axis=0, tiled=True)  65.9 us
    all_to_all x8, starting transfers between devices, exchange(): return lax.all_to_all(pieces, axes, split_axis=0, concat_axis=0, tiled=True)  57.7 us
    pallas_call x1, Pallas kernels, fold(): pl.pallas_call(fold_kernel, grid=(count // FOLD_BLOCK,), in_specs=[row, r...  39.9 us
    ppermute x4, waiting for transfers between devices, shift(): lax.ppermute(value, axis, [(i, (i + step) % RING) for i in range(RING)])  35.7 us
    dot_general x8, matrix products, matmul_tn(): lax.dot_general(left, right, (((0,), (0,)), ((), ())), preferred_element_...  30 us
    pallas_call x1, Pallas kernels, look_up(): pl.pallas_call(look_kernel, grid=(count // LOOK_BLOCK,), in_specs=[row, r...  24.2 us
    pallas_call x1, Pallas kernels, layer_backward(): pl.pallas_call(backward_kernel, grid=(HEADS // 2,), in_specs=[whole(live,...  22.3 us
  transfers between devices with their start and end apart: 29, of which 13 were waited for; matrix products, arithmetic and copies ran while one was open for 14% of the time, Pallas kernels for 15%

profile of v5, /device:TPU:1, one launch (start us, length us, event | category | flops | bytes accessed | tf_op | source)
XLA Modules:
  0.0 672.6 jit_solution(5297877647749029964)
XLA Ops:
  19.7 20.3 %all_to_all.60 = f32[64,1,256]{2,1,0:T(1,128)S(1)} all-to-all(f32[64,1,256]{2,1,0:T(1,128)S(1)} %broadcast_in_dim.82), channel_id=1, replica_groups=mesh['cand'=2,'x'=4,'y'=4,'z'=4] {'x','y','z'}, dimensions={0} | all-to-all | bytes 131072 | tf_op jit(solution)/shard_map/all_to_all | solution.py:42
  43.5 24.2 %look_up.1 = f32[16,12288]{1,0:T(8,128)S(1)} custom-call(s32[1,12288]{1,0:T(1,128)S(1)} %and_select_fusion.1.high_ref, s32[1,12288]{1,0:T(1,128)S(1)} %get-tuple-element.148.low_ref, f32[16,50304]{1,0:T(8,128)S(1)} %bitcast.126), custom_call_target="tpu_custom_call" | custom-call | flops 19830669312 | bytes 3219456 | tf_op jit(solution)/shard_map/look_up/pallas_call | solution.py:131
  78.4 13.2 %all-to-all-done.1 = bf16[64,16,192]{2,1,0:T(8,128)(2,1)S(1)} async-done(((bf16[64,16,192]{2,1,0:T(8,128)(2,1)}), bf16[64,16,192]{2,1,0:T(8,128)(2,1)S(1)}, u32[]{:S(2)}, u32[]{:S(2)}) %all-to-all-start.1) | async-done | bytes 393248 | tf_op jit(solution)/shard_map/all_to_all | solution.py:42
  102.0 17.3 %all-gather.2.cloned.1.call-done.query_w.key_w.value_w.proj_w.up_w.down_w = bf16[1024,12288]{1,0:T(8,128)(2,1)} async-done(((bf16[8,12288]{1,0:T(8,128)(2,1)}), bf16[1024,12288]{1,0:T(8,128)(2,1)}) %all-gather.2.cloned.1.call-update) | async-done | bytes 25165840 | tf_op jit(solution)/shard_map/all_gather | solution.py:611
  119.3 17.4 %layer_forward.1 = (bf16[96,1024]{1,0:T(8,128)(2,1)S(1)}, bf16[192,1024]{1,0:T(8,128)(2,1)S(1)}, bf16[192,1024]{1,0:T(8,128)(2,1)S(1)}, bf16[96,1024]{1,0:T(8,12...) custom-call(bf16[192,1024]{1,0:T(8,128)(2,1)S(1)} %add_convert_fusion.2.attn_ref, ...), custom_call_target="tpu_custom_call" | custom-call | flops 3221225472 | bytes 67108864 | tf_op jit(solution)/shard_map/layer_forward/pallas_call | solution.py:453
  140.7 8.8 %all-to-all-done.2 = bf16[4,448,1024]{2,1,0:T(8,128)(2,1)} async-done(((bf16[4,448,1024]{2,1,0:T(8,128)(2,1)}), bf16[4,448,1024]{2,1,0:T(8,128)(2,1)}, u32[]{:S(2)}, u32[]{:S(2)}) %all-to-all-start.2) | async-done | bytes 3670048 | tf_op jit(solution)/shard_map/all_to_all | solution.py:42
  171.1 30.8 %all-to-all-done.3 = bf16[16,96,1024]{2,1,0:T(8,128)(2,1)} async-done(((bf16[16,96,1024]{2,1,0:T(8,128)(2,1)}), bf16[16,96,1024]{2,1,0:T(8,128)(2,1)}, u32[]{:S(2)}, u32[]{:S(2)}) %all-to-all-start.3) | async-done | bytes 3145760 | tf_op jit(solution)/shard_map/all_to_all | solution.py:42
  201.8 19.4 %fusion.110 = (f32[1536]{0:T(1024)S(1)}, f32[1536,3584]{1,0:T(8,128)}) fusion(bf16[1536,1024]{1,0:T(8,128)(2,1)} %bitcast.21, bf16[3584,1024]{1,0:T(8,128)(2,1)} %constant_dynamic-update-slice_fusion.5, pred[3584]{0:T(1024)(128)(4,1)S(1)} %fusion.48), kind=kOutput, calls=%fused_computation.313 | convolution fusion | flops 11285297152 | bytes 32515584 | tf_op jit(solution)/shard_map/dot_general | solution.py:226
  221.3 10.7 %exponential_reduce_fusion = (f32[1536]{0:T(1024)S(1)}, f32[1536]{0:T(1024)S(1)}) fusion(f32[1536,3584]{1,0:T(8,128)} %get-tuple-element.193, f32[1536]{0:T(1024)S(1)} %get-tuple-element.192, s32[1536]{0:T(1024)S(1)} %fusion.57), kind=kLoop, calls=%fused_computation.3 | loop fusion | flops 27522048 | bytes 22044672 | tf_op jit(solution)/shard_map/reduce_sum | solution.py:693
  232.8 11.4 %all-to-all-start.4 = ((f32[16,3,96]{2,1,0:T(4,128)}), f32[16,3,96]{2,1,0:T(4,128)S(1)}, u32[]{:S(2)}, u32[]{:S(2)}) async-start(f32[16,3,96]{2,1,0:T(4,128)} %copy.110), calls=%async_computation.4 | async-start | bytes 65536 | tf_op jit(solution)/shard_map/all_to_all | solution.py:42
  261.3 10.0 %all_to_all.61 = f32[16,2,96]{2,1,0:T(2,128)S(1)} all-to-all(f32[16,2,96]{2,1,0:T(2,128)S(1)} %broadcast_in_dim.95), channel_id=1, replica_groups=mesh['cand'=2,'x'=4,'y'=4,'z'=4] {'x','y'}, dimensions={0} | all-to-all | bytes 24576 | tf_op jit(solution)/shard_map/all_to_all | solution.py:42
  271.5 11.7 %multiply_convert_fusion = bf16[1536,3584]{1,0:T(8,128)(2,1)S(1)} fusion(f32[1536,3584]{1,0:T(8,128)} %get-tuple-element.193, f32[1536]{0:T(1024)S(1)} %sub.191, f32[1536]{0:T(1024)S(1)} %mul.644, s32[1536]{0:T(1024)S(1)} %fusion.57), kind=kLoop, calls=%fused_computation | loop fusion | flops 33030144 | bytes 33048576 | tf_op jit(solution)/shard_map/convert_element_type | solution.py:723
  283.2 18.2 %convolution_convert_fusion.1 = bf16[1536,1024]{1,0:T(8,128)(2,1)} fusion(bf16[1536,3584]{1,0:T(8,128)(2,1)S(1)} %multiply_convert_fusion, bf16[3584,1024]{1,0:T(8,128)(2,1)} %constant_dynamic-update-slice_fusion.5), kind=kOutput, calls=%fused_computation.19 | convolution fusion | flops 11275862016 | bytes 21495808 | tf_op jit(solution)/shard_map/dot_general | solution.py:216
  301.4 9.3 %fusion.4 = bf16[1792,1024]{1,0:T(8,128)(2,1)} fusion(bf16[1536,1024]{1,0:T(8,128)(2,1)} %bitcast.21, bf16[1536,3584]{1,0:T(8,128)(2,1)S(1)} %multiply_convert_fusion), kind=kOutput, calls=%fused_computation.20 | convolution fusion | flops 5638979584 | bytes 12320768 | tf_op jit(solution)/shard_map/dot_general | solution.py:220
  319.3 10.7 %add_convert_fusion = bf16[1792,1024]{1,0:T(8,128)(2,1)} fusion(bf16[1792,1024]{1,0:T(8,128)(2,1)} %collective-permute-done.4, bf16[1536,1024]{1,0:T(8,128)(2,1)} %bitcast.21, bf16[1536,3584]{1,0:T(8,128)(2,1)} %copy-done.29), kind=kOutput, calls=%fused_computation.10 | convolution fusion | flops 5642649600 | bytes 15990784 | tf_op jit(solution)/shard_map/dot_general | solution.py:220
  329.9 29.8 %all-to-all-done.6 = bf16[16,96,1024]{2,1,0:T(8,128)(2,1)} async-done(((bf16[16,96,1024]{2,1,0:T(8,128)(2,1)}), bf16[16,96,1024]{2,1,0:T(8,128)(2,1)}, u32[]{:S(2)}, u32[]{:S(2)}) %all-to-all-start.6) | async-done | bytes 3145760 | tf_op jit(solution)/shard_map/all_to_all | solution.py:42
  372.1 11.6 %all-to-all-start.7 = ((bf16[64,40,1024]{2,1,0:T(8,128)(2,1)}), bf16[64,40,1024]{2,1,0:T(8,128)(2,1)}, u32[]{:S(2)}, u32[]{:S(2)}) async-start(bf16[64,40,1024]{2,1,0:T(8,128)(2,1)} %pad_maximum_fusion), calls=%async_computation.7 | async-start | bytes 10485760 | tf_op jit(solution)/shard_map/all_to_all | solution.py:42
  390.1 22.3 %layer_backward.1 = (bf16[96,1024]{1,0:T(8,128)(2,1)S(1)}, bf16[192,1024]{1,0:T(8,128)(2,1)S(1)}, bf16[192,1024]{1,0:T(8,128)(2,1)S(1)}, bf16[96,4096]{1,0:T(8,1...) custom-call(bf16[96,1024]{1,0:T(8,128)(2,1)S(1)} %get-tuple-element., ...), custom_call_target="tpu_custom_call" | custom-call | flops 3221225472 | bytes 67108864 | tf_op jit(solution)/shard_map/layer_backward/pallas_call | solution.py:497
  420.9 35.7 %collective-permute-done.13 = bf16[224,1024]{1,0:T(8,128)(2,1)S(1)} collective-permute-done((bf16[224,1024]{1,0:T(8,128)(2,1)S(1)}, bf16[224,1024]{1,0:T(8,128)(2,1)S(1)}, u32[]{:S(2)}, u32[]{:S(2)}) %collective-permute-start.13) | collective-permute-done | bytes 458784 | tf_op jit(solution)/shard_map/ppermute | solution.py:51
  473.0 7.6 %all-to-all-start.8 = ((bf16[64,24,192]{2,1,0:T(8,128)(2,1)}), bf16[64,24,192]{2,1,0:T(8,128)(2,1)S(1)}, u32[]{:S(2)}, u32[]{:S(2)}) async-start(bf16[64,24,192]{2,1,0:T(8,128)(2,1)} %fusion.20), calls=%async_computation.8 | async-start | bytes 1572864 | tf_op jit(solution)/shard_map/all_to_all | solution.py:42
  507.7 39.9 %fold.1 = f32[16,50304]{1,0:T(8,128)S(1)} custom-call(s32[1,12288]{1,0:T(1,128)S(1)} %copy-done.24, s32[1,12288]{1,0:T(1,128)S(1)} %copy-done.22, f32[16,12288]{1,0:T(8,128)S(1)} %copy-done.5), custom_call_target="tpu_custom_call" | custom-call | flops 19830669312 | bytes 3219456 | tf_op jit(solution)/shard_map/fold/pallas_call | solution.py:199
  567.1 26.4 %all-to-all-done.9 = bf16[64,8,7168]{2,1,0:T(8,128)(2,1)} async-done(((bf16[64,8,7168]{2,1,0:T(8,128)(2,1)}), bf16[64,8,7168]{2,1,0:T(8,128)(2,1)}, u32[]{:S(2)}, u32[]{:S(2)}) %all-to-all-start.9) | async-done | bytes 7340064 | tf_op jit(solution)/shard_map/all_to_all | solution.py:42
  602.4 35.7 %all_to_all.62 = f32[128,1,3]{2,1,0:T(1,128)} all-to-all(f32[128,1,3]{2,1,0:T(1,128)S(1)} %broadcast_in_dim.167), channel_id=1, replica_groups=mesh['cand'=2,'x'=4,'y'=4,'z'=4] {'cand','x','y','z'}, dimensions={0} | all-to-all | bytes 3072 | tf_op jit(solution)/shard_map/all_to_all | solution.py:42
  647.4 7.8 %multiply_subtract_fusion.1 = (f32[50304,16]{0,1:T(8,128)}, f32[50304,16]{0,1:T(8,128)}, f32[50304,16]{0,1:T(8,128)}) fusion(f32[50304,16]{0,1:T(8,128)S(1)} %copy-done.1, f32[16,50304]{1,0:T(8,128)} %get-tuple-element.128, f32[]{:T(128)S(6)} %min.3, f32[50304,16]{0,1:T(8,128)} %param.40, f32[50304,16]{0,1:T(8,128)} %param.39), kind=kLoop, calls=%fused_computation.32 | loop fusion | flops 12877824 | bytes 22536196 | tf_op jit(solution)/shard_map/sub | solution.py:565
  (357 shorter events, 193.2 us)
Async XLA Ops:
  7.2 112.1 %all-gather.2.cloned.1.call-start = ((), (), s32[]{:S(2)}) async-start(), calls=%async_computation.11 | async-start | bytes 25362432 | tf_op jit(solution)/shard_map/all_gather | solution.py:611
  69.5 22.2 %all-to-all-start.1 = ((bf16[64,16,192]{2,1,0:T(8,128)(2,1)}), bf16[64,16,192]{2,1,0:T(8,128)(2,1)S(1)}, u32[]{:S(2)}, u32[]{:S(2)}) async-start(bf16[64,16,192]{2,1,0:T(8,128)(2,1)} %bitcast.117), calls=%async_computation.1 | async-start | bytes 1048576 | tf_op jit(solution)/shard_map/all_to_all | solution.py:42
  96.0 53.6 %all-to-all-start.2 = ((bf16[4,448,1024]{2,1,0:T(8,128)(2,1)}), bf16[4,448,1024]{2,1,0:T(8,128)(2,1)}, u32[]{:S(2)}, u32[]{:S(2)}) async-start(bf16[4,448,1024]{2,1,0:T(8,128)(2,1)} %broadcast_in_dim.86), calls=%async_computation.2 | async-start | bytes 7340032 | tf_op jit(solution)/shard_map/all_to_all | solution.py:42
  149.6 17.2 %collective-permute-start.2 = (bf16[1792,1024]{1,0:T(8,128)(2,1)}, bf16[1792,1024]{1,0:T(8,128)(2,1)}, u32[]{:S(2)}, u32[]{:S(2)}) collective-permute-start(bf16[1792,1024]{1,0:T(8,128)(2,1)} %bitcast.20), channel_id=1, source_target_pairs={{0,64},{64,0},{1,65},{65,1},{2,66},{66,2},{3,67},{67,3},{4,68},{68... | collective-permute-start | bytes 11010056 | tf_op jit(solution)/shard_map/ppermute | solution.py:38
  153.4 48.5 %all-to-all-start.3 = ((bf16[16,96,1024]{2,1,0:T(8,128)(2,1)}), bf16[16,96,1024]{2,1,0:T(8,128)(2,1)}, u32[]{:S(2)}, u32[]{:S(2)}) async-start(bf16[16,96,1024]{2,1,0:T(8,128)(2,1)} %broadcast_in_dim.87), calls=%async_computation.3 | async-start | bytes 6291456 | tf_op jit(solution)/shard_map/all_to_all | solution.py:42
  232.8 17.9 %all-to-all-start.4 = ((f32[16,3,96]{2,1,0:T(4,128)}), f32[16,3,96]{2,1,0:T(4,128)S(1)}, u32[]{:S(2)}, u32[]{:S(2)}) async-start(f32[16,3,96]{2,1,0:T(4,128)} %copy.110), calls=%async_computation.4 | async-start | bytes 65536 | tf_op jit(solution)/shard_map/all_to_all | solution.py:42
  251.6 3.4 collective-permute-start.3
  310.7 8.5 %collective-permute-start.4 = (bf16[1792,1024]{1,0:T(8,128)(2,1)}, bf16[1792,1024]{1,0:T(8,128)(2,1)}, u32[]{:S(2)}, u32[]{:S(2)}) collective-permute-start(bf16[1792,1024]{1,0:T(8,128)(2,1)} %fusion.4), channel_id=1, source_target_pairs={{0,64},{64,0},{1,65},{65,1},{2,66},{66,2},{3,67},{67,3},{4,68},{68... | collective-permute-start | bytes 11010056 | tf_op jit(solution)/shard_map/ppermute | solution.py:38
  312.5 47.2 %all-to-all-start.6 = ((bf16[16,96,1024]{2,1,0:T(8,128)(2,1)}), bf16[16,96,1024]{2,1,0:T(8,128)(2,1)}, u32[]{:S(2)}, u32[]{:S(2)}) async-start(bf16[16,96,1024]{2,1,0:T(8,128)(2,1)} %bitcast.146), calls=%async_computation.6 | async-start | bytes 6291456 | tf_op jit(solution)/shard_map/all_to_all | solution.py:42
  319.1 47.6 %collective-permute-start.10 = (bf16[96,2048]{1,0:T(8,128)(2,1)}, bf16[96,2048]{1,0:T(8,128)(2,1)}, u32[]{:S(2)}, u32[]{:S(2)}) collective-permute-start(bf16[96,2048]{1,0:T(8,128)(2,1)} %get-tuple-element.159), channel_id=1, source_target_pairs={{0,64},{64,0},{1,65},{65,1},{2,66},{66,2},{3,67},{67,3},{4,68},{68... | collective-permute-start | bytes 1179656 | tf_op jit(solution)/shard_map/ppermute | solution.py:38
  372.1 93.7 %all-to-all-start.7 = ((bf16[64,40,1024]{2,1,0:T(8,128)(2,1)}), bf16[64,40,1024]{2,1,0:T(8,128)(2,1)}, u32[]{:S(2)}, u32[]{:S(2)}) async-start(bf16[64,40,1024]{2,1,0:T(8,128)(2,1)} %pad_maximum_fusion), calls=%async_computation.7 | async-start | bytes 10485760 | tf_op jit(solution)/shard_map/all_to_all | solution.py:42
  383.9 31.9 %collective-permute-start.6 = (bf16[192,512]{1,0:T(8,128)(2,1)S(1)}, bf16[192,512]{1,0:T(8,128)(2,1)S(1)}, u32[]{:S(2)}, u32[]{:S(2)}) collective-permute-start(bf16[192,512]{1,0:T(8,128)(2,1)S(1)} %get-tuple-element.161), channel_id=1, source_target_pairs={{0,64},{64,0},{1,65},{65,1},{2,66},{66,2},{3,67},{67,3},{4,68},{68... | collective-permute-start | bytes 589832 | tf_op jit(solution)/shard_map/ppermute | solution.py:38
  412.4 4.9 collective-permute-start.9
  412.5 6.6 collective-permute-start.8
  413.3 43.2 %collective-permute-start.13 = (bf16[224,1024]{1,0:T(8,128)(2,1)S(1)}, bf16[224,1024]{1,0:T(8,128)(2,1)S(1)}, u32[]{:S(2)}, u32[]{:S(2)}) collective-permute-start(bf16[224,1024]{1,0:T(8,128)(2,1)S(1)} %get-tuple-element.154), channel_id=1, source_target_pairs={{0,3},{1,0},{2,1},{3,2},{4,7},{5,4},{6,5},{7,6},{8,11},{9,8},{10,9... | collective-permute-start | bytes 1376264 | tf_op jit(solution)/shard_map/ppermute | solution.py:51
  415.8 40.7 %collective-permute-start.15 = (bf16[224,1024]{1,0:T(8,128)(2,1)S(1)}, bf16[224,1024]{1,0:T(8,128)(2,1)S(1)}, u32[]{:S(2)}, u32[]{:S(2)}) collective-permute-start(bf16[224,1024]{1,0:T(8,128)(2,1)S(1)} %get-tuple-element.156), channel_id=1, source_target_pairs={{0,1},{1,2},{2,3},{3,0},{4,5},{5,6},{6,7},{7,4},{8,9},{9,10},{10,1... | collective-permute-start | bytes 1376264 | tf_op jit(solution)/shard_map/ppermute | solution.py:51
  415.9 46.5 %collective-permute-start = (bf16[96,512]{1,0:T(8,128)(2,1)S(1)}, bf16[96,512]{1,0:T(8,128)(2,1)S(1)}, u32[]{:S(2)}, u32[]{:S(2)}) collective-permute-start(bf16[96,512]{1,0:T(8,128)(2,1)S(1)} %get-tuple-element.165), channel_id=1, source_target_pairs={{0,64},{64,0},{1,65},{65,1},{2,66},{66,2},{3,67},{67,3},{4,68},{68... | collective-permute-start | bytes 294920 | tf_op jit(solution)/shard_map/ppermute | solution.py:38
  417.3 45.0 %collective-permute-start.5 = (bf16[96,4096]{1,0:T(8,128)(2,1)S(1)}, bf16[96,4096]{1,0:T(8,128)(2,1)S(1)}, u32[]{:S(2)}, u32[]{:S(2)}) collective-permute-start(bf16[96,4096]{1,0:T(8,128)(2,1)S(1)} %get-tuple-element.65), channel_id=1, source_target_pairs={{0,64},{64,0},{1,65},{65,1},{2,66},{66,2},{3,67},{67,3},{4,68},{68... | collective-permute-start | bytes 2359304 | tf_op jit(solution)/shard_map/ppermute | solution.py:38
  457.9 28.8 %collective-permute-start.16 = (bf16[448,1024]{1,0:T(8,128)(2,1)}, bf16[448,1024]{1,0:T(8,128)(2,1)}, u32[]{:S(2)}, u32[]{:S(2)}) collective-permute-start(bf16[448,1024]{1,0:T(8,128)(2,1)} %pad_maximum_fusion.4), channel_id=1, source_target_pairs={{0,1},{1,2},{2,3},{3,0},{4,5},{5,6},{6,7},{7,4},{8,9},{9,10},{10,1... | collective-permute-start | bytes 2752520 | tf_op jit(solution)/shard_map/ppermute | solution.py:51
  458.9 27.8 %collective-permute-start.14 = (bf16[448,1024]{1,0:T(8,128)(2,1)}, bf16[448,1024]{1,0:T(8,128)(2,1)}, u32[]{:S(2)}, u32[]{:S(2)}) collective-permute-start(bf16[448,1024]{1,0:T(8,128)(2,1)} %pad_maximum_fusion.3), channel_id=1, source_target_pairs={{0,3},{1,0},{2,1},{3,2},{4,7},{5,4},{6,5},{7,6},{8,11},{9,8},{10,9... | collective-permute-start | bytes 2752520 | tf_op jit(solution)/shard_map/ppermute | solution.py:51
  473.0 21.4 %all-to-all-start.8 = ((bf16[64,24,192]{2,1,0:T(8,128)(2,1)}), bf16[64,24,192]{2,1,0:T(8,128)(2,1)S(1)}, u32[]{:S(2)}, u32[]{:S(2)}) async-start(bf16[64,24,192]{2,1,0:T(8,128)(2,1)} %fusion.20), calls=%async_computation.8 | async-start | bytes 1572864 | tf_op jit(solution)/shard_map/all_to_all | solution.py:42
  497.4 96.1 %all-to-all-start.9 = ((bf16[64,8,7168]{2,1,0:T(8,128)(2,1)}), bf16[64,8,7168]{2,1,0:T(8,128)(2,1)}, u32[]{:S(2)}, u32[]{:S(2)}) async-start(bf16[64,8,7168]{2,1,0:T(8,128)(2,1)} %maximum_bitcast_fusion), calls=%async_computation.9 | async-start | bytes 14680064 | tf_op jit(solution)/shard_map/all_to_all | solution.py:42
  503.4 45.7 %collective-permute-start.19 = (f32[448,1024]{1,0:T(8,128)}, f32[448,1024]{1,0:T(8,128)}, u32[]{:S(2)}, u32[]{:S(2)}) collective-permute-start(f32[448,1024]{1,0:T(8,128)} %convert_add_fusion), channel_id=1, source_target_pairs={{0,64},{64,0},{1,65},{65,1},{2,66},{66,2},{3,67},{67,3},{4,68},{68... | collective-permute-start | bytes 5505032 | tf_op jit(solution)/shard_map/ppermute | solution.py:38
  547.7 13.2 %collective-permute-start.18 = (f32[16,50304]{1,0:T(8,128)S(1)}, f32[16,50304]{1,0:T(8,128)}, u32[]{:S(2)}, u32[]{:S(2)}) collective-permute-start(f32[16,50304]{1,0:T(8,128)S(1)} %fold.1), channel_id=1, source_target_pairs={{0,64},{64,0},{1,65},{65,1},{2,66},{66,2},{3,67},{67,3},{4,68},{68... | collective-permute-start | bytes 9658376 | tf_op jit(solution)/shard_map/ppermute | solution.py:38
  (71 other events, 808.4 us)
Sparse Core Ops, SparseCore 0:
  11.7 107.5 all-gather.1
